TPU v7x, 32 devices: a whole 2x2x4 slice. The times are simulated.
32 devices in a mesh: fsdp: 16 (over z, y, core), tp: 2 (over x).
Axes of the slice: x: 2, y: 2, z: 4, core: 2. Of those that a mesh axis runs over, the one named last changes fastest.
Arguments:
- inputs: bfloat16 [32, 1024, 1024], P('fsdp', 'tp'), may hold values from -6 to 6
- segment_ids: int32 [32, 1024], P('fsdp'), may hold values from 0 to 3, as said below
- valid_mask: int32 [32, 1024], P('fsdp', 'tp'), may hold values from 0 to 1
- teacher: bfloat16 [32, 1024, 1024], P('fsdp', 'tp'), may hold values from -6 to 6
- w_query: bfloat16 [1024, 1024], P('fsdp', 'tp'), may hold values from -0.1875 to 0.1875
- w_key: bfloat16 [1024, 1024], P('fsdp', 'tp'), may hold values from -0.1875 to 0.1875
- w_value: bfloat16 [1024, 1024], P('fsdp', 'tp'), may hold values from -0.1875 to 0.1875
- w_out: bfloat16 [1024, 1024], P('tp', 'fsdp'), may hold values from -0.75 to 0.75
- b_query: bfloat16 [1024], P(('tp', 'fsdp')), may hold values from -3 to 3
- b_value: bfloat16 [1024], P(('tp', 'fsdp')), may hold values from -3 to 3
- w_up: bfloat16 [1024, 4096], P('fsdp', 'tp'), may hold values from -0.1875 to 0.1875
- b_up: bfloat16 [4096], P(('tp', 'fsdp')), may hold values from -3 to 3
- w_down: bfloat16 [4096, 1024], P('tp', 'fsdp'), may hold values from -0.09375 to 0.09375
- ln_gains: bfloat16 [2, 1024], P(None, 'fsdp'), may hold values from 0.5 to 1.5
- ln_shifts: bfloat16 [4, 1024], P(None, 'fsdp'), may hold values from -2 to 2
Outputs:
- hidden_out: bfloat16 [32, 1024, 1024], P('fsdp', 'tp')
- loss_value: float32 [], replicated
- grad_inputs: bfloat16 [32, 1024, 1024], P('fsdp', 'tp')
- grad_w_query: float32 [1024, 1024], P('fsdp', 'tp')
- grad_w_key: float32 [1024, 1024], P('fsdp', 'tp')
- grad_w_value: float32 [1024, 1024], P('fsdp', 'tp')
- grad_w_out: float32 [1024, 1024], P('tp', 'fsdp')
- grad_b_query: float32 [1024], P(('tp', 'fsdp'))
- grad_b_value: float32 [1024], P(('tp', 'fsdp'))
- grad_w_up: float32 [1024, 4096], P('fsdp', 'tp')
- grad_b_up: float32 [4096], P(('tp', 'fsdp'))
- grad_w_down: float32 [4096, 1024], P('tp', 'fsdp')
- grad_ln_gains: float32 [2, 1024], P(None, 'fsdp')
- grad_ln_shifts: float32 [4, 1024], P(None, 'fsdp')
Inputs may be any that keep to these rules, and one draw needn't show every extreme that they name: `segment_ids`: ids never fall along a row.
All inputs are finite; a program needn't handle non-finite values.
Results may differ from a plain program's by a relative error of at most 0.022.
Values may be sent and summed in bfloat16 or wider, within the bound.
No kernel may reach another device: no remote copies, remote signals or barrier semaphores. Data moves between devices by JAX's collectives and lax.ppermute only.
A program may use at most 384 MiB of HBM per device.

v0:
```python
from functools import partial
import math

import jax
import jax.numpy as jnp
from jax import lax
from jax.sharding import PartitionSpec as P

HEAD_DIM = 64
WINDOW = 512


EPSILON = 1e-05
MASKED = -1e30


def layer_norm_parts(values, gain_row, shift_row):
    centre = jnp.mean(values, axis=-1, keepdims=True)
    centred = values - centre
    inverse = lax.rsqrt(jnp.mean(centred * centred, axis=-1, keepdims=True) + EPSILON)
    normed = centred * inverse
    return (normed * gain_row + shift_row, normed, inverse)


def norm_backward(normed, inverse, gain_row, grad_out):
    scaled = grad_out * gain_row
    return inverse * (
        scaled
        - jnp.mean(scaled, axis=-1, keepdims=True)
        - normed * jnp.mean(scaled * normed, axis=-1, keepdims=True)
    )


def dot_first(left_side, right_side):
    return lax.dot_general(
        left_side, right_side, (((0,), (0,)), ((), ())), preferred_element_type=jnp.float32
    )


def dot_last(left_side, right_side):
    return lax.dot_general(
        left_side, right_side, (((1,), (1,)), ((), ())), preferred_element_type=jnp.float32
    )


def own_rows(source, offset_own, piece_len):
    return lax.dynamic_slice_in_dim(source, offset_own, piece_len, 1)


def allowed_mask(seg_row, offset, block_len):
    length = seg_row.shape[0]
    position = jnp.arange(length, dtype=jnp.int32)
    query_pos = offset + jnp.arange(block_len, dtype=jnp.int32)
    same_doc = seg_row[offset : offset + block_len][:, None] == seg_row[None, :]
    return same_doc & (jnp.abs(query_pos[:, None] - position[None, :]) < WINDOW)


def block_scores(query_part, key_heads, allowed):
    scores = jnp.einsum(
        "qhd,khd->hqk", query_part, key_heads, preferred_element_type=jnp.float32
    ) / math.sqrt(HEAD_DIM)
    return jnp.where(allowed[None], scores, MASKED)


def attention_forward(queries, key_all, value_all, segment_ids):
    seq_count, length = (queries.shape[0], queries.shape[1])
    block_len = min(512, length)
    outputs, summaries = ([], [])
    for row_index in range(seq_count):
        row_out, row_lse = ([], [])
        for offset in range(0, length, block_len):
            allowed = allowed_mask(segment_ids[row_index], offset, block_len)
            scores = block_scores(
                queries[row_index, offset : offset + block_len], key_all[row_index], allowed
            )
            row_top = jnp.max(scores, axis=-1, keepdims=True)
            raised = jnp.exp(scores - row_top)
            norm_sum = jnp.sum(raised, axis=-1, keepdims=True)
            softened = (raised / norm_sum).astype(jnp.bfloat16)
            row_out.append(
                jnp.einsum(
                    "hqk,khd->qhd",
                    softened,
                    value_all[row_index],
                    preferred_element_type=jnp.float32,
                )
            )
            row_lse.append(row_top + jnp.log(norm_sum))
        outputs.append(jnp.concatenate(row_out, axis=0))
        summaries.append(jnp.concatenate(row_lse, axis=1))
    return (jnp.stack(outputs), jnp.stack(summaries))


def attention_backward(queries, key_all, value_all, segment_ids, summaries, grad_mixed):
    seq_count, length = (queries.shape[0], queries.shape[1])
    block_len = min(512, length)
    root_dim = math.sqrt(HEAD_DIM)
    query_rows, key_rows, value_rows = ([], [], [])
    for row_index in range(seq_count):
        key_grad = jnp.zeros(key_all.shape[1:], jnp.float32)
        value_grad = jnp.zeros(value_all.shape[1:], jnp.float32)
        query_parts = []
        for offset in range(0, length, block_len):
            allowed = allowed_mask(segment_ids[row_index], offset, block_len)
            query_part = queries[row_index, offset : offset + block_len]
            scores = block_scores(query_part, key_all[row_index], allowed)
            softened = jnp.exp(scores - summaries[row_index, :, offset : offset + block_len])
            grad_part = grad_mixed[row_index, offset : offset + block_len]
            value_grad = value_grad + jnp.einsum(
                "hqk,qhd->khd",
                softened.astype(jnp.bfloat16),
                grad_part,
                preferred_element_type=jnp.float32,
            )
            grad_soft = jnp.einsum(
                "qhd,khd->hqk", grad_part, value_all[row_index], preferred_element_type=jnp.float32
            )
            grad_score = (
                softened * (grad_soft - jnp.sum(softened * grad_soft, axis=-1, keepdims=True))
            ).astype(jnp.bfloat16)
            query_parts.append(
                jnp.einsum(
                    "hqk,khd->qhd",
                    grad_score,
                    key_all[row_index],
                    preferred_element_type=jnp.float32,
                )
                / root_dim
            )
            key_grad = (
                key_grad
                + jnp.einsum(
                    "hqk,qhd->khd", grad_score, query_part, preferred_element_type=jnp.float32
                )
                / root_dim
            )
        query_rows.append(jnp.concatenate(query_parts, axis=0))
        key_rows.append(key_grad)
        value_rows.append(value_grad)
    return (jnp.stack(query_rows), jnp.stack(key_rows), jnp.stack(value_rows))


def on_device(
    inputs,
    segment_ids,
    valid_mask,
    teacher,
    w_query,
    w_key,
    w_value,
    w_out,
    b_query,
    b_value,
    w_up,
    b_up,
    w_down,
    ln_gains,
    ln_shifts,
):
    seq_count, piece_len, features = inputs.shape
    tp_count = lax.axis_size("tp")
    tp_rank = lax.axis_index("tp")
    length = piece_len * tp_count
    total_tokens = seq_count * length * lax.axis_size("fsdp")
    offset_own = tp_rank * piece_len
    (
        full_query,
        full_key,
        full_value,
        full_out,
        full_bquery,
        full_bvalue,
        full_up,
        full_bup,
        full_down,
        full_gains,
        full_shifts,
    ) = (
        lax.all_gather(w_query, "fsdp", axis=0, tiled=True),
        lax.all_gather(w_key, "fsdp", axis=0, tiled=True),
        lax.all_gather(w_value, "fsdp", axis=0, tiled=True),
        lax.all_gather(w_out, "fsdp", axis=1, tiled=True),
        lax.all_gather(b_query, "fsdp", axis=0, tiled=True),
        lax.all_gather(b_value, "fsdp", axis=0, tiled=True),
        lax.all_gather(w_up, "fsdp", axis=0, tiled=True),
        lax.all_gather(b_up, "fsdp", axis=0, tiled=True),
        lax.all_gather(w_down, "fsdp", axis=1, tiled=True),
        lax.all_gather(ln_gains, "fsdp", axis=1, tiled=True),
        lax.all_gather(ln_shifts, "fsdp", axis=1, tiled=True),
    )
    gains = full_gains.astype(jnp.float32)
    shifts = full_shifts.astype(jnp.float32)
    local_width = full_query.shape[1]
    head_local = local_width // HEAD_DIM
    token_count = seq_count * length
    token_full = lax.all_gather(inputs, "tp", axis=1, tiled=True)
    flat_in = token_full.reshape(token_count, features)
    query_flat = (
        jnp.dot(flat_in, full_query, preferred_element_type=jnp.float32)
        + full_bquery.astype(jnp.float32)
    ).astype(jnp.bfloat16)
    key_flat = jnp.dot(flat_in, full_key, preferred_element_type=jnp.float32).astype(jnp.bfloat16)
    value_flat = (
        jnp.dot(flat_in, full_value, preferred_element_type=jnp.float32)
        + full_bvalue.astype(jnp.float32)
    ).astype(jnp.bfloat16)
    head_shape = (seq_count, length, head_local, HEAD_DIM)
    query_heads = query_flat.reshape(head_shape)
    key_heads = key_flat.reshape(head_shape)
    value_heads = value_flat.reshape(head_shape)
    mixed_heads, summaries = attention_forward(query_heads, key_heads, value_heads, segment_ids)
    mixed_low = mixed_heads.reshape(token_count, local_width).astype(jnp.bfloat16)
    attend_part = jnp.dot(mixed_low, full_out, preferred_element_type=jnp.float32).reshape(
        seq_count, length, features
    )
    attend_all = lax.psum(attend_part.astype(jnp.bfloat16), "tp").astype(jnp.float32)
    pre_first = token_full.astype(jnp.float32) + attend_all + shifts[2]
    normed_first, unit_first, inverse_first = layer_norm_parts(pre_first, gains[0], shifts[0])
    hidden_full = normed_first.astype(jnp.bfloat16)
    normed_own = own_rows(normed_first, offset_own, piece_len)
    hidden_flat = hidden_full.reshape(token_count, features)
    up_all = jnp.dot(hidden_flat, full_up, preferred_element_type=jnp.float32) + full_bup.astype(
        jnp.float32
    )
    active = jax.nn.gelu(up_all, approximate=False).astype(jnp.bfloat16)
    down_part = jnp.dot(active, full_down, preferred_element_type=jnp.float32).reshape(
        seq_count, length, features
    )
    down_own = lax.psum_scatter(
        down_part.astype(jnp.bfloat16), "tp", scatter_dimension=1, tiled=True
    ).astype(jnp.float32)
    pre_second = normed_own + down_own + shifts[3]
    result, unit_second, inverse_second = layer_norm_parts(pre_second, gains[1], shifts[1])
    differ = result - teacher.astype(jnp.float32)
    mask_float = valid_mask.astype(jnp.float32)[..., None]
    squares, valid_count = lax.psum(
        (jnp.sum(mask_float * differ * differ), jnp.sum(mask_float)), ("fsdp", "tp")
    )
    loss_value = squares / (features * valid_count)
    grad_result = mask_float * differ * (total_tokens / valid_count)
    grad_second = norm_backward(unit_second, inverse_second, gains[1], grad_result)
    grad_down_full = lax.all_gather(grad_second.astype(jnp.bfloat16), "tp", axis=1, tiled=True)
    grad_down_flat = grad_down_full.reshape(token_count, features)
    weight_down = dot_first(active, grad_down_flat)
    grad_active = dot_last(grad_down_flat, full_down)
    gelu_back = jax.vjp(partial(jax.nn.gelu, approximate=False), up_all)[1]
    grad_up = gelu_back(grad_active)[0].astype(jnp.bfloat16)
    weight_up = dot_first(hidden_flat, grad_up)
    bias_up = jnp.sum(grad_up.astype(jnp.float32), axis=0)
    hidden_part = dot_last(grad_up, full_up).reshape(seq_count, length, features)
    current = own_rows(hidden_part, offset_own, piece_len)
    hidden_part = lax.dynamic_update_slice_in_dim(hidden_part, current + grad_second, offset_own, 1)
    grad_hidden_all = lax.psum(hidden_part.astype(jnp.bfloat16), "tp").astype(jnp.float32)
    grad_first_all = norm_backward(unit_first, inverse_first, gains[0], grad_hidden_all)
    grad_mix_full = grad_first_all.astype(jnp.bfloat16)
    grad_first_own = own_rows(grad_first_all, offset_own, piece_len)
    grad_hidden_own = own_rows(grad_hidden_all, offset_own, piece_len)
    unit_first_own = own_rows(unit_first, offset_own, piece_len)
    grad_mix_flat = grad_mix_full.reshape(token_count, features)
    weight_out = dot_first(mixed_low, grad_mix_flat)
    grad_mixed = dot_last(grad_mix_flat, full_out).astype(jnp.bfloat16).reshape(head_shape)
    grad_query, grad_key, grad_value = attention_backward(
        query_heads, key_heads, value_heads, segment_ids, summaries, grad_mixed
    )
    query_low = grad_query.astype(jnp.bfloat16).reshape(token_count, local_width)
    key_low = grad_key.astype(jnp.bfloat16).reshape(token_count, local_width)
    value_low = grad_value.astype(jnp.bfloat16).reshape(token_count, local_width)
    weight_query = dot_first(flat_in, query_low)
    weight_key = dot_first(flat_in, key_low)
    weight_value = dot_first(flat_in, value_low)
    bias_query = jnp.sum(query_low.astype(jnp.float32), axis=0)
    bias_value = jnp.sum(value_low.astype(jnp.float32), axis=0)
    input_part = (
        dot_last(query_low, full_query)
        + dot_last(key_low, full_key)
        + dot_last(value_low, full_value)
    )
    grad_inputs = (
        lax.psum_scatter(
            input_part.reshape(seq_count, length, features).astype(jnp.bfloat16),
            "tp",
            scatter_dimension=1,
            tiled=True,
        ).astype(jnp.float32)
        + grad_first_own
    )
    gain_part = jnp.stack(
        [
            jnp.sum(grad_hidden_own * unit_first_own, axis=(0, 1)),
            jnp.sum(grad_result * unit_second, axis=(0, 1)),
        ]
    )
    shift_part = jnp.stack(
        [
            jnp.sum(grad_hidden_own, axis=(0, 1)),
            jnp.sum(grad_result, axis=(0, 1)),
            jnp.sum(grad_first_own, axis=(0, 1)),
            jnp.sum(grad_second, axis=(0, 1)),
        ]
    )
    gain_sum, shift_sum = lax.psum((gain_part, shift_part), "tp")
    gradients = (
        lax.psum_scatter(
            weight_query.astype(jnp.bfloat16), "fsdp", scatter_dimension=0, tiled=True
        ).astype(jnp.float32),
        lax.psum_scatter(
            weight_key.astype(jnp.bfloat16), "fsdp", scatter_dimension=0, tiled=True
        ).astype(jnp.float32),
        lax.psum_scatter(
            weight_value.astype(jnp.bfloat16), "fsdp", scatter_dimension=0, tiled=True
        ).astype(jnp.float32),
        lax.psum_scatter(
            weight_out.astype(jnp.bfloat16), "fsdp", scatter_dimension=1, tiled=True
        ).astype(jnp.float32),
        lax.psum_scatter(
            bias_query.astype(jnp.bfloat16), "fsdp", scatter_dimension=0, tiled=True
        ).astype(jnp.float32),
        lax.psum_scatter(
            bias_value.astype(jnp.bfloat16), "fsdp", scatter_dimension=0, tiled=True
        ).astype(jnp.float32),
        lax.psum_scatter(
            weight_up.astype(jnp.bfloat16), "fsdp", scatter_dimension=0, tiled=True
        ).astype(jnp.float32),
        lax.psum_scatter(
            bias_up.astype(jnp.bfloat16), "fsdp", scatter_dimension=0, tiled=True
        ).astype(jnp.float32),
        lax.psum_scatter(
            weight_down.astype(jnp.bfloat16), "fsdp", scatter_dimension=1, tiled=True
        ).astype(jnp.float32),
        lax.psum_scatter(
            gain_sum.astype(jnp.bfloat16), "fsdp", scatter_dimension=1, tiled=True
        ).astype(jnp.float32),
        lax.psum_scatter(
            shift_sum.astype(jnp.bfloat16), "fsdp", scatter_dimension=1, tiled=True
        ).astype(jnp.float32),
    )
    return (
        result.astype(jnp.bfloat16),
        loss_value,
        grad_inputs.astype(jnp.bfloat16),
        gradients[0],
        gradients[1],
        gradients[2],
        gradients[3],
        gradients[4],
        gradients[5],
        gradients[6],
        gradients[7],
        gradients[8],
        gradients[9],
        gradients[10],
    )


def solution(mesh):
    in_specs = (
        P("fsdp", "tp", None),
        P("fsdp", None),
        P("fsdp", "tp"),
        P("fsdp", "tp", None),
        P("fsdp", "tp"),
        P("fsdp", "tp"),
        P("fsdp", "tp"),
        P("tp", "fsdp"),
        P(("tp", "fsdp")),
        P(("tp", "fsdp")),
        P("fsdp", "tp"),
        P(("tp", "fsdp")),
        P("tp", "fsdp"),
        P(None, "fsdp"),
        P(None, "fsdp"),
    )
    out_specs = (
        P("fsdp", "tp", None),
        P(),
        P("fsdp", "tp", None),
        P("fsdp", "tp"),
        P("fsdp", "tp"),
        P("fsdp", "tp"),
        P("tp", "fsdp"),
        P(("tp", "fsdp")),
        P(("tp", "fsdp")),
        P("fsdp", "tp"),
        P(("tp", "fsdp")),
        P("tp", "fsdp"),
        P(None, "fsdp"),
        P(None, "fsdp"),
    )
    return jax.shard_map(
        on_device, mesh=mesh, in_specs=in_specs, out_specs=out_specs, check_vma=False
    )
```

profile of v0, /device:TPU:0, one launch (start us, length us, event | category | flops | bytes accessed | tf_op | source)
XLA Modules:
  0.0 1547.6 jit_solution(2023426575819351262)
XLA Ops:
  15.9 35.1 %all-reduce.7 = (bf16[512]{0:T(512)(128)(2,1)S(1)}, bf16[512]{0:T(512)(128)(2,1)S(1)}) all-reduce(bf16[512]{0:T(512)(128)(2,1)S(1)} %dynamic-update-slice, bf16[512]{0:T(512)(128)(2,1)S(1)} %dynamic-update-slice.1), channel_id=1, replica_groups=mesh['fsdp'=16,'tp'=2] {'fsdp'}, use_global_device_ids=true, to_apply=%add | all-reduce | flops 1024 | bytes 4096
  55.9 52.3 %all-gather.12.cloned.1.call-done = bf16[2,1024,1024]{2,1,0:T(8,128)(2,1)} async-done(((bf16[2,512,1024]{2,1,0:T(8,128)(2,1)}), bf16[2,1024,1024]{2,1,0:T(8,128)(2,1)}) %all-gather.12.cloned.1.call-update) | async-done | bytes 4194320 | tf_op jit(solution)/shard_map/all_gather | solution.py:196
  113.2 35.1 %all-gather.16.cloned.1.call-done = bf16[1024,512]{1,0:T(8,128)(2,1)} async-done(((bf16[64,512]{1,0:T(8,128)(2,1)}), bf16[1024,512]{1,0:T(8,128)(2,1)}) %all-gather.16.cloned.1.call-update) | async-done | bytes 1048592 | tf_op jit(solution)/shard_map/all_gather | solution.py:179
  256.5 19.2 %all-gather.2 = bf16[16,1,128]{2,1,0:T(2,128)(2,1)S(1)} all-gather(bf16[1,1,128]{2,1,0:T(2,128)(2,1)S(1)} %bitcast.342), channel_id=1, replica_groups=mesh['fsdp'=16,'tp'=2] {'fsdp'}, dimensions={0}, use_global_device_ids=true | all-gather | bytes 4352 | tf_op jit(solution)/shard_map/all_gather | solution.py:186
  275.8 17.3 %all-gather.1 = bf16[16,64,2]{1,2,0:T(2,128)(2,1)S(1)} all-gather(bf16[1,64,2]{1,2,0:T(2,128)(2,1)S(1)} %bitcast.343), channel_id=1, replica_groups=mesh['fsdp'=16,'tp'=2] {'fsdp'}, dimensions={0}, use_global_device_ids=true | all-gather | bytes 4352 | tf_op jit(solution)/shard_map/all_gather | solution.py:188
  293.7 18.8 %all-gather = bf16[16,64,4]{1,2,0:T(4,128)(2,1)S(1)} all-gather(bf16[1,64,4]{1,2,0:T(4,128)(2,1)S(1)} %bitcast.341), channel_id=1, replica_groups=mesh['fsdp'=16,'tp'=2] {'fsdp'}, dimensions={0}, use_global_device_ids=true | all-gather | bytes 8704 | tf_op jit(solution)/shard_map/all_gather | solution.py:189
  313.2 48.6 %all-reduce.11.cloned.1.call-done = bf16[2,1024,1024]{2,1,0:T(8,128)(2,1)} async-done(((bf16[2,1024,1024]{2,1,0:T(8,128)(2,1)}), bf16[2,1024,1024]{2,1,0:T(8,128)(2,1)}) %all-reduce.11.cloned.1.call-update) | async-done | bytes 4194320 | tf_op jit(solution)/shard_map/psum | solution.py:216
  379.5 35.5 %all-gather.22.cloned.1.call-done = bf16[1024,2048]{1,0:T(8,128)(2,1)} async-done(((bf16[64,2048]{1,0:T(8,128)(2,1)}), bf16[1024,2048]{1,0:T(8,128)(2,1)}) %all-gather.22.cloned.1.call-update) | async-done | bytes 4194320 | tf_op jit(solution)/shard_map/all_gather | solution.py:185
  415.0 49.1 %multiply_convert_fusion.4 = (bf16[2048,2048]{1,0:T(8,128)(2,1)}, f32[2048,2048]{1,0:T(8,128)}, f32[2048,2048]{1,0:T(8,128)}) fusion(f32[2048]{0:T(1024)S(1)} %bitcast.339, bf16[2048,1024]{1,0:T(8,128)(2,1)} %bitcast.298, bf16[1024,2048]{1,0:T(8,128)(2,1)} %all-gather.22.cloned.1.call-done), kind=kOutput, calls=%fused_computation.15 | convolution fusion | flops 8866758656 | bytes 50339840 | tf_op jit(solution)/shard_map/dot_general | solution.py:222
  481.3 40.0 %psum.44 = f32[]{:T(128)} all-reduce(f32[]{:T(128)} %convert_reduce_fusion), channel_id=1, replica_groups=mesh['fsdp'=16,'tp'=2] {'fsdp','tp'}, use_global_device_ids=true, to_apply=%region_17.18 | all-reduce | flops 1 | bytes 8 | tf_op jit(solution)/shard_map/psum | solution.py:236
  544.8 56.7 %all-gather.26.cloned.1.call-done = bf16[2,1024,1024]{2,1,0:T(8,128)(2,1)} async-done(((bf16[2,512,1024]{2,1,0:T(8,128)(2,1)}), bf16[2,1024,1024]{2,1,0:T(8,128)(2,1)}) %all-gather.26.cloned.1.call-update) | async-done | bytes 4194320 | tf_op jit(solution)/shard_map/all_gather | solution.py:242
  601.5 28.2 %fusion.97 = (bf16[2048]{0:T(1024)(128)(2,1)}, bf16[2048,2048]{1,0:T(8,128)(2,1)}) fusion(f32[2048,2048]{1,0:T(8,128)} %get-tuple-element.96, bf16[2048,1024]{1,0:T(8,128)(2,1)} %bitcast.344, bf16[2048,1024]{0,1:T(8,128)(2,1)} %all-gather.24.cloned.1.call-done, f32[2048,2048]{1,0:T(8,128)} %get-tuple-element.147, f32[2048]{0:T(1024)S(1)} %bitcast.340), kind=kOutput, calls=%fused_computation.208 | convolution fusion | flops 8657041408 | bytes 50343936 | tf_op jit(solution)/shard_map/dot_general | solution.py:41
  652.0 106.6 %all-reduce.13.cloned.1.call-done = bf16[2,1024,1024]{2,1,0:T(8,128)(2,1)} async-done(((bf16[2,1024,1024]{2,1,0:T(8,128)(2,1)}), bf16[2,1024,1024]{2,1,0:T(8,128)(2,1)}) %all-reduce.13.cloned.1.call-update) | async-done | bytes 4194320 | tf_op jit(solution)/shard_map/psum | solution.py:253
  789.0 15.9 %multiply_reduce_fusion.3 = (f32[8,512]{1,0:T(8,128)}, f32[8,512,1024]{2,1,0:T(8,128)}) fusion(f32[8,512,1024]{2,1,0:T(8,128)} %copy-done.3, f32[8,512]{1,0:T(8,128)} %get-tuple-element.117, bf16[1024,8,64]{0,2,1:T(8,128)(2,1)S(1)} %bitcast.287, bf16[1,512,8,64]{1,3,2,0:T(8,128)(2,1)S(1)} %copy.123), kind=kOutput, calls=%fused_computation.12 | convolution fusion | flops 549449728 | bytes 35160064 | tf_op jit(solution)/shard_map/qhd,khd->hqk/dot_general | solution.py:115
  849.4 15.1 multiply_reduce_fusion.1
  1032.2 40.9 %psum.43 = f32[]{:T(128)} all-reduce(f32[]{:T(128)} %get-tuple-element.73), channel_id=1, replica_groups=mesh['fsdp'=16,'tp'=2] {'fsdp','tp'}, use_global_device_ids=true, to_apply=%region_15.16 | all-reduce | flops 1 | bytes 8 | tf_op jit(solution)/shard_map/psum | solution.py:236
  1080.4 31.9 %all-reduce.6 = (bf16[512]{0:T(512)(128)(2,1)S(1)}, bf16[512]{0:T(512)(128)(2,1)S(1)}, bf16[2048]{0:T(1024)(128)(2,1)S(1)}) all-reduce(bf16[512]{0:T(512)(128)(2,1)S(1)} %reduce_sum.275, bf16[512]{0:T(512)(128)(2,1)S(1)} %reduce_sum.277, bf16[2048]{0:T(1024)(128)(2,1)S(1)} %copy-done.86), channel_id=8, replica_groups=mesh['fsdp'=16,'tp'=2] {'fsdp'}, use_global_device_ids=true, to_apply=%region_33.34.clone | all-reduce | flops 3072 | bytes 12288
  1134.7 16.4 %reduce-scatter.35.cloned.1.call-done = bf16[64,512]{1,0:T(8,128)(2,1)} async-done(((bf16[1024,512]{1,0:T(8,128)(2,1)}), bf16[64,512]{1,0:T(8,128)(2,1)}) %reduce-scatter.35.cloned.1.call-update) | async-done | bytes 65552
  1152.8 58.1 %reduce-scatter.31.cloned.1.call-done = bf16[64,512]{1,0:T(8,128)(2,1)} async-done(((bf16[1024,512]{1,0:T(8,128)(2,1)}), bf16[64,512]{1,0:T(8,128)(2,1)}) %reduce-scatter.31.cloned.1.call-update) | async-done | bytes 65552
  1212.6 58.6 %reduce-scatter.25.cloned.1.call-done = bf16[512,64]{0,1:T(8,128)(2,1)} async-done(((bf16[512,1024]{0,1:T(8,128)(2,1)}), bf16[512,64]{0,1:T(8,128)(2,1)}) %reduce-scatter.25.cloned.1.call-update) | async-done | bytes 65552 | tf_op jit(solution)/shard_map/reduce_scatter | solution.py:312
  1272.7 73.9 %reduce-scatter.29.cloned.1.call-done = bf16[2048,64]{0,1:T(8,128)(2,1)} async-done(((bf16[2048,1024]{0,1:T(8,128)(2,1)}), bf16[2048,64]{0,1:T(8,128)(2,1)}) %reduce-scatter.29.cloned.1.call-update) | async-done | bytes 262160 | tf_op jit(solution)/shard_map/reduce_scatter | solution.py:327
  1348.4 74.0 %reduce-scatter.27.cloned.1.call-done = bf16[64,2048]{1,0:T(8,128)(2,1)} async-done(((bf16[1024,2048]{1,0:T(8,128)(2,1)}), bf16[64,2048]{1,0:T(8,128)(2,1)}) %reduce-scatter.27.cloned.1.call-update) | async-done | bytes 262160 | tf_op jit(solution)/shard_map/reduce_scatter | solution.py:321
  1424.2 56.1 %reduce-scatter.37.cloned.1.call-done = bf16[64,2]{1,0:T(8,128)(2,1)} async-done(((bf16[1024,2]{1,0:T(8,128)(2,1)}), bf16[64,2]{1,0:T(8,128)(2,1)}) %reduce-scatter.37.cloned.1.call-update) | async-done | bytes 272
  1481.6 56.4 %reduce-scatter.39.cloned.1.call-done = bf16[64,4]{1,0:T(8,128)(2,1)} async-done(((bf16[1024,4]{1,0:T(8,128)(2,1)}), bf16[64,4]{1,0:T(8,128)(2,1)}) %reduce-scatter.39.cloned.1.call-update) | async-done | bytes 528
  (425 shorter events, 486.4 us)
Async XLA Ops:
  7.2 48.7 %all-gather.14.cloned.1.call-start = ((), (), s32[]{:S(2)}) async-start(), calls=%async_computation.11 | async-start | bytes 1114112 | tf_op jit(solution)/shard_map/all_gather | solution.py:181
  7.9 100.2 %all-gather.12.cloned.1.call-start = ((), (), s32[]{:S(2)}) async-start(), calls=%async_computation.10 | async-start | bytes 6291456 | tf_op jit(solution)/shard_map/all_gather | solution.py:196
  8.7 139.6 %all-gather.16.cloned.1.call-start = ((), (), s32[]{:S(2)}) async-start(), calls=%async_computation.12 | async-start | bytes 1114112 | tf_op jit(solution)/shard_map/all_gather | solution.py:179
  9.4 177.8 %all-gather.18.cloned.1.call-start = ((), (), s32[]{:S(2)}) async-start(), calls=%async_computation.13 | async-start | bytes 1114112 | tf_op jit(solution)/shard_map/all_gather | solution.py:180
  10.0 239.0 %all-gather.20.cloned.1.call-start = ((), (), s32[]{:S(2)}) async-start(), calls=%async_computation.14 | async-start | bytes 1114112 | tf_op jit(solution)/shard_map/all_gather | solution.py:182
  10.6 351.3 %all-reduce.11.cloned.1.call-start = ((), (), s32[]{:S(2)}) async-start(), calls=%async_computation.15 | async-start | bytes 8388608 | tf_op jit(solution)/shard_map/psum | solution.py:216
  113.2 99.1 %copy-start.18 = (bf16[1024,512]{0,1:T(8,128)(2,1)}, bf16[1024,512]{0,1:T(8,128)(2,1)S(1)}, u32[]{:S(2)}) copy-start(bf16[1024,512]{0,1:T(8,128)(2,1)S(1)} %get-tuple-element.116) | copy-start | bytes 3145732
  113.2 128.9 %copy-start.20 = (bf16[1024,512]{0,1:T(8,128)(2,1)}, bf16[1024,512]{0,1:T(8,128)(2,1)S(1)}, u32[]{:S(2)}) copy-start(bf16[1024,512]{0,1:T(8,128)(2,1)S(1)} %get-tuple-element.115) | copy-start | bytes 3145732
  255.0 160.1 %all-gather.22.cloned.1.call-start = ((), (), s32[]{:S(2)}) async-start(), calls=%async_computation.16 | async-start | bytes 4456448 | tf_op jit(solution)/shard_map/all_gather | solution.py:185
  255.7 210.8 %all-gather.24.cloned.1.call-start = ((), (), s32[]{:S(2)}) async-start(), calls=%async_computation.17 | async-start | bytes 4456448 | tf_op jit(solution)/shard_map/all_gather | solution.py:187
  256.5 278.5 %reduce-scatter.21.cloned.1.call-start = ((), (), s32[]{:S(2)}) async-start(), calls=%async_computation.18 | async-start | bytes 6291456 | tf_op jit(solution)/shard_map/reduce_scatter | solution.py:229
  480.6 120.9 %all-gather.26.cloned.1.call-start = ((), (), s32[]{:S(2)}) async-start(), calls=%async_computation.19 | async-start | bytes 6291456 | tf_op jit(solution)/shard_map/all_gather | solution.py:242
  544.8 213.8 %all-reduce.13.cloned.1.call-start = ((), (), s32[]{:S(2)}) async-start(), calls=%async_computation.20 | async-start | bytes 8388608 | tf_op jit(solution)/shard_map/psum | solution.py:253
  647.8 110.8 %copy-start.78 = (f32[1,1024]{1,0:T(1,128)S(1)}, f32[1,1024]{1,0:T(1,128)}, u32[]{:S(2)}) copy-start(f32[1,1024]{1,0:T(1,128)} %copy-done.77) | copy-start | bytes 12292
  650.5 114.5 %copy-start.66 = (f32[2,1024]{1,0:T(2,128)S(1)}, f32[2,1024]{1,0:T(2,128)}, u32[]{:S(2)}) copy-start(f32[2,1024]{1,0:T(2,128)} %copy-done.65) | copy-start | bytes 24580
  650.5 466.6 %reduce-scatter.23.cloned.1.call-start = ((), (), s32[]{:S(2)}) async-start(), calls=%async_computation.21 | async-start | bytes 6291456 | tf_op jit(solution)/shard_map/reduce_scatter | solution.py:279
  975.2 157.8 %reduce-scatter.33.cloned.1.call-start = ((), (), s32[]{:S(2)}) async-start(), calls=%async_computation.26 | async-start | bytes 1114112
  981.7 169.4 %reduce-scatter.35.cloned.1.call-start = ((), (), s32[]{:S(2)}) async-start(), calls=%async_computation.27 | async-start | bytes 1114112
  987.7 223.2 %reduce-scatter.31.cloned.1.call-start = ((), (), s32[]{:S(2)}) async-start(), calls=%async_computation.25 | async-start | bytes 1114112
  994.4 276.8 %reduce-scatter.25.cloned.1.call-start = ((), (), s32[]{:S(2)}) async-start(), calls=%async_computation.22 | async-start | bytes 1114112 | tf_op jit(solution)/shard_map/reduce_scatter | solution.py:312
  1001.6 345.0 %reduce-scatter.29.cloned.1.call-start = ((), (), s32[]{:S(2)}) async-start(), calls=%async_computation.24 | async-start | bytes 4456448 | tf_op jit(solution)/shard_map/reduce_scatter | solution.py:327
  1015.8 406.7 %reduce-scatter.27.cloned.1.call-start = ((), (), s32[]{:S(2)}) async-start(), calls=%async_computation.23 | async-start | bytes 4456448 | tf_op jit(solution)/shard_map/reduce_scatter | solution.py:321
  1030.2 450.1 %reduce-scatter.37.cloned.1.call-start = ((), (), s32[]{:S(2)}) async-start(), calls=%async_computation.28 | async-start | bytes 278528
  1130.8 407.2 %reduce-scatter.39.cloned.1.call-start = ((), (), s32[]{:S(2)}) async-start(), calls=%async_computation.29 | async-start | bytes 278528
  (105 other events, 1243.9 us)
Sparse Core Ops, SparseCore 0:
  10.2 40.5 all-gather.13
  52.3 55.7 all-gather.11
  110.3 37.9 all-gather.15
  150.3 36.8 all-gather.17
  189.2 36.8 all-gather.19
  255.1 106.7 all-reduce.10
  364.3 50.7 all-gather.21
  417.4 49.0 all-gather.23
  480.7 54.1 reduce-scatter.20
  544.9 56.5 all-gather.25
  650.6 107.8 all-reduce.12
  975.3 54.3 reduce-scatter.22
  1033.2 57.3 reduce-scatter.32
  1094.6 56.4 reduce-scatter.34
  1154.5 56.3 reduce-scatter.30
  1214.8 56.3 reduce-scatter.24
  1274.9 71.6 reduce-scatter.28
  1350.9 71.5 reduce-scatter.26
  1425.9 54.2 reduce-scatter.36
  1483.6 54.3 reduce-scatter.38
where the time goes:
time: 1550 us
  waiting for transfers between devices  761 us (49%)
  matrix products  332 us (21%)
  blocking collectives  211 us (14%)
  other arithmetic  134 us (9%)
  local copies, waits for them, and re-layouts  86.6 us (6%)
  between operations  21.3 us (1%)
    unnamed x25, waiting for transfers between devices  192 us
    psum x1, waiting for transfers between devices, on_device(): lax.psum(hidden_part.astype(jnp.bfloat16), 'tp').astype(jnp.float32)  107 us
    psum x2, blocking collectives, on_device(): lax.psum((jnp.sum(mask_float * differ * differ), jnp.sum(mask_float)), ('...  81 us
    reduce_scatter x1, waiting for transfers between devices, on_device(): lax.psum_scatter(weight_up.astype(jnp.bfloat16), 'fsdp', scatter_dimensio...  74 us
    reduce_scatter x1, waiting for transfers between devices, on_device(): lax.psum_scatter(weight_down.astype(jnp.bfloat16), 'fsdp', scatter_dimens...  73.9 us
    unnamed x2, blocking collectives  67 us
    reduce_scatter x1, waiting for transfers between devices, on_device(): lax.psum_scatter(weight_out.astype(jnp.bfloat16), 'fsdp', scatter_dimensi...  58.6 us
    dot_general x4, matrix products, attention_backward(): jnp.einsum('qhd,khd->hqk', grad_part, value_all[row_index], preferred_ele...  56.9 us
  transfers between devices with their start and end apart: 20, of which 16 were waited for; matrix products, arithmetic and copies ran while one was open for 16% of the time, Pallas kernels for 0%

commit v1 on v0

--- a/solution.py
+++ b/solution.py
@@ -4,6 +4,8 @@
 import jax
 import jax.numpy as jnp
 from jax import lax
+from jax.experimental import pallas as pl
+from jax.experimental.pallas import tpu as pltpu
 from jax.sharding import PartitionSpec as P
 
 HEAD_DIM = 64
@@ -140,7 +142,7 @@
     return (jnp.stack(query_rows), jnp.stack(key_rows), jnp.stack(value_rows))
 
 
-def on_device(
+def on_device_heads(
     inputs,
     segment_ids,
     valid_mask,
@@ -352,6 +354,632 @@
     )
 
 
+BLOCK = 256
+LOG2E = math.log2(math.e)
+SHARD_ROWS_PARTS = 2
+
+
+def rows_plan_fits(mesh):
+    fsdp_count, tp_count = (mesh.shape["fsdp"], mesh.shape["tp"])
+    return tp_count == 2 and fsdp_count >= 8 and fsdp_count & (fsdp_count - 1) == 0
+
+
+def dot_plain(left_side, right_side):
+    return lax.dot_general(
+        left_side, right_side, (((1,), (0,)), ((), ())), preferred_element_type=jnp.float32
+    )
+
+
+def exchange(values, step):
+    axis, bit = step
+    count = lax.axis_size(axis)
+    return lax.ppermute(values, axis, [(index, index ^ bit) for index in range(count)])
+
+
+def step_orders():
+    count = lax.axis_size("fsdp")
+    across = ("tp", 1)
+    core = ("fsdp", 1)
+    side = ("fsdp", 2)
+    far = [("fsdp", 1 << place) for place in range(2, count.bit_length() - 1)]
+    far.reverse()
+    first = tuple(far) + (across, side)
+    second = (far[0], across, side) + tuple(far[1:])
+    return core, (first, second)
+
+
+def order_masks(order):
+    masks = [(0, 0)]
+    for axis, bit in order:
+        fsdp_bit, tp_bit = (bit, 0) if axis == "fsdp" else (0, bit)
+        masks = masks + [(high ^ fsdp_bit, low ^ tp_bit) for high, low in masks]
+    return masks
+
+
+def gather_part(shard, order, core):
+    held = shard[None]
+    for step in order[:-1]:
+        held = jnp.concatenate([held, exchange(held, step)], axis=0)
+    other = exchange(held, order[-1])
+    return [held, other, exchange(held, core), exchange(other, core)]
+
+
+def gather_masks(order, core):
+    masks = order_masks(order)
+    half = len(masks) // 2
+    near = [masks[:half], masks[half:]]
+    return near + [[(high ^ core[1], low) for high, low in group] for group in near]
+
+
+def add_low(left_side, right_side):
+    return (left_side.astype(jnp.float32) + right_side.astype(jnp.float32)).astype(jnp.bfloat16)
+
+
+def scatter_part(kept, sent, order, core):
+    received = exchange(sent, core)
+    for step in order:
+        half = kept.shape[0] // 2
+        outgoing = add_low(kept[half:], received[half:])
+        arrived = exchange(outgoing, step)
+        kept, received = (add_low(kept[:half], received[:half]), arrived)
+    return kept[0].astype(jnp.float32) + received[0].astype(jnp.float32)
+
+
+def scatter_masks(order):
+    return order_masks(tuple(reversed(order)))
+
+
+def assemble_kernel(plan, place_ref, *refs):
+    sources, targets, sem = (refs[: plan["sources"]], refs[plan["sources"] : -1], refs[-1])
+    me_fsdp, me_tp = (place_ref[0], place_ref[1])
+    rows = plan["rows"]
+    copies = []
+    for source, place, start, width, high, low, target, per_tp, column in plan["copies"]:
+        row = pl.multiple_of((me_fsdp ^ high) * rows, rows)
+        lane = pl.multiple_of((me_tp ^ low) * per_tp + column, 128)
+        full = (target, pl.ds(row, rows), pl.ds(lane, width))
+        piece = (source, place, slice(None), pl.ds(start, width))
+        if plan["gather"]:
+            from_ref = sources[piece[0]].at[piece[1], :, piece[3]]
+            to_ref = targets[full[0]].at[full[1], full[2]]
+        else:
+            from_ref = sources[full[0]].at[full[1], full[2]]
+            to_ref = targets[piece[0]].at[piece[1], :, piece[3]]
+        copy = pltpu.make_async_copy(from_ref, to_ref, sem)
+        copy.start()
+        copies.append(copy)
+    for copy in copies:
+        copy.wait()
+
+
+def run_assemble(plan, place, sources, out_shapes, name):
+    any_spec = pl.BlockSpec(memory_space=pl.ANY)
+    moved = sum(math.prod(out.shape) * 2 for out in out_shapes)
+    return pl.pallas_call(
+        partial(assemble_kernel, plan),
+        in_specs=[pl.BlockSpec(memory_space=pltpu.SMEM)] + [any_spec] * len(sources),
+        out_specs=[any_spec] * len(out_shapes),
+        out_shape=out_shapes,
+        scratch_shapes=[pltpu.SemaphoreType.DMA],
+        cost_estimate=pl.CostEstimate(flops=0, bytes_accessed=2 * moved, transcendentals=0),
+        name=name,
+    )(place, *sources)
+
+
+def gather_group(shard, place, columns, widths, name):
+    core, orders = step_orders()
+    rows, width = shard.shape
+    part_width = width // 2
+    sources, copies = ([], [])
+    for part, order in enumerate(orders):
+        pieces = gather_part(shard[:, part * part_width : (part + 1) * part_width], order, core)
+        for piece, masks in zip(pieces, gather_masks(order, core)):
+            for place_at, (high, low) in enumerate(masks):
+                for start, span_width, target, per_tp, column in columns[part]:
+                    copies.append(
+                        (len(sources), place_at, start, span_width, high, low, target, per_tp, column)
+                    )
+            sources.append(piece)
+    plan = dict(gather=True, sources=len(sources), rows=rows, copies=copies)
+    full_rows = rows * lax.axis_size("fsdp")
+    shapes = [jax.ShapeDtypeStruct((full_rows, span), jnp.bfloat16) for span in widths]
+    return run_assemble(plan, place, sources, shapes, name)
+
+
+def scatter_group(fulls, place, columns, rows, part_width, name):
+    core, orders = step_orders()
+    copies, shapes = ([], [])
+    for part, order in enumerate(orders):
+        masks = scatter_masks(order)
+        for flip in (0, core[1]):
+            for place_at, (high, low) in enumerate(masks):
+                for start, span_width, target, per_tp, column in columns[part]:
+                    copies.append(
+                        (len(shapes), place_at, start, span_width, high ^ flip, low, target, per_tp, column)
+                    )
+            shapes.append(jax.ShapeDtypeStruct((len(masks), rows, part_width), jnp.bfloat16))
+    plan = dict(gather=False, sources=len(fulls), rows=rows, copies=copies)
+    pieces = run_assemble(plan, place, fulls, shapes, name)
+    parts = [
+        scatter_part(pieces[2 * part], pieces[2 * part + 1], order, core)
+        for part, order in enumerate(orders)
+    ]
+    return jnp.concatenate(parts, axis=1)
+
+
+def bit_steps():
+    steps = []
+    for axis in ("fsdp", "tp"):
+        for place in range(lax.axis_size(axis).bit_length() - 1):
+            steps.append((axis, 1 << place))
+    return steps
+
+
+def gather_small(values):
+    for step in bit_steps():
+        mine = (lax.axis_index(step[0]) & step[1]) != 0
+        arrived = exchange(values, step)
+        values = jnp.concatenate(
+            [jnp.where(mine, arrived, values), jnp.where(mine, values, arrived)], axis=0
+        )
+    return values
+
+
+def scatter_small(values):
+    for step in reversed(bit_steps()):
+        mine = (lax.axis_index(step[0]) & step[1]) != 0
+        half = values.shape[0] // 2
+        low, high = (values[:half], values[half:])
+        values = jnp.where(mine, high, low) + exchange(jnp.where(mine, low, high), step)
+    return values[0]
+
+
+def block_span(block, count):
+    reach = -(-WINDOW // BLOCK)
+    return max(0, block - reach), min(count - 1, block + reach)
+
+
+def split_three(values):
+    high = values.astype(jnp.bfloat16)
+    rest = values - high.astype(jnp.float32)
+    mid = rest.astype(jnp.bfloat16)
+    low = (rest - mid.astype(jnp.float32)).astype(jnp.bfloat16)
+    return high, mid, low
+
+
+def window_edge(tile, row_block, column_block):
+    if (abs(row_block - column_block) + 1) * BLOCK - 1 < WINDOW:
+        return tile
+    row = lax.broadcasted_iota(jnp.int32, tile.shape, 0) + row_block * BLOCK
+    column = lax.broadcasted_iota(jnp.int32, tile.shape, 1) + column_block * BLOCK
+    return jnp.where(jnp.abs(row - column) < WINDOW, tile, MASKED)
+
+
+def attend_kernel(seg_ref, q_ref, k_ref, v_ref, out_ref, qx_ref, kx_ref, held_ref):
+    length = q_ref.shape[0]
+    count = length // BLOCK
+    lane = lax.broadcasted_iota(jnp.int32, (length, 128), 1)
+    seg = seg_ref[...]
+    q_heads, k_heads, v_heads = ([], [], [])
+    for head in range(2):
+        own = (lane < 64) if head == 0 else (lane >= 64)
+        extra = lane - 64 if head == 0 else lane
+        same = extra == seg
+        q_extra = jnp.where(same, 1.0, 0.0).astype(jnp.bfloat16)
+        k_extra = jnp.where(
+            extra < 4, jnp.where(same, 0.0, MASKED), jnp.where(extra < 7, -1.0, 0.0)
+        ).astype(jnp.bfloat16)
+        v_extra = jnp.where(extra == 0, 1.0, 0.0).astype(jnp.bfloat16)
+        q_heads.append(jnp.where(own, q_ref[...], q_extra))
+        k_heads.append(jnp.where(own, k_ref[...], k_extra))
+        v_heads.append(jnp.where(own, v_ref[...], v_extra))
+        kx_ref[head] = k_heads[head]
+    units = [(head, block) for head in range(2) for block in range(count)]
+
+    def score(unit):
+        head, block = unit
+        low, high = block_span(block, count)
+        rows = slice(block * BLOCK, (block + 1) * BLOCK)
+        tile = dot_last(q_heads[head][rows], k_heads[head][low * BLOCK : (high + 1) * BLOCK])
+        return [
+            window_edge(tile[:, (at - low) * BLOCK : (at - low + 1) * BLOCK], block, at)
+            for at in range(low, high + 1)
+        ]
+
+    def finish(unit, tiles):
+        head, block = unit
+        low, high = block_span(block, count)
+        rows = slice(block * BLOCK, (block + 1) * BLOCK)
+        most = tiles[0]
+        for tile in tiles[1:]:
+            most = jnp.maximum(most, tile)
+        top = jnp.max(most, axis=1, keepdims=True)
+        raised = jnp.concatenate(
+            [jnp.exp2(tile - top).astype(jnp.bfloat16) for tile in tiles], axis=1
+        )
+        mixed = dot_plain(raised, v_heads[head][low * BLOCK : (high + 1) * BLOCK])
+        norm_sum = mixed[:, 64:65] if head == 0 else mixed[:, 0:1]
+        held_ref[head, rows, :] = mixed * (1.0 / norm_sum)
+        first, second, third = split_three(top + jnp.log2(norm_sum))
+        extra = lane[:BLOCK] - 64 if head == 0 else lane[:BLOCK]
+        qx_ref[head, rows, :] = jnp.where(
+            extra == 4,
+            first,
+            jnp.where(extra == 5, second, jnp.where(extra == 6, third, q_heads[head][rows])),
+        )
+
+    tiles = score(units[0])
+    for at, unit in enumerate(units):
+        following = score(units[at + 1]) if at + 1 < len(units) else None
+        finish(unit, tiles)
+        tiles = following
+    out_ref[...] = jnp.where(lane < 64, held_ref[0], held_ref[1]).astype(jnp.bfloat16)
+
+
+def attend(queries, keys, values, seg):
+    length, width = queries.shape
+    heads = width // HEAD_DIM
+    pair = pl.BlockSpec((length, 128), lambda step: (0, step))
+    padded = pl.BlockSpec((2, length, 128), lambda step: (step, 0, 0))
+    return pl.pallas_call(
+        attend_kernel,
+        grid=(heads // 2,),
+        in_specs=[pl.BlockSpec((length, 1), lambda step: (0, 0)), pair, pair, pair],
+        out_specs=[pair, padded, padded],
+        out_shape=[
+            jax.ShapeDtypeStruct((length, width), jnp.bfloat16),
+            jax.ShapeDtypeStruct((heads, length, 128), jnp.bfloat16),
+            jax.ShapeDtypeStruct((heads, length, 128), jnp.bfloat16),
+        ],
+        scratch_shapes=[pltpu.VMEM((2, length, 128), jnp.float32)],
+        compiler_params=pltpu.CompilerParams(vmem_limit_bytes=40 << 20),
+        cost_estimate=pl.CostEstimate(
+            flops=28 * 10**9, bytes_accessed=16 << 20, transcendentals=heads * length * length
+        ),
+        name="attend",
+    )(seg, queries, keys, values)
+
+
+def attend_back_kernel(qx_ref, kx_ref, v_ref, out_ref, grad_ref, dq_ref, dk_ref, dv_ref, held_ref):
+    length = v_ref.shape[0]
+    count = length // BLOCK
+    lane = lax.broadcasted_iota(jnp.int32, (length, 128), 1)
+    grad = grad_ref[...]
+    for head in range(2):
+        mine = slice(head * 64, (head + 1) * 64)
+        own = (lane < 64) if head == 0 else (lane >= 64)
+        extra = lane - 64 if head == 0 else lane
+        product = jnp.where(
+            own, grad.astype(jnp.float32) * out_ref[...].astype(jnp.float32), 0.0
+        )
+        first, second, third = split_three(-jnp.sum(product, axis=1, keepdims=True))
+        grad_head = jnp.where(
+            own,
+            grad,
+            jnp.where(
+                extra == 0,
+                first,
+                jnp.where(extra == 1, second, jnp.where(extra == 2, third, jnp.zeros_like(grad))),
+            ),
+        )
+        v_head = jnp.where(own, v_ref[...], jnp.where(extra < 3, 1.0, 0.0).astype(jnp.bfloat16))
+        q_head, k_head = (qx_ref[head], kx_ref[head])
+        k_turned = k_head.T[mine]
+        for block in range(count):
+            low, high = block_span(block, count)
+            keys = slice(block * BLOCK, (block + 1) * BLOCK)
+            span = slice(low * BLOCK, (high + 1) * BLOCK)
+            tile = dot_last(k_head[keys], q_head[span])
+            soft = jnp.concatenate(
+                [
+                    jnp.exp2(
+                        window_edge(tile[:, (at - low) * BLOCK : (at - low + 1) * BLOCK], block, at)
+                    )
+                    for at in range(low, high + 1)
+                ],
+                axis=1,
+            )
+            grad_soft = dot_last(v_head[keys], grad_head[span])
+            grad_score = (soft * grad_soft).astype(jnp.bfloat16)
+            grad_value = dot_plain(soft.astype(jnp.bfloat16), grad_head[span])
+            grad_key = dot_plain(grad_score, q_head[span]) * (1.0 / LOG2E)
+            dv_ref[keys, mine] = grad_value[:, mine].astype(jnp.bfloat16)
+            dk_ref[keys, mine] = grad_key[:, mine].astype(jnp.bfloat16)
+            grad_query = dot_plain(k_turned[:, keys], grad_score)
+            if block == 0:
+                held_ref[mine, span] = grad_query
+                if high + 1 < count:
+                    held_ref[mine, (high + 1) * BLOCK :] = jnp.zeros(
+                        (64, length - (high + 1) * BLOCK), jnp.float32
+                    )
+            else:
+                held_ref[mine, span] += grad_query
+    dq_ref[...] = (held_ref[...] * (1.0 / math.sqrt(HEAD_DIM))).T.astype(jnp.bfloat16)
+
+
+def attend_back(q_padded, k_padded, values, mixed, grad_mixed):
+    length, width = values.shape
+    heads = width // HEAD_DIM
+    pair = pl.BlockSpec((length, 128), lambda step: (0, step))
+    padded = pl.BlockSpec((2, length, 128), lambda step: (step, 0, 0))
+    return pl.pallas_call(
+        attend_back_kernel,
+        grid=(heads // 2,),
+        in_specs=[padded, padded, pair, pair, pair],
+        out_specs=[pair, pair, pair],
+        out_shape=[jax.ShapeDtypeStruct((length, width), jnp.bfloat16)] * 3,
+        scratch_shapes=[pltpu.VMEM((128, length), jnp.float32)],
+        compiler_params=pltpu.CompilerParams(vmem_limit_bytes=40 << 20),
+        cost_estimate=pl.CostEstimate(
+            flops=40 * 10**9, bytes_accessed=20 << 20, transcendentals=heads * length * length
+        ),
+        name="attend_back",
+    )(q_padded, k_padded, values, mixed, grad_mixed)
+
+
+def up_kernel(x_ref, w_ref, b_ref, active_ref, slope_ref):
+    length = x_ref.shape[0]
+    count = length // BLOCK
+
+    def product(block):
+        rows = slice(block * BLOCK, (block + 1) * BLOCK)
+        return dot_plain(x_ref[rows], w_ref[...]) + b_ref[...]
+
+    up = product(0)
+    for block in range(count):
+        following = product(block + 1) if block + 1 < count else None
+        rows = slice(block * BLOCK, (block + 1) * BLOCK)
+        cumulative = 0.5 * (1.0 + lax.erf(up * math.sqrt(0.5)))
+        density = jnp.exp2(up * up * (-0.5 * LOG2E)) * (1.0 / math.sqrt(2.0 * math.pi))
+        active_ref[rows] = (up * cumulative).astype(jnp.bfloat16)
+        slope_ref[rows] = (cumulative + up * density).astype(jnp.bfloat16)
+        up = following
+
+
+def up_project(hidden, weight, bias):
+    length, features = hidden.shape
+    width = weight.shape[1]
+    block_width = math.gcd(width, 512)
+    column = pl.BlockSpec((length, block_width), lambda step: (0, step))
+    return pl.pallas_call(
+        up_kernel,
+        grid=(width // block_width,),
+        in_specs=[
+            pl.BlockSpec((length, features), lambda step: (0, 0)),
+            pl.BlockSpec((features, block_width), lambda step: (0, step)),
+            pl.BlockSpec((1, block_width), lambda step: (0, step)),
+        ],
+        out_specs=[column, column],
+        out_shape=[jax.ShapeDtypeStruct((length, width), jnp.bfloat16)] * 2,
+        compiler_params=pltpu.CompilerParams(vmem_limit_bytes=40 << 20),
+        cost_estimate=pl.CostEstimate(
+            flops=2 * length * features * width,
+            bytes_accessed=2 * (length * features + features * width + 2 * length * width),
+            transcendentals=2 * length * width,
+        ),
+        name="up_project",
+    )(hidden, weight, bias)
+
+
+def own_first(row_values, tp_rank, piece_len):
+    mine = lax.dynamic_slice_in_dim(row_values, tp_rank * piece_len, piece_len, 0)
+    theirs = lax.dynamic_slice_in_dim(row_values, (1 - tp_rank) * piece_len, piece_len, 0)
+    return mine, theirs
+
+
+def swap_in(pieces, tp_rank):
+    mine = lax.dynamic_index_in_dim(pieces, tp_rank, 0, keepdims=False)
+    theirs = lax.dynamic_index_in_dim(pieces, 1 - tp_rank, 0, keepdims=False)
+    arrived = exchange(theirs, ("tp", 1))
+    first = tp_rank == 0
+    return jnp.concatenate(
+        [jnp.where(first, mine, arrived), jnp.where(first, arrived, mine)], axis=0
+    )
+
+
+def swap_out(row_values, tp_rank, piece_len):
+    mine, theirs = own_first(row_values, tp_rank, piece_len)
+    arrived = exchange(theirs, ("tp", 1))
+    first = tp_rank == 0
+    return jnp.stack([jnp.where(first, mine, arrived), jnp.where(first, arrived, mine)])
+
+
+def on_device_rows(
+    inputs,
+    segment_ids,
+    valid_mask,
+    teacher,
+    w_query,
+    w_key,
+    w_value,
+    w_out,
+    b_query,
+    b_value,
+    w_up,
+    b_up,
+    w_down,
+    ln_gains,
+    ln_shifts,
+):
+    seq_count, piece_len, features = inputs.shape
+    fsdp_count, tp_count = (lax.axis_size("fsdp"), lax.axis_size("tp"))
+    fsdp_rank, tp_rank = (lax.axis_index("fsdp"), lax.axis_index("tp"))
+    assert seq_count == tp_count
+    total_tokens = seq_count * piece_len * tp_count * fsdp_count
+    shard_rows, local_width = w_query.shape
+    local_hidden = w_up.shape[1]
+    width, hidden_units = (local_width * tp_count, local_hidden * tp_count)
+    place = jnp.stack([fsdp_rank, tp_rank]).astype(jnp.int32)
+
+    row_low = swap_in(inputs, tp_rank)
+    seg = lax.dynamic_index_in_dim(segment_ids, tp_rank, 0, keepdims=False)[:, None]
+
+    half = local_width
+    attend_shard = jnp.concatenate([w_query, w_key, w_value, w_out.T], axis=1)
+    attend_columns = [
+        [(0, half, 0, half, 0), (half, half, 0, half, width)],
+        [(0, half, 0, half, 2 * width), (half, half, 1, half, 0)],
+    ]
+    full_qkv, full_out = gather_group(
+        attend_shard, place, attend_columns, [3 * width, width], "gather_attend"
+    )
+    part_width = local_hidden // 2
+    wide_columns = [
+        [(0, part_width, 0, local_hidden, part * part_width)] for part in range(2)
+    ]
+    (full_up,) = gather_group(w_up, place, wide_columns, [hidden_units], "gather_up")
+    (full_down,) = gather_group(w_down.T, place, wide_columns, [hidden_units], "gather_down")
+
+    valid_row = swap_in(valid_mask[..., None], tp_rank).astype(jnp.float32)
+    small = jnp.concatenate(
+        [
+            b_query.astype(jnp.float32),
+            b_value.astype(jnp.float32),
+            b_up.astype(jnp.float32),
+            ln_gains.astype(jnp.float32).reshape(-1),
+            ln_shifts.astype(jnp.float32).reshape(-1),
+            jnp.sum(valid_mask.astype(jnp.float32))[None],
+        ]
+    )
+    small_len = small.shape[0]
+    padded_len = -(-small_len // 128) * 128
+    small = jnp.pad(small, (0, padded_len - small_len)).reshape(1, padded_len // 128, 128)
+    small_all = gather_small(small).reshape(tp_count * fsdp_count, padded_len)
+    cuts = []
+    at = 0
+    for count in (b_query.size, b_value.size, b_up.size, ln_gains.size, ln_shifts.size, 1):
+        cuts.append(small_all[:, at : at + count])
+        at += count
+    bias_query, bias_value, bias_up = (cuts[0].reshape(-1), cuts[1].reshape(-1), cuts[2].reshape(-1))
+
+    def feature_rows(columns, rows):
+        return (
+            columns[:fsdp_count]
+            .reshape(fsdp_count, rows, features // fsdp_count)
+            .transpose(1, 0, 2)
+            .reshape(rows, features)
+        )
+
+    gains = feature_rows(cuts[3], 2)
+    shifts = feature_rows(cuts[4], 4)
+    valid_count = jnp.sum(cuts[5])
+    teacher_row = swap_in(teacher, tp_rank).astype(jnp.float32)
+
+    scale = LOG2E / math.sqrt(HEAD_DIM)
+    queries = (
+        (dot_plain(row_low, full_qkv[:, :width]) + bias_query) * scale
+    ).astype(jnp.bfloat16)
+    keys = dot_plain(row_low, full_qkv[:, width : 2 * width]).astype(jnp.bfloat16)
+    values = (dot_plain(row_low, full_qkv[:, 2 * width :]) + bias_value).astype(jnp.bfloat16)
+    mixed, q_padded, k_padded = attend(queries, keys, values, seg)
+    pre_first = row_low.astype(jnp.float32) + dot_last(mixed, full_out) + shifts[2]
+    normed_first, unit_first, inverse_first = layer_norm_parts(pre_first, gains[0], shifts[0])
+    hidden_low = normed_first.astype(jnp.bfloat16)
+    active, slope = up_project(hidden_low, full_up, bias_up[None])
+    pre_second = normed_first + dot_last(active, full_down) + shifts[3]
+    result, unit_second, inverse_second = layer_norm_parts(pre_second, gains[1], shifts[1])
+    hidden_out = swap_out(result.astype(jnp.bfloat16), tp_rank, piece_len)
+
+    differ = result - teacher_row
+    grad_result = valid_row * differ * (total_tokens / valid_count)
+    squares = jnp.sum(valid_row * differ * differ)
+    grad_second = norm_backward(unit_second, inverse_second, gains[1], grad_result)
+    grad_down = grad_second.astype(jnp.bfloat16)
+    weight_down = dot_first(grad_down, active).astype(jnp.bfloat16)
+    grad_w_down = scatter_group(
+        [weight_down], place, wide_columns, shard_rows, part_width, "scatter_down"
+    ).T
+    grad_up = (dot_plain(grad_down, full_down) * slope.astype(jnp.float32)).astype(jnp.bfloat16)
+    grad_b_up = jnp.sum(grad_up.astype(jnp.float32), axis=0)
+    weight_up = dot_first(hidden_low, grad_up).astype(jnp.bfloat16)
+    grad_w_up = scatter_group(
+        [weight_up], place, wide_columns, shard_rows, part_width, "scatter_up"
+    )
+    grad_hidden = grad_second + dot_last(grad_up, full_up)
+    grad_first = norm_backward(unit_first, inverse_first, gains[0], grad_hidden)
+    grad_attend = grad_first.astype(jnp.bfloat16)
+    weight_out = dot_first(grad_attend, mixed).astype(jnp.bfloat16)
+    grad_mixed = dot_plain(grad_attend, full_out).astype(jnp.bfloat16)
+    grad_query, grad_key, grad_value = attend_back(q_padded, k_padded, values, mixed, grad_mixed)
+    grad_row = (
+        grad_first
+        + dot_last(grad_query, full_qkv[:, :width])
+        + dot_last(grad_key, full_qkv[:, width : 2 * width])
+        + dot_last(grad_value, full_qkv[:, 2 * width :])
+    ).astype(jnp.bfloat16)
+    grad_inputs = swap_out(grad_row, tp_rank, piece_len)
+    weight_qkv = [
+        dot_first(row_low, part).astype(jnp.bfloat16) for part in (grad_query, grad_key, grad_value)
+    ]
+    split_columns = [
+        [(0, half, 0, half, 0), (half, half, 1, half, 0)],
+        [(0, half, 2, half, 0), (half, half, 3, half, 0)],
+    ]
+    grad_attend_shard = scatter_group(
+        weight_qkv + [weight_out], place, split_columns, shard_rows, 2 * half, "scatter_attend"
+    )
+    grad_w_query, grad_w_key, grad_w_value, grad_w_out = [
+        grad_attend_shard[:, at * half : (at + 1) * half] for at in range(4)
+    ]
+
+    def feature_pieces(rows):
+        pieces = rows.reshape(rows.shape[0], fsdp_count, -1).transpose(1, 0, 2).reshape(fsdp_count, -1)
+        return jnp.concatenate([pieces] * tp_count, axis=0)
+
+    devices = tp_count * fsdp_count
+    pieces = jnp.concatenate(
+        [
+            jnp.sum(grad_query.astype(jnp.float32), axis=0).reshape(devices, -1),
+            jnp.sum(grad_value.astype(jnp.float32), axis=0).reshape(devices, -1),
+            grad_b_up.reshape(devices, -1),
+            feature_pieces(
+                jnp.stack(
+                    [
+                        jnp.sum(grad_hidden * unit_first, axis=0),
+                        jnp.sum(grad_result * unit_second, axis=0),
+                    ]
+                )
+            ),
+            feature_pieces(
+                jnp.stack(
+                    [
+                        jnp.sum(grad_hidden, axis=0),
+                        jnp.sum(grad_result, axis=0),
+                        jnp.sum(grad_first, axis=0),
+                        jnp.sum(grad_second, axis=0),
+                    ]
+                )
+            ),
+            jnp.full((devices, 1), squares),
+        ],
+        axis=1,
+    )
+    pieces = jnp.pad(pieces, ((0, 0), (0, padded_len - small_len)))
+    own = scatter_small(pieces.reshape(devices, padded_len // 128, 128)).reshape(padded_len)
+    results = []
+    at = 0
+    for count in (b_query.size, b_value.size, b_up.size, ln_gains.size, ln_shifts.size, 1):
+        results.append(own[at : at + count])
+        at += count
+    loss_value = results[5][0] / (features * valid_count)
+    return (
+        hidden_out,
+        loss_value,
+        grad_inputs,
+        grad_w_query,
+        grad_w_key,
+        grad_w_value,
+        grad_w_out.T,
+        results[0],
+        results[1],
+        grad_w_up,
+        results[2],
+        grad_w_down,
+        results[3].reshape(ln_gains.shape),
+        results[4].reshape(ln_shifts.shape),
+    )
+
+
 def solution(mesh):
     in_specs = (
         P("fsdp", "tp", None),
@@ -386,6 +1014,7 @@
         P(None, "fsdp"),
         P(None, "fsdp"),
     )
+    rows_plan = rows_plan_fits(mesh)
     return jax.shard_map(
-        on_device, mesh=mesh, in_specs=in_specs, out_specs=out_specs, check_vma=False
-    )
+        on_device_rows if rows_plan else on_device_heads, mesh=mesh, in_specs=in_specs, out_specs=out_specs, check_vma=False
+    )

time: 1550 us -> 2330 us (1.50)
  Pallas kernels: 0 us -> 1620 us
  waiting for transfers between devices: 761 us -> 395 us
  blocking collectives: 211 us -> 0 us
  matrix products: 332 us -> 126 us
  starting transfers between devices: 1.38 us -> 78.3 us
  other arithmetic: 134 us -> 62.8 us
  local copies, waits for them, and re-layouts: 86.6 us -> 33.3 us
    pallas_call x0 -> x9, Pallas kernels: none -> 1620 us  [the longest x6 1540 us: run_assemble(): pl.pallas_call(partial(assemble_kernel, plan), in_specs=[pl.BlockSpec(mem...]
    ppermute x0 -> x81, waiting for transfers between devices: none -> 395 us  [exchange(): lax.ppermute(values, axis, [(index, index ^ bit) for index in range(count)])]
    reduce_scatter x5 -> x0, waiting for transfers between devices: 219 us -> none  [the longest x1 74 us: on_device(): lax.psum_scatter(weight_up.astype(jnp.bfloat16), 'fsdp', scatter_dimensio...]
    dot_general x30 -> x5, matrix products: 231 us -> 26.2 us  [dot_plain(): lax.dot_general(left_side, right_side, (((1,), (0,)), ((), ())), preferre...]
    all_gather x8 -> x0, waiting for transfers between devices: 195 us -> none  [the longest x1 56.7 us: on_device(): lax.all_gather(grad_second.astype(jnp.bfloat16), 'tp', axis=1, tiled=True)]
    unnamed x25 -> x0, waiting for transfers between devices: 192 us -> none
    psum x2 -> x0, waiting for transfers between devices: 155 us -> none  [the longest x1 107 us: on_device(): lax.psum(hidden_part.astype(jnp.bfloat16), 'tp').astype(jnp.float32)]
    psum x3 -> x0, blocking collectives: 88.7 us -> none  [the longest x2 81 us: on_device(): lax.psum((jnp.sum(mask_float * differ * differ), jnp.sum(mask_float)), ('...]
  transfers between devices with their start and end apart: 20 -> 81, of which waited for: 16 -> 27; matrix products, arithmetic and copies ran while one was open for 16% -> 4% of each run, Pallas kernels for 0% -> 46%
where the time goes in v1:
time: 2330 us
  Pallas kernels  1620 us (70%)
  waiting for transfers between devices  395 us (17%)
  matrix products  126 us (5%)
  starting transfers between devices  78.3 us (3%)
  other arithmetic  62.8 us (3%)
  local copies, waits for them, and re-layouts  33.3 us (1%)
    pallas_call x6, Pallas kernels, run_assemble(): pl.pallas_call(partial(assemble_kernel, plan), in_specs=[pl.BlockSpec(mem...  1540 us
    ppermute x81, waiting for transfers between devices, exchange(): lax.ppermute(values, axis, [(index, index ^ bit) for index in range(count)])  395 us
    ppermute x81, starting transfers between devices, exchange(): lax.ppermute(values, axis, [(index, index ^ bit) for index in range(count)])  78.3 us
    dot_general x6, matrix products, dot_last(): lax.dot_general(left_side, right_side, (((1,), (1,)), ((), ())), preferre...  54.3 us
  transfers between devices with their start and end apart: 81, of which 27 were waited for; matrix products, arithmetic and copies ran while one was open for 4% of the time, Pallas kernels for 46%

profile of v1, /device:TPU:0, one launch (start us, length us, event | category | flops | bytes accessed | tf_op | source)
XLA Modules:
  0.0 2325.3 jit_solution(2855425662715564233)
XLA Ops:
  76.8 32.8 %collective-permute-done.17 = f32[16,5,128]{2,1,0:T(8,128)S(1)} collective-permute-done((f32[16,5,128]{2,1,0:T(8,128)S(1)}, f32[16,5,128]{2,1,0:T(8,128)S(1)}, u32[]{:S(2)}, u32[]{:S(2)}) %collective-permute-start.17) | collective-permute-done | bytes 40992 | tf_op jit(solution)/shard_map/ppermute | solution.py:376
  133.9 17.1 collective-permute-done.38
  173.0 255.9 %gather_attend.1 = (bf16[1024,3072]{1,0:T(8,128)(2,1)}, bf16[1024,1024]{1,0:T(8,128)(2,1)}) custom-call(s32[2]{0:T(128)} %pad_add_fusion.place_ref, bf16[8,64,1024]{2,1,0:T(8,128)(2,1)} %copy-done.18, bf16[8,64,1024]{2,1,0:T(8,128)(2,1)} %collective-permute-done.4.refs_1_, bf16[8,64,1024]{2,1,0:T(8,128)(2,1)} %copy-done.45, ...), custom_call_target="tpu_custom_call" | custom-call | bytes 16777216 | tf_op jit(solution)/shard_map/gather_attend/pallas_call | solution.py:458
  438.1 27.2 %attend.1 = (bf16[1024,1024]{1,0:T(8,128)(2,1)S(1)}, bf16[16,1024,128]{2,1,0:T(8,128)(2,1)S(1)}, bf16[16,1024,128]{2,1,0:T(8,128)(2,1)}) custom-call(s32[1024,1]{1,0:T(8,128)S(1)} %copy.30.seg_ref, bf16[1024,1024]{1,0:T(8,128)(2,1)S(1)} %multiply_convert_fusion.1.q_ref, bf16[1024,1024]{1,0:T(8,128)(2,1)S(1)} %convolution_convert_fusion.7.k_ref, ...), custom_call_target="tpu_custom_call" | custom-call | flops 28000000000 | bytes 16777216 | tf_op jit(solution)/shard_map/attend/pallas_call | solution.py:624
  472.7 18.3 collective-permute-done.39.refs_5_
  491.5 255.9 %gather_up.1.w_ref = bf16[1024,4096]{1,0:T(8,128)(2,1)} custom-call(s32[2]{0:T(128)} %pad_add_fusion.place_ref, bf16[8,64,1024]{2,1,0:T(8,128)(2,1)} %pad_maximum_fusion.6.refs_0_, bf16[8,64,1024]{2,1,0:T(8,128)(2,1)} %collective-permute-done.21.refs_1_, bf16[8,64,1024]{2,1,0:T(8,128)(2,1)} %collective-permute-done.22.refs_2_, ...), custom_call_target="tpu_custom_call" | custom-call | bytes 16777216 | tf_op jit(solution)/shard_map/gather_up/pallas_call | solution.py:458
  750.3 18.5 up_project.1
  772.1 255.9 %gather_down.1 = bf16[1024,4096]{1,0:T(8,128)(2,1)} custom-call(s32[2]{0:T(128)} %pad_add_fusion.place_ref, bf16[8,64,1024]{2,1,0:T(8,128)(2,1)} %pad_maximum_fusion.8.refs_0_, bf16[8,64,1024]{2,1,0:T(8,128)(2,1)} %collective-permute-done.33.refs_1_, bf16[8,64,1024]{2,1,0:T(8,128)(2,1)} %collective-permute-done.34.refs_2_, ...), custom_call_target="tpu_custom_call" | custom-call | bytes 16777216 | tf_op jit(solution)/shard_map/gather_down/pallas_call | solution.py:458
  1028.0 15.3 fusion.29
  1054.9 14.0 convolution_convert_fusion.refs_0_
  1069.0 14.7 convert_reduce_fusion
  1083.7 14.8 convolution_convert_fusion.1.refs_0_
  1098.5 15.6 multiply_reduce_fusion.1
  1121.8 43.1 %attend_back.1 = (bf16[1024,1024]{1,0:T(8,128)(2,1)S(1)}, bf16[1024,1024]{1,0:T(8,128)(2,1)S(1)}, bf16[1024,1024]{1,0:T(8,128)(2,1)S(1)}) custom-call(bf16[16,1024,128]{2,1,0:T(8,128)(2,1)} %copy-done.10, bf16[16,1024,128]{2,1,0:T(8,128)(2,1)} %get-tuple-element.41.kx_ref, bf16[1024,1024]{1,0:T(8,128)(2,1)S(1)} %copy-done.9, ...), custom_call_target="tpu_custom_call" | custom-call | flops 40000000000 | bytes 20971520 | tf_op jit(solution)/shard_map/attend_back/pallas_call | solution.py:705
  1175.5 255.9 %scatter_down.1 = (bf16[16,64,1024]{2,1,0:T(8,128)(2,1)}, bf16[16,64,1024]{2,1,0:T(8,128)(2,1)}, bf16[16,64,1024]{2,1,0:T(8,128)(2,1)}, bf16[16,64,1024]{2,1,0:T(8,128)(2,1)}) custom-call(s32[2]{0:T(128)} %pad_add_fusion.place_ref, bf16[1024,4096]{1,0:T(8,128)(2,1)} %convolution_convert_fusion.refs_0_), custom_call_target="tpu_custom_call" | custom-call | bytes 16777216 | tf_op jit(solution)/shard_map/scatter_down/pallas_call | solution.py:458
  1467.0 255.9 %scatter_up.1 = (bf16[16,64,1024]{2,1,0:T(8,128)(2,1)}, bf16[16,64,1024]{2,1,0:T(8,128)(2,1)}, bf16[16,64,1024]{2,1,0:T(8,128)(2,1)}, bf16[16,64,1024]{2,1,0:T(8,128)(2,1)}) custom-call(s32[2]{0:T(128)} %pad_add_fusion.place_ref, bf16[1024,4096]{1,0:T(8,128)(2,1)} %convolution_convert_fusion.1.refs_0_), custom_call_target="tpu_custom_call" | custom-call | bytes 16777216 | tf_op jit(solution)/shard_map/scatter_up/pallas_call | solution.py:458
  1728.4 256.0 %scatter_attend.1 = (bf16[16,64,1024]{2,1,0:T(8,128)(2,1)}, bf16[16,64,1024]{2,1,0:T(8,128)(2,1)}, bf16[16,64,1024]{2,1,0:T(8,128)(2,1)}, bf16[16,64,1024]{2,1,0:T(8,128)(2,1)}) custom-call(s32[2]{0:T(128)} %pad_add_fusion.place_ref, bf16[1024,1024]{1,0:T(8,128)(2,1)} %convolution_convert_fusion.5.refs_0_, ...), custom_call_target="tpu_custom_call" | custom-call | bytes 16777216 | tf_op jit(solution)/shard_map/scatter_attend/pallas_call | solution.py:458
  2014.3 122.7 %collective-permute-done.72 = bf16[8,64,1024]{2,1,0:T(8,128)(2,1)S(1)} collective-permute-done((bf16[8,64,1024]{2,1,0:T(8,128)(2,1)S(1)}, bf16[8,64,1024]{2,1,0:T(8,128)(2,1)S(1)}, u32[]{:S(2)}, u32[]{:S(2)}) %collective-permute-start.72) | collective-permute-done | bytes 1048608 | tf_op jit(solution)/shard_map/ppermute | solution.py:376
  2137.4 44.5 %collective-permute-done.77 = bf16[8,64,1024]{2,1,0:T(8,128)(2,1)S(1)} collective-permute-done((bf16[8,64,1024]{2,1,0:T(8,128)(2,1)S(1)}, bf16[8,64,1024]{2,1,0:T(8,128)(2,1)S(1)}, u32[]{:S(2)}, u32[]{:S(2)}) %collective-permute-start.77) | collective-permute-done | bytes 1048608 | tf_op jit(solution)/shard_map/ppermute | solution.py:376
  2182.4 22.1 collective-permute-done.62
  2206.3 20.7 collective-permute-done.67
  2227.4 22.0 collective-permute-done.57
  2251.3 20.2 collective-permute-done.52
  2273.3 9.6 collective-permute-done.73
  (447 shorter events, 290.9 us)
Async XLA Ops:
  60.9 90.0 %collective-permute-start = (bf16[512,1024]{1,0:T(8,128)(2,1)}, bf16[512,1024]{1,0:T(8,128)(2,1)}, u32[]{:S(2)}, u32[]{:S(2)}) collective-permute-start(bf16[512,1024]{1,0:T(8,128)(2,1)} %dynamic-slice_bitcast_fusion.1), channel_id=1, source_target_pairs={{0,1},{1,0},{2,3},{3,2},{4,5},{5,4},{6,7},{7,6},{8,9},{9,8},{10,11... | collective-permute-start | bytes 3145736 | tf_op jit(solution)/shard_map/ppermute | solution.py:376
  163.5 301.8 %collective-permute-start.21 = (bf16[8,64,1024]{2,1,0:T(8,128)(2,1)}, bf16[8,64,1024]{2,1,0:T(8,128)(2,1)}, u32[]{:S(2)}, u32[]{:S(2)}) collective-permute-start(bf16[8,64,1024]{2,1,0:T(8,128)(2,1)} %pad_maximum_fusion.6.refs_0_), channel_id=1, source_target_pairs={{0,4},{2,6},{4,0},{6,2},{8,12},{10,14},{12,8},{14,10},{16,20},{18,... | collective-permute-start | bytes 3145736 | tf_op jit(solution)/shard_map/ppermute | solution.py:376
  166.8 299.6 %collective-permute-start.22 = (bf16[8,64,1024]{2,1,0:T(8,128)(2,1)}, bf16[8,64,1024]{2,1,0:T(8,128)(2,1)}, u32[]{:S(2)}, u32[]{:S(2)}) collective-permute-start(bf16[8,64,1024]{2,1,0:T(8,128)(2,1)} %pad_maximum_fusion.6.refs_0_), channel_id=1, source_target_pairs={{0,2},{2,0},{4,6},{6,4},{8,10},{10,8},{12,14},{14,12},{16,18},{18,... | collective-permute-start | bytes 3145736 | tf_op jit(solution)/shard_map/ppermute | solution.py:376
  167.8 298.6 %collective-permute-start.27 = (bf16[8,64,1024]{2,1,0:T(8,128)(2,1)}, bf16[8,64,1024]{2,1,0:T(8,128)(2,1)S(1)}, u32[]{:S(2)}, u32[]{:S(2)}) collective-permute-start(bf16[8,64,1024]{2,1,0:T(8,128)(2,1)} %pad_maximum_fusion.7.refs_4_), channel_id=1, source_target_pairs={{0,8},{2,10},{4,12},{6,14},{8,0},{10,2},{12,4},{14,6},{16,24},{18,... | collective-permute-start | bytes 3145736 | tf_op jit(solution)/shard_map/ppermute | solution.py:376
  172.7 299.4 %collective-permute-start.28 = (bf16[8,64,1024]{2,1,0:T(8,128)(2,1)}, bf16[8,64,1024]{2,1,0:T(8,128)(2,1)}, u32[]{:S(2)}, u32[]{:S(2)}) collective-permute-start(bf16[8,64,1024]{2,1,0:T(8,128)(2,1)} %pad_maximum_fusion.7.refs_4_), channel_id=1, source_target_pairs={{0,2},{2,0},{4,6},{6,4},{8,10},{10,8},{12,14},{14,12},{16,18},{18,... | collective-permute-start | bytes 3145736 | tf_op jit(solution)/shard_map/ppermute | solution.py:376
  172.7 299.5 %collective-permute-start.33 = (bf16[8,64,1024]{2,1,0:T(8,128)(2,1)}, bf16[8,64,1024]{2,1,0:T(8,128)(2,1)}, u32[]{:S(2)}, u32[]{:S(2)}) collective-permute-start(bf16[8,64,1024]{2,1,0:T(8,128)(2,1)} %pad_maximum_fusion.8.refs_0_), channel_id=1, source_target_pairs={{0,4},{2,6},{4,0},{6,2},{8,12},{10,14},{12,8},{14,10},{16,20},{18,... | collective-permute-start | bytes 3145736 | tf_op jit(solution)/shard_map/ppermute | solution.py:376
  472.1 300.0 %collective-permute-start.34 = (bf16[8,64,1024]{2,1,0:T(8,128)(2,1)}, bf16[8,64,1024]{2,1,0:T(8,128)(2,1)}, u32[]{:S(2)}, u32[]{:S(2)}) collective-permute-start(bf16[8,64,1024]{2,1,0:T(8,128)(2,1)} %pad_maximum_fusion.8.refs_0_), channel_id=1, source_target_pairs={{0,2},{2,0},{4,6},{6,4},{8,10},{10,8},{12,14},{14,12},{16,18},{18,... | collective-permute-start | bytes 3145736 | tf_op jit(solution)/shard_map/ppermute | solution.py:376
  472.2 299.9 %collective-permute-start.40 = (bf16[8,64,1024]{2,1,0:T(8,128)(2,1)}, bf16[8,64,1024]{2,1,0:T(8,128)(2,1)}, u32[]{:S(2)}, u32[]{:S(2)}) collective-permute-start(bf16[8,64,1024]{2,1,0:T(8,128)(2,1)} %pad_maximum_fusion.9.refs_4_), channel_id=1, source_target_pairs={{0,2},{2,0},{4,6},{6,4},{8,10},{10,8},{12,14},{14,12},{16,18},{18,... | collective-permute-start | bytes 3145736 | tf_op jit(solution)/shard_map/ppermute | solution.py:376
  491.0 281.1 %collective-permute-start.35 = (bf16[8,64,1024]{2,1,0:T(8,128)(2,1)}, bf16[8,64,1024]{2,1,0:T(8,128)(2,1)}, u32[]{:S(2)}, u32[]{:S(2)}) collective-permute-start(bf16[8,64,1024]{2,1,0:T(8,128)(2,1)} %collective-permute-done.33.refs_1_), channel_id=1, source_target_pairs={{0,2},{2,0},{4,6},{6,4},{8,10},{10,8},{12,14},{14,12},{16,18},{18,... | collective-permute-start | bytes 3145736 | tf_op jit(solution)/shard_map/ppermute | solution.py:376
  491.0 281.1 %collective-permute-start.41 = (bf16[8,64,1024]{2,1,0:T(8,128)(2,1)}, bf16[8,64,1024]{2,1,0:T(8,128)(2,1)}, u32[]{:S(2)}, u32[]{:S(2)}) collective-permute-start(bf16[8,64,1024]{2,1,0:T(8,128)(2,1)} %collective-permute-done.39.refs_5_), channel_id=1, source_target_pairs={{0,2},{2,0},{4,6},{6,4},{8,10},{10,8},{12,14},{14,12},{16,18},{18,... | collective-permute-start | bytes 3145736 | tf_op jit(solution)/shard_map/ppermute | solution.py:376
  1431.4 557.3 %collective-permute-start.71 = (bf16[16,64,1024]{2,1,0:T(8,128)(2,1)}, bf16[16,64,1024]{2,1,0:T(8,128)(2,1)}, u32[]{:S(2)}, u32[]{:S(2)}) collective-permute-start(bf16[16,64,1024]{2,1,0:T(8,128)(2,1)} %get-tuple-element.55), channel_id=1, source_target_pairs={{0,2},{2,0},{4,6},{6,4},{8,10},{10,8},{12,14},{14,12},{16,18},{18,... | collective-permute-start | bytes 6291464 | tf_op jit(solution)/shard_map/ppermute | solution.py:376
  1431.4 566.3 %collective-permute-start.76 = (bf16[16,64,1024]{2,1,0:T(8,128)(2,1)}, bf16[16,64,1024]{2,1,0:T(8,128)(2,1)}, u32[]{:S(2)}, u32[]{:S(2)}) collective-permute-start(bf16[16,64,1024]{2,1,0:T(8,128)(2,1)} %get-tuple-element.57), channel_id=1, source_target_pairs={{0,2},{2,0},{4,6},{6,4},{8,10},{10,8},{12,14},{14,12},{16,18},{18,... | collective-permute-start | bytes 6291464 | tf_op jit(solution)/shard_map/ppermute | solution.py:376
  1457.5 526.9 %collective-permute-start.50 = (bf16[512,1024]{1,0:T(8,128)(2,1)}, bf16[512,1024]{1,0:T(8,128)(2,1)}, u32[]{:S(2)}, u32[]{:S(2)}) collective-permute-start(bf16[512,1024]{1,0:T(8,128)(2,1)} %constant_dynamic-slice_fusion), channel_id=1, source_target_pairs={{0,1},{1,0},{2,3},{3,2},{4,5},{5,4},{6,7},{7,6},{8,9},{9,8},{10,11... | collective-permute-start | bytes 3145736 | tf_op jit(solution)/shard_map/ppermute | solution.py:376
  1460.8 523.7 %collective-permute-start.42 = (bf16[512,1024]{1,0:T(8,128)(2,1)}, bf16[512,1024]{1,0:T(8,128)(2,1)}, u32[]{:S(2)}, u32[]{:S(2)}) collective-permute-start(bf16[512,1024]{1,0:T(8,128)(2,1)} %constant_dynamic-slice_fusion.3), channel_id=1, source_target_pairs={{0,1},{1,0},{2,3},{3,2},{4,5},{5,4},{6,7},{7,6},{8,9},{9,8},{10,11... | collective-permute-start | bytes 3145736 | tf_op jit(solution)/shard_map/ppermute | solution.py:376
  1463.0 260.0 %collective-permute-start.49 = (f32[1,5,128]{2,1,0:T(8,128)S(1)}, f32[1,5,128]{2,1,0:T(8,128)S(1)}, u32[]{:S(2)}, u32[]{:S(2)}) collective-permute-start(f32[1,5,128]{2,1,0:T(8,128)S(1)} %slice_select_fusion.3), channel_id=1, source_target_pairs={{0,2},{2,0},{4,6},{6,4},{8,10},{10,8},{12,14},{14,12},{16,18},{18,... | collective-permute-start | bytes 7688 | tf_op jit(solution)/shard_map/ppermute | solution.py:376
  1722.9 277.4 %collective-permute-start.61 = (bf16[16,64,1024]{2,1,0:T(8,128)(2,1)}, bf16[16,64,1024]{2,1,0:T(8,128)(2,1)}, u32[]{:S(2)}, u32[]{:S(2)}) collective-permute-start(bf16[16,64,1024]{2,1,0:T(8,128)(2,1)} %get-tuple-element.51), channel_id=1, source_target_pairs={{0,2},{2,0},{4,6},{6,4},{8,10},{10,8},{12,14},{14,12},{16,18},{18,... | collective-permute-start | bytes 6291464 | tf_op jit(solution)/shard_map/ppermute | solution.py:376
  1997.8 139.2 %collective-permute-start.72 = (bf16[8,64,1024]{2,1,0:T(8,128)(2,1)S(1)}, bf16[8,64,1024]{2,1,0:T(8,128)(2,1)S(1)}, u32[]{:S(2)}, u32[]{:S(2)}) collective-permute-start(bf16[8,64,1024]{2,1,0:T(8,128)(2,1)S(1)} %get-tuple-element.79), channel_id=1, source_target_pairs={{0,16},{2,18},{4,20},{6,22},{8,24},{10,26},{12,28},{14,30},{16,0},... | collective-permute-start | bytes 3145736 | tf_op jit(solution)/shard_map/ppermute | solution.py:376
  2000.3 181.6 %collective-permute-start.77 = (bf16[8,64,1024]{2,1,0:T(8,128)(2,1)S(1)}, bf16[8,64,1024]{2,1,0:T(8,128)(2,1)S(1)}, u32[]{:S(2)}, u32[]{:S(2)}) collective-permute-start(bf16[8,64,1024]{2,1,0:T(8,128)(2,1)S(1)} %get-tuple-element.81), channel_id=1, source_target_pairs={{0,16},{2,18},{4,20},{6,22},{8,24},{10,26},{12,28},{14,30},{16,0},... | collective-permute-start | bytes 3145736 | tf_op jit(solution)/shard_map/ppermute | solution.py:376
  2005.2 199.3 %collective-permute-start.62 = (bf16[8,64,1024]{2,1,0:T(8,128)(2,1)S(1)}, bf16[8,64,1024]{2,1,0:T(8,128)(2,1)S(1)}, u32[]{:S(2)}, u32[]{:S(2)}) collective-permute-start(bf16[8,64,1024]{2,1,0:T(8,128)(2,1)S(1)} %get-tuple-element.83), channel_id=1, source_target_pairs={{0,16},{2,18},{4,20},{6,22},{8,24},{10,26},{12,28},{14,30},{16,0},... | collective-permute-start | bytes 3145736 | tf_op jit(solution)/shard_map/ppermute | solution.py:376
  2008.0 218.9 %collective-permute-start.67 = (bf16[8,64,1024]{2,1,0:T(8,128)(2,1)S(1)}, bf16[8,64,1024]{2,1,0:T(8,128)(2,1)S(1)}, u32[]{:S(2)}, u32[]{:S(2)}) collective-permute-start(bf16[8,64,1024]{2,1,0:T(8,128)(2,1)S(1)} %get-tuple-element.85), channel_id=1, source_target_pairs={{0,16},{2,18},{4,20},{6,22},{8,24},{10,26},{12,28},{14,30},{16,0},... | collective-permute-start | bytes 3145736 | tf_op jit(solution)/shard_map/ppermute | solution.py:376
  2012.7 236.7 %collective-permute-start.57 = (bf16[8,64,1024]{2,1,0:T(8,128)(2,1)S(1)}, bf16[8,64,1024]{2,1,0:T(8,128)(2,1)S(1)}, u32[]{:S(2)}, u32[]{:S(2)}) collective-permute-start(bf16[8,64,1024]{2,1,0:T(8,128)(2,1)S(1)} %get-tuple-element.87), channel_id=1, source_target_pairs={{0,16},{2,18},{4,20},{6,22},{8,24},{10,26},{12,28},{14,30},{16,0},... | collective-permute-start | bytes 3145736 | tf_op jit(solution)/shard_map/ppermute | solution.py:376
  2137.0 134.5 %collective-permute-start.52 = (bf16[8,64,1024]{2,1,0:T(8,128)(2,1)S(1)}, bf16[8,64,1024]{2,1,0:T(8,128)(2,1)S(1)}, u32[]{:S(2)}, u32[]{:S(2)}) collective-permute-start(bf16[8,64,1024]{2,1,0:T(8,128)(2,1)S(1)} %get-tuple-element.89), channel_id=1, source_target_pairs={{0,16},{2,18},{4,20},{6,22},{8,24},{10,26},{12,28},{14,30},{16,0},... | collective-permute-start | bytes 3145736 | tf_op jit(solution)/shard_map/ppermute | solution.py:376
  2181.9 101.0 %collective-permute-start.73 = (bf16[4,64,1024]{2,1,0:T(8,128)(2,1)S(1)}, bf16[4,64,1024]{2,1,0:T(8,128)(2,1)S(1)}, u32[]{:S(2)}, u32[]{:S(2)}) collective-permute-start(bf16[4,64,1024]{2,1,0:T(8,128)(2,1)S(1)} %get-tuple-element.99), channel_id=1, source_target_pairs={{0,8},{2,10},{4,12},{6,14},{8,0},{10,2},{12,4},{14,6},{16,24},{18,... | collective-permute-start | bytes 1572872 | tf_op jit(solution)/shard_map/ppermute | solution.py:376
  2204.5 78.7 %collective-permute-start.78 = (bf16[4,64,1024]{2,1,0:T(8,128)(2,1)S(1)}, bf16[4,64,1024]{2,1,0:T(8,128)(2,1)S(1)}, u32[]{:S(2)}, u32[]{:S(2)}) collective-permute-start(bf16[4,64,1024]{2,1,0:T(8,128)(2,1)S(1)} %get-tuple-element.101), channel_id=1, source_target_pairs={{0,1},{1,0},{2,3},{3,2},{4,5},{5,4},{6,7},{7,6},{8,9},{9,8},{10,11... | collective-permute-start | bytes 1572872 | tf_op jit(solution)/shard_map/ppermute | solution.py:376
  (121 other events, 2654.6 us)

commit v2 on v1

--- a/solution.py
+++ b/solution.py
@@ -396,12 +396,43 @@
     return masks
 
 
-def gather_part(shard, order, core):
-    held = shard[None]
-    for step in order[:-1]:
-        held = jnp.concatenate([held, exchange(held, step)], axis=0)
-    other = exchange(held, order[-1])
-    return [held, other, exchange(held, core), exchange(other, core)]
+def tie(values, *others):
+    return lax.optimization_barrier((values, others))[0]
+
+
+class GatherChain:
+
+    def __init__(self, shard):
+        self.core, self.orders = step_orders()
+        half = shard.shape[1] // 2
+        self.part_width = half
+        self.held = [shard[None, :, :half], shard[None, :, half:]]
+        self.arrived = None
+        self.at = 0
+
+    def advance(self, *after):
+        if self.arrived is not None:
+            self.held = [
+                jnp.concatenate(pair, axis=0) for pair in zip(self.held, self.arrived)
+            ]
+        if after:
+            self.held = tie(self.held, *after)
+        self.arrived = [
+            exchange(held, order[self.at]) for held, order in zip(self.held, self.orders)
+        ]
+        self.at += 1
+
+    def finish(self, *after):
+        if after:
+            self.arrived = tie(self.arrived, *after)
+        self.pieces = []
+        for held, arrived in zip(self.held, self.arrived):
+            self.pieces.append(
+                [held, arrived, exchange(held, self.core), exchange(arrived, self.core)]
+            )
+
+    def marks(self):
+        return self.held
 
 
 def gather_masks(order, core):
@@ -415,72 +446,113 @@
     return (left_side.astype(jnp.float32) + right_side.astype(jnp.float32)).astype(jnp.bfloat16)
 
 
-def scatter_part(kept, sent, order, core):
-    received = exchange(sent, core)
-    for step in order:
-        half = kept.shape[0] // 2
-        outgoing = add_low(kept[half:], received[half:])
-        arrived = exchange(outgoing, step)
-        kept, received = (add_low(kept[:half], received[:half]), arrived)
-    return kept[0].astype(jnp.float32) + received[0].astype(jnp.float32)
+class ScatterChain:
+
+    def __init__(self, pieces):
+        self.core, orders = step_orders()
+        self.orders = [tuple(reversed(order)) for order in orders]
+        self.kept = [pieces[0], pieces[2]]
+        self.sent = [pieces[1], pieces[3]]
+        self.arrived = [exchange(sent, self.core) for sent in self.sent]
+        self.at = 0
+
+    def advance(self, *after):
+        if after:
+            self.arrived = tie(self.arrived, *after)
+        half = self.kept[0].shape[0] // 2
+        self.sent = [
+            add_low(kept[half:], arrived[half:]) for kept, arrived in zip(self.kept, self.arrived)
+        ]
+        self.kept = [
+            add_low(kept[:half], arrived[:half]) for kept, arrived in zip(self.kept, self.arrived)
+        ]
+        self.arrived = [
+            exchange(sent, order[self.at]) for sent, order in zip(self.sent, self.orders)
+        ]
+        self.at += 1
+
+    def done(self):
+        return self.at == len(self.orders[0])
+
+    def finish(self):
+        return jnp.concatenate(
+            [
+                kept[0].astype(jnp.float32) + arrived[0].astype(jnp.float32)
+                for kept, arrived in zip(self.kept, self.arrived)
+            ],
+            axis=1,
+        )
+
+    def marks(self):
+        return (self.kept, self.sent)
 
 
 def scatter_masks(order):
-    return order_masks(tuple(reversed(order)))
+    return order_masks(order)
 
 
 def assemble_kernel(plan, place_ref, *refs):
-    sources, targets, sem = (refs[: plan["sources"]], refs[plan["sources"] : -1], refs[-1])
+    count = plan["sources"]
+    sources, targets, (held, in_sems, out_sems) = (refs[:count], refs[count:-3], refs[-3:])
     me_fsdp, me_tp = (place_ref[0], place_ref[1])
     rows = plan["rows"]
-    copies = []
-    for source, place, start, width, high, low, target, per_tp, column in plan["copies"]:
+    arriving, leaving = ([], [])
+    for at, entry in enumerate(plan["copies"]):
+        source, place, start, width, high, low, target, per_tp, column = entry
         row = pl.multiple_of((me_fsdp ^ high) * rows, rows)
         lane = pl.multiple_of((me_tp ^ low) * per_tp + column, 128)
-        full = (target, pl.ds(row, rows), pl.ds(lane, width))
-        piece = (source, place, slice(None), pl.ds(start, width))
+        between = held.at[plan["slots"][at], :, pl.ds(start, width)]
         if plan["gather"]:
-            from_ref = sources[piece[0]].at[piece[1], :, piece[3]]
-            to_ref = targets[full[0]].at[full[1], full[2]]
+            from_ref = sources[source].at[place, :, pl.ds(start, width)]
+            to_ref = targets[target].at[pl.ds(row, rows), pl.ds(lane, width)]
         else:
-            from_ref = sources[full[0]].at[full[1], full[2]]
-            to_ref = targets[piece[0]].at[piece[1], :, piece[3]]
-        copy = pltpu.make_async_copy(from_ref, to_ref, sem)
+            from_ref = sources[target].at[pl.ds(row, rows), pl.ds(lane, width)]
+            to_ref = targets[source].at[place, :, pl.ds(start, width)]
+        copy = pltpu.make_async_copy(from_ref, between, in_sems.at[at])
         copy.start()
-        copies.append(copy)
-    for copy in copies:
-        copy.wait()
+        arriving.append(copy)
+        leaving.append(pltpu.make_async_copy(between, to_ref, out_sems.at[at]))
+    for first, second in zip(arriving, leaving):
+        first.wait()
+        second.start()
+    for second in leaving:
+        second.wait()
 
 
 def run_assemble(plan, place, sources, out_shapes, name):
     any_spec = pl.BlockSpec(memory_space=pl.ANY)
     moved = sum(math.prod(out.shape) * 2 for out in out_shapes)
+    copies = len(plan["copies"])
+    slots = {}
+    plan["slots"] = [slots.setdefault(entry[:2], len(slots)) for entry in plan["copies"]]
     return pl.pallas_call(
         partial(assemble_kernel, plan),
         in_specs=[pl.BlockSpec(memory_space=pltpu.SMEM)] + [any_spec] * len(sources),
         out_specs=[any_spec] * len(out_shapes),
         out_shape=out_shapes,
-        scratch_shapes=[pltpu.SemaphoreType.DMA],
+        scratch_shapes=[
+            pltpu.VMEM((len(slots), plan["rows"], plan["span"]), jnp.bfloat16),
+            pltpu.SemaphoreType.DMA((copies,)),
+            pltpu.SemaphoreType.DMA((copies,)),
+        ],
+        compiler_params=pltpu.CompilerParams(vmem_limit_bytes=24 << 20),
         cost_estimate=pl.CostEstimate(flops=0, bytes_accessed=2 * moved, transcendentals=0),
         name=name,
     )(place, *sources)
 
 
-def gather_group(shard, place, columns, widths, name):
-    core, orders = step_orders()
-    rows, width = shard.shape
-    part_width = width // 2
+def gather_group(chain, place, rows, columns, widths, name):
     sources, copies = ([], [])
-    for part, order in enumerate(orders):
-        pieces = gather_part(shard[:, part * part_width : (part + 1) * part_width], order, core)
-        for piece, masks in zip(pieces, gather_masks(order, core)):
+    for part, order in enumerate(chain.orders):
+        for piece, masks in zip(chain.pieces[part], gather_masks(order, chain.core)):
             for place_at, (high, low) in enumerate(masks):
-                for start, span_width, target, per_tp, column in columns[part]:
+                for entry in columns[part]:
+                    start, width, target, per_tp, column = entry
                     copies.append(
-                        (len(sources), place_at, start, span_width, high, low, target, per_tp, column)
+                        (len(sources), place_at, start, width, high, low, target, per_tp, column)
                     )
             sources.append(piece)
-    plan = dict(gather=True, sources=len(sources), rows=rows, copies=copies)
+    plan = dict(gather=True, sources=len(sources), rows=rows, copies=copies, span=chain.part_width)
     full_rows = rows * lax.axis_size("fsdp")
     shapes = [jax.ShapeDtypeStruct((full_rows, span), jnp.bfloat16) for span in widths]
     return run_assemble(plan, place, sources, shapes, name)
@@ -493,18 +565,13 @@
         masks = scatter_masks(order)
         for flip in (0, core[1]):
             for place_at, (high, low) in enumerate(masks):
-                for start, span_width, target, per_tp, column in columns[part]:
+                for start, width, target, per_tp, column in columns[part]:
                     copies.append(
-                        (len(shapes), place_at, start, span_width, high ^ flip, low, target, per_tp, column)
+                        (len(shapes), place_at, start, width, high ^ flip, low, target, per_tp, column)
                     )
             shapes.append(jax.ShapeDtypeStruct((len(masks), rows, part_width), jnp.bfloat16))
-    plan = dict(gather=False, sources=len(fulls), rows=rows, copies=copies)
-    pieces = run_assemble(plan, place, fulls, shapes, name)
-    parts = [
-        scatter_part(pieces[2 * part], pieces[2 * part + 1], order, core)
-        for part, order in enumerate(orders)
-    ]
-    return jnp.concatenate(parts, axis=1)
+    plan = dict(gather=False, sources=len(fulls), rows=rows, copies=copies, span=part_width)
+    return ScatterChain(run_assemble(plan, place, fulls, shapes, name))
 
 
 def bit_steps():
@@ -616,28 +683,37 @@
     out_ref[...] = jnp.where(lane < 64, held_ref[0], held_ref[1]).astype(jnp.bfloat16)
 
 
-def attend(queries, keys, values, seg):
+def attend(queries, keys, values, seg, first, count, earlier=None):
     length, width = queries.shape
-    heads = width // HEAD_DIM
-    pair = pl.BlockSpec((length, 128), lambda step: (0, step))
-    padded = pl.BlockSpec((2, length, 128), lambda step: (step, 0, 0))
+    pair = pl.BlockSpec((length, 128), lambda step: (0, first + step))
+    padded = pl.BlockSpec((2, length, 128), lambda step: (first + step, 0, 0))
+    passed = 0 if earlier is None else 3
+    operands = (seg, queries, keys, values) + (earlier or ())
+
+    def kernel(seg_ref, q_ref, k_ref, v_ref, *refs):
+        attend_kernel(seg_ref, q_ref, k_ref, v_ref, *refs[passed:])
+
     return pl.pallas_call(
-        attend_kernel,
-        grid=(heads // 2,),
-        in_specs=[pl.BlockSpec((length, 1), lambda step: (0, 0)), pair, pair, pair],
+        kernel,
+        grid=(count,),
+        in_specs=[pl.BlockSpec((length, 1), lambda step: (0, 0)), pair, pair, pair]
+        + [pl.BlockSpec(memory_space=pl.ANY)] * passed,
         out_specs=[pair, padded, padded],
         out_shape=[
             jax.ShapeDtypeStruct((length, width), jnp.bfloat16),
-            jax.ShapeDtypeStruct((heads, length, 128), jnp.bfloat16),
-            jax.ShapeDtypeStruct((heads, length, 128), jnp.bfloat16),
+            jax.ShapeDtypeStruct((width // HEAD_DIM, length, 128), jnp.bfloat16),
+            jax.ShapeDtypeStruct((width // HEAD_DIM, length, 128), jnp.bfloat16),
         ],
         scratch_shapes=[pltpu.VMEM((2, length, 128), jnp.float32)],
+        input_output_aliases={4 + at: at for at in range(passed)},
         compiler_params=pltpu.CompilerParams(vmem_limit_bytes=40 << 20),
         cost_estimate=pl.CostEstimate(
-            flops=28 * 10**9, bytes_accessed=16 << 20, transcendentals=heads * length * length
+            flops=3_500_000_000 * count,
+            bytes_accessed=(2 << 20) * count,
+            transcendentals=2 * count * length * length,
         ),
         name="attend",
-    )(seg, queries, keys, values)
+    )(*operands)
 
 
 def attend_back_kernel(qx_ref, kx_ref, v_ref, out_ref, grad_ref, dq_ref, dk_ref, dv_ref, held_ref):
@@ -697,24 +773,34 @@
     dq_ref[...] = (held_ref[...] * (1.0 / math.sqrt(HEAD_DIM))).T.astype(jnp.bfloat16)
 
 
-def attend_back(q_padded, k_padded, values, mixed, grad_mixed):
+def attend_back(q_padded, k_padded, values, mixed, grad_mixed, first, count, out_first, earlier=None):
     length, width = values.shape
-    heads = width // HEAD_DIM
-    pair = pl.BlockSpec((length, 128), lambda step: (0, step))
-    padded = pl.BlockSpec((2, length, 128), lambda step: (step, 0, 0))
+    pair = pl.BlockSpec((length, 128), lambda step: (0, first + step))
+    out_pair = pl.BlockSpec((length, 128), lambda step: (0, first - out_first + step))
+    padded = pl.BlockSpec((2, length, 128), lambda step: (first + step, 0, 0))
+    passed = 0 if earlier is None else 3
+    operands = (q_padded, k_padded, values, mixed, grad_mixed) + tuple(earlier or ())
+
+    def kernel(qx_ref, kx_ref, v_ref, out_ref, grad_ref, *refs):
+        attend_back_kernel(qx_ref, kx_ref, v_ref, out_ref, grad_ref, *refs[passed:])
+
     return pl.pallas_call(
-        attend_back_kernel,
-        grid=(heads // 2,),
-        in_specs=[padded, padded, pair, pair, pair],
-        out_specs=[pair, pair, pair],
-        out_shape=[jax.ShapeDtypeStruct((length, width), jnp.bfloat16)] * 3,
+        kernel,
+        grid=(count,),
+        in_specs=[padded, padded, pair, pair, pair]
+        + [pl.BlockSpec(memory_space=pl.ANY)] * passed,
+        out_specs=[out_pair, out_pair, out_pair],
+        out_shape=[jax.ShapeDtypeStruct((length, width // 2), jnp.bfloat16)] * 3,
         scratch_shapes=[pltpu.VMEM((128, length), jnp.float32)],
+        input_output_aliases={5 + at: at for at in range(passed)},
         compiler_params=pltpu.CompilerParams(vmem_limit_bytes=40 << 20),
         cost_estimate=pl.CostEstimate(
-            flops=40 * 10**9, bytes_accessed=20 << 20, transcendentals=heads * length * length
+            flops=5_000_000_000 * count,
+            bytes_accessed=(2 << 20) * count,
+            transcendentals=2 * count * length * length,
         ),
         name="attend_back",
-    )(q_padded, k_padded, values, mixed, grad_mixed)
+    )(*operands)
 
 
 def up_kernel(x_ref, w_ref, b_ref, active_ref, slope_ref):
@@ -814,21 +900,38 @@
     row_low = swap_in(inputs, tp_rank)
     seg = lax.dynamic_index_in_dim(segment_ids, tp_rank, 0, keepdims=False)[:, None]
 
-    half = local_width
-    attend_shard = jnp.concatenate([w_query, w_key, w_value, w_out.T], axis=1)
-    attend_columns = [
-        [(0, half, 0, half, 0), (half, half, 0, half, width)],
-        [(0, half, 0, half, 2 * width), (half, half, 1, half, 0)],
+    quarter = local_width // 2
+    part_width = local_hidden // 2
+    qkv_spans = [(at // 2 * width + at % 2 * local_width) for at in range(6)]
+    qkv_columns = [
+        [(at * quarter, quarter, 0, quarter, qkv_spans[3 * part + at]) for at in range(3)]
+        for part in range(2)
     ]
-    full_qkv, full_out = gather_group(
-        attend_shard, place, attend_columns, [3 * width, width], "gather_attend"
-    )
-    part_width = local_hidden // 2
+    up_cut = (local_hidden + local_width) // 2
+    up_rest = local_hidden - up_cut
+    up_columns = [
+        [(0, up_cut, 0, local_hidden, 0)],
+        [
+            (0, up_rest, 0, local_hidden, up_cut),
+            (up_rest, quarter, 1, quarter, 0),
+            (up_rest + quarter, quarter, 1, quarter, local_width),
+        ],
+    ]
     wide_columns = [
         [(0, part_width, 0, local_hidden, part * part_width)] for part in range(2)
     ]
-    (full_up,) = gather_group(w_up, place, wide_columns, [hidden_units], "gather_up")
-    (full_down,) = gather_group(w_down.T, place, wide_columns, [hidden_units], "gather_down")
+    chain_qkv = GatherChain(jnp.concatenate([w_query, w_key, w_value], axis=1))
+    chain_up = GatherChain(jnp.concatenate([w_up, w_out.T], axis=1))
+    chain_down = GatherChain(w_down.T)
+    chain_qkv.advance()
+    chain_qkv.advance()
+    chain_qkv.advance()
+    chain_up.advance(chain_qkv.marks())
+    chain_qkv.advance()
+    chain_up.advance(chain_qkv.marks())
+    chain_qkv.finish()
+    chain_up.advance(chain_qkv.pieces)
+    chain_down.advance(chain_qkv.pieces)
 
     valid_row = swap_in(valid_mask[..., None], tp_rank).astype(jnp.float32)
     small = jnp.concatenate(
@@ -850,7 +953,11 @@
     for count in (b_query.size, b_value.size, b_up.size, ln_gains.size, ln_shifts.size, 1):
         cuts.append(small_all[:, at : at + count])
         at += count
-    bias_query, bias_value, bias_up = (cuts[0].reshape(-1), cuts[1].reshape(-1), cuts[2].reshape(-1))
+    def head_order(columns):
+        return columns.reshape(tp_count, 2, quarter).transpose(1, 0, 2).reshape(width)
+
+    bias_query, bias_value = (head_order(cuts[0]), head_order(cuts[1]))
+    bias_up = cuts[2].reshape(-1)
 
     def feature_rows(columns, rows):
         return (
@@ -866,16 +973,42 @@
     teacher_row = swap_in(teacher, tp_rank).astype(jnp.float32)
 
     scale = LOG2E / math.sqrt(HEAD_DIM)
+    (full_qkv,) = gather_group(
+        chain_qkv, tie(place, chain_up.marks(), chain_down.marks()), shard_rows, qkv_columns, [3 * width], "gather_qkv"
+    )
     queries = (
         (dot_plain(row_low, full_qkv[:, :width]) + bias_query) * scale
     ).astype(jnp.bfloat16)
     keys = dot_plain(row_low, full_qkv[:, width : 2 * width]).astype(jnp.bfloat16)
     values = (dot_plain(row_low, full_qkv[:, 2 * width :]) + bias_value).astype(jnp.bfloat16)
-    mixed, q_padded, k_padded = attend(queries, keys, values, seg)
+    pairs = width // 128
+    chain_up.advance(queries, keys, values)
+    chain_down.advance(queries, keys, values)
+    queries = tie(queries, chain_up.marks(), chain_down.marks())
+    attended = attend(queries, keys, values, seg, 0, pairs // 4)
+    chain_down.advance(attended)
+    attended = attend(
+        queries, keys, tie(values, chain_down.marks()), seg, pairs // 4, pairs // 4, attended
+    )
+    chain_up.finish(attended)
+    attended = attend(
+        queries, keys, tie(values, chain_up.pieces), seg, pairs // 2, pairs // 4, attended
+    )
+    chain_down.advance(attended)
+    mixed, q_padded, k_padded = attend(
+        queries, keys, tie(values, chain_down.marks()), seg, 3 * pairs // 4, pairs // 4, attended
+    )
+    full_up, full_out = gather_group(
+        chain_up, tie(place, mixed), shard_rows, up_columns, [hidden_units, width], "gather_up"
+    )
     pre_first = row_low.astype(jnp.float32) + dot_last(mixed, full_out) + shifts[2]
     normed_first, unit_first, inverse_first = layer_norm_parts(pre_first, gains[0], shifts[0])
     hidden_low = normed_first.astype(jnp.bfloat16)
-    active, slope = up_project(hidden_low, full_up, bias_up[None])
+    chain_down.finish(hidden_low)
+    active, slope = up_project(tie(hidden_low, chain_down.pieces), full_up, bias_up[None])
+    (full_down,) = gather_group(
+        chain_down, tie(place, active), shard_rows, wide_columns, [hidden_units], "gather_down"
+    )
     pre_second = normed_first + dot_last(active, full_down) + shifts[3]
     result, unit_second, inverse_second = layer_norm_parts(pre_second, gains[1], shifts[1])
     hidden_out = swap_out(result.astype(jnp.bfloat16), tp_rank, piece_len)
@@ -886,21 +1019,80 @@
     grad_second = norm_backward(unit_second, inverse_second, gains[1], grad_result)
     grad_down = grad_second.astype(jnp.bfloat16)
     weight_down = dot_first(grad_down, active).astype(jnp.bfloat16)
-    grad_w_down = scatter_group(
+    sum_down = scatter_group(
         [weight_down], place, wide_columns, shard_rows, part_width, "scatter_down"
-    ).T
+    )
+    grad_down = tie(grad_down, sum_down.marks())
     grad_up = (dot_plain(grad_down, full_down) * slope.astype(jnp.float32)).astype(jnp.bfloat16)
     grad_b_up = jnp.sum(grad_up.astype(jnp.float32), axis=0)
+    sum_down.advance(grad_up)
+    grad_up = tie(grad_up, sum_down.marks())
     weight_up = dot_first(hidden_low, grad_up).astype(jnp.bfloat16)
-    grad_w_up = scatter_group(
+    sum_up = scatter_group(
         [weight_up], place, wide_columns, shard_rows, part_width, "scatter_up"
     )
+    sum_down.advance(weight_up)
+    grad_up = tie(grad_up, sum_up.marks(), sum_down.marks())
     grad_hidden = grad_second + dot_last(grad_up, full_up)
     grad_first = norm_backward(unit_first, inverse_first, gains[0], grad_hidden)
     grad_attend = grad_first.astype(jnp.bfloat16)
+    sum_up.advance(grad_attend)
+    sum_down.advance(grad_attend)
+    grad_attend = tie(grad_attend, sum_up.marks(), sum_down.marks())
     weight_out = dot_first(grad_attend, mixed).astype(jnp.bfloat16)
     grad_mixed = dot_plain(grad_attend, full_out).astype(jnp.bfloat16)
-    grad_query, grad_key, grad_value = attend_back(q_padded, k_padded, values, mixed, grad_mixed)
+    back = partial(attend_back, q_padded, k_padded, values, mixed)
+    sum_down.advance(grad_mixed)
+    first_grads = back(tie(grad_mixed, sum_down.marks()), 0, pairs // 4, 0)
+    sum_up.advance(first_grads)
+    first_grads = back(
+        tie(grad_mixed, sum_up.marks()), pairs // 4, pairs // 4, 0, first_grads
+    )
+    sum_up.advance(first_grads)
+    weight_first = [
+        dot_first(tie(row_low, sum_up.marks()), part).astype(jnp.bfloat16) for part in first_grads
+    ]
+    first_columns = [
+        [
+            (0, quarter, 0, quarter, 0),
+            (quarter, quarter, 0, quarter, local_width),
+            (2 * quarter, quarter // 2, 1, quarter, 0),
+        ],
+        [
+            (0, quarter // 2, 1, quarter, quarter // 2),
+            (quarter // 2, quarter, 2, quarter, 0),
+            (quarter // 2 + quarter, quarter, 3, quarter, 0),
+        ],
+    ]
+    sum_first = scatter_group(
+        [weight_out] + weight_first, place, first_columns, shard_rows, 5 * quarter // 2, "scatter_first"
+    )
+    second_grads = back(tie(grad_mixed, sum_first.marks()), pairs // 2, pairs // 4, pairs // 2)
+    sum_up.advance(second_grads)
+    sum_first.advance(second_grads)
+    second_grads = back(
+        tie(grad_mixed, sum_up.marks(), sum_first.marks()),
+        3 * pairs // 4,
+        pairs // 4,
+        pairs // 2,
+        second_grads,
+    )
+    sum_first.advance(second_grads)
+    second_grads = tie(second_grads, sum_first.marks())
+    weight_second = [dot_first(row_low, part).astype(jnp.bfloat16) for part in second_grads]
+    second_columns = [
+        [(0, quarter, 0, quarter, 0), (quarter, quarter // 2, 1, quarter, 0)],
+        [(0, quarter // 2, 1, quarter, quarter // 2), (quarter // 2, quarter, 2, quarter, 0)],
+    ]
+    sum_second = scatter_group(
+        weight_second, place, second_columns, shard_rows, 3 * quarter // 2, "scatter_second"
+    )
+    sum_first.advance(weight_second)
+    halves = [
+        jnp.concatenate(pair, axis=1) for pair in zip(first_grads, second_grads)
+    ]
+    halves = tie(halves, sum_second.marks(), sum_first.marks())
+    grad_query, grad_key, grad_value = halves
     grad_row = (
         grad_first
         + dot_last(grad_query, full_qkv[:, :width])
@@ -908,19 +1100,27 @@
         + dot_last(grad_value, full_qkv[:, 2 * width :])
     ).astype(jnp.bfloat16)
     grad_inputs = swap_out(grad_row, tp_rank, piece_len)
-    weight_qkv = [
-        dot_first(row_low, part).astype(jnp.bfloat16) for part in (grad_query, grad_key, grad_value)
+    sum_second.advance(grad_row)
+    sum_first.advance(grad_row)
+    for _ in range(3):
+        sum_second.advance()
+    grad_w_down = sum_down.finish().T
+    grad_w_up = sum_up.finish()
+    first_shard, second_shard = (sum_first.finish(), sum_second.finish())
+    grad_w_out = first_shard[:, : 2 * quarter]
+    grad_w_query, grad_w_key, grad_w_value = [
+        jnp.concatenate(
+            [
+                first_shard[:, (2 + at) * quarter : (3 + at) * quarter],
+                second_shard[:, at * quarter : (at + 1) * quarter],
+            ],
+            axis=1,
+        )
+        for at in range(3)
     ]
-    split_columns = [
-        [(0, half, 0, half, 0), (half, half, 1, half, 0)],
-        [(0, half, 2, half, 0), (half, half, 3, half, 0)],
-    ]
-    grad_attend_shard = scatter_group(
-        weight_qkv + [weight_out], place, split_columns, shard_rows, 2 * half, "scatter_attend"
-    )
-    grad_w_query, grad_w_key, grad_w_value, grad_w_out = [
-        grad_attend_shard[:, at * half : (at + 1) * half] for at in range(4)
-    ]
+
+    def device_order(columns):
+        return columns.reshape(2, tp_count, quarter).transpose(1, 0, 2).reshape(devices, -1)
 
     def feature_pieces(rows):
         pieces = rows.reshape(rows.shape[0], fsdp_count, -1).transpose(1, 0, 2).reshape(fsdp_count, -1)
@@ -929,8 +1129,8 @@
     devices = tp_count * fsdp_count
     pieces = jnp.concatenate(
         [
-            jnp.sum(grad_query.astype(jnp.float32), axis=0).reshape(devices, -1),
-            jnp.sum(grad_value.astype(jnp.float32), axis=0).reshape(devices, -1),
+            device_order(jnp.sum(grad_query.astype(jnp.float32), axis=0)),
+            device_order(jnp.sum(grad_value.astype(jnp.float32), axis=0)),
             grad_b_up.reshape(devices, -1),
             feature_pieces(
                 jnp.stack(

time: 2330 us -> 645 us (0.28)
  Pallas kernels: 1620 us -> 149 us
  waiting for transfers between devices: 395 us -> 142 us
  other arithmetic: 62.8 us -> 98.5 us
    pallas_call x6 -> x7, Pallas kernels: 1540 us -> 55.5 us  [run_assemble(): pl.pallas_call(partial(assemble_kernel, plan), in_specs=[pl.BlockSpec(mem...]
    ppermute x81 -> x91, waiting for transfers between devices: 395 us -> 142 us  [exchange(): lax.ppermute(values, axis, [(index, index ^ bit) for index in range(count)])]
    ppermute x81 -> x91, starting transfers between devices: 78.3 us -> 91.4 us  [exchange(): lax.ppermute(values, axis, [(index, index ^ bit) for index in range(count)])]
    pallas_call x2 -> x8, Pallas kernels: 70.3 us -> 75.1 us  [the longest x4 45.3 us: attend_back(): pl.pallas_call(kernel, grid=(count,), in_specs=[padded, padded, pair, pai...]
  transfers between devices with their start and end apart: 81 -> 91, of which waited for: 27 -> 34; matrix products, arithmetic and copies ran while one was open for 4% -> 28% of each run, Pallas kernels for 46% -> 18%
where the time goes in v2:
time: 645 us; the launch traced here: 641 us
  Pallas kernels  149 us (23%)
  waiting for transfers between devices  142 us (22%)
  matrix products  105 us (16%)
  other arithmetic  98.5 us (15%)
  starting transfers between devices  91.4 us (14%)
  local copies, waits for them, and re-layouts  49.4 us (8%)
    ppermute x91, waiting for transfers between devices, exchange(): lax.ppermute(values, axis, [(index, index ^ bit) for index in range(count)])  142 us
    ppermute x91, starting transfers between devices, exchange(): lax.ppermute(values, axis, [(index, index ^ bit) for index in range(count)])  91.4 us
    pallas_call x7, Pallas kernels, run_assemble(): pl.pallas_call(partial(assemble_kernel, plan), in_specs=[pl.BlockSpec(mem...  55.5 us
    pallas_call x4, Pallas kernels, attend_back(): pl.pallas_call(kernel, grid=(count,), in_specs=[padded, padded, pair, pai...  45.3 us
    dot_general x6, matrix products, dot_last(): lax.dot_general(left_side, right_side, (((1,), (1,)), ((), ())), preferre...  43.1 us
    convert_element_type x32, other arithmetic, add_low(): (left_side.astype(jnp.float32) + right_side.astype(jnp.float32)).astype(j...  33.9 us
    dot_general x9, matrix products, dot_first(): lax.dot_general(left_side, right_side, (((0,), (0,)), ((), ())), preferre...  31.6 us
    dot_general x5, matrix products, dot_plain(): lax.dot_general(left_side, right_side, (((1,), (0,)), ((), ())), preferre...  30.2 us
  transfers between devices with their start and end apart: 91, of which 34 were waited for; matrix products, arithmetic and copies ran while one was open for 28% of the time, Pallas kernels for 18%

profile of v2, /device:TPU:0, one launch (start us, length us, event | category | flops | bytes accessed | tf_op | source)
XLA Modules:
  0.0 640.7 jit_solution(17643640723254774614)
XLA Ops:
  34.5 11.5 %collective-permute-done.4 = bf16[2,64,768]{2,1,0:T(8,128)(2,1)S(1)} collective-permute-done((bf16[2,64,768]{2,1,0:T(8,128)(2,1)S(1)}, bf16[2,64,768]{2,1,0:T(8,128)(2,1)S(1)}, u32[]{:S(2)}, u32[]{:S(2)}) %collective-permute-start.4) | collective-permute-done | bytes 196640 | tf_op jit(solution)/shard_map/ppermute | solution.py:376
  67.4 19.1 %collective-permute-done.9 = bf16[2,64,1280]{2,1,0:T(8,128)(2,1)} collective-permute-done((bf16[2,64,1280]{2,1,0:T(8,128)(2,1)S(1)}, bf16[2,64,1280]{2,1,0:T(8,128)(2,1)}, u32[]{:S(2)}, u32[]{:S(2)}) %collective-permute-start.9) | collective-permute-done | bytes 327712 | tf_op jit(solution)/shard_map/ppermute | solution.py:376
  137.0 7.5 %attend.4 = (bf16[1024,1024]{1,0:T(8,128)(2,1)S(1)}, bf16[16,1024,128]{2,1,0:T(8,128)(2,1)S(1)}, bf16[16,1024,128]{2,1,0:T(8,128)(2,1)}) custom-call(s32[1024,1]{1,0:T(8,128)S(1)} %copy.57.seg_ref, bf16[1024,1024]{1,0:T(8,128)(2,1)S(1)} %copy-done.23, bf16[1024,1024]{1,0:T(8,128)(2,1)S(1)} %copy-done.25, bf16[1024,1024]{1,0:T(8,128)(2,1)S(1)} %copy-done.19), custom_call_target="tpu_custom_call" | custom-call | flops 7000000000 | bytes 4194304 | tf_op jit(solution)/shard_map/attend/pallas_call | solution.py:696
  144.5 7.4 %attend.5 = (bf16[1024,1024]{1,0:T(8,128)(2,1)S(1)}, bf16[16,1024,128]{2,1,0:T(8,128)(2,1)S(1)}, bf16[16,1024,128]{2,1,0:T(8,128)(2,1)}) custom-call(s32[1024,1]{1,0:T(8,128)S(1)} %copy.57.seg_ref, bf16[1024,1024]{1,0:T(8,128)(2,1)S(1)} %copy-done.23, bf16[1024,1024]{1,0:T(8,128)(2,1)S(1)} %copy-done.25, ...), custom_call_target="tpu_custom_call", output_to_operand_aliasing={{0}: (4, {}), {1}: (5, {}), {2}: (6, {})} | custom-call | flops 7000000000 | bytes 4194304 | tf_op jit(solution)/shard_map/attend/pallas_call | solution.py:696
  155.2 8.6 %collective-permute-done.30.refs_1_ = bf16[8,64,1280]{2,1,0:T(8,128)(2,1)} collective-permute-done((bf16[8,64,1280]{2,1,0:T(8,128)(2,1)S(1)}, bf16[8,64,1280]{2,1,0:T(8,128)(2,1)}, u32[]{:S(2)}, u32[]{:S(2)}) %collective-permute-start.30) | collective-permute-done | bytes 1310752 | tf_op jit(solution)/shard_map/ppermute | solution.py:376
  166.1 12.3 %collective-permute-done.28 = bf16[4,64,1024]{2,1,0:T(8,128)(2,1)S(1)} collective-permute-done((bf16[4,64,1024]{2,1,0:T(8,128)(2,1)S(1)}, bf16[4,64,1024]{2,1,0:T(8,128)(2,1)S(1)}, u32[]{:S(2)}, u32[]{:S(2)}) %collective-permute-start.28) | collective-permute-done | bytes 524320 | tf_op jit(solution)/shard_map/ppermute | solution.py:376
  184.1 7.6 %collective-permute-done.29 = bf16[4,64,1024]{2,1,0:T(8,128)(2,1)} collective-permute-done((bf16[4,64,1024]{2,1,0:T(8,128)(2,1)}, bf16[4,64,1024]{2,1,0:T(8,128)(2,1)}, u32[]{:S(2)}, u32[]{:S(2)}) %collective-permute-start.29) | collective-permute-done | bytes 524320 | tf_op jit(solution)/shard_map/ppermute | solution.py:376
  201.5 7.4 %attend.6 = (bf16[1024,1024]{1,0:T(8,128)(2,1)S(1)}, bf16[16,1024,128]{2,1,0:T(8,128)(2,1)S(1)}, bf16[16,1024,128]{2,1,0:T(8,128)(2,1)}) custom-call(s32[1024,1]{1,0:T(8,128)S(1)} %copy.57.seg_ref, bf16[1024,1024]{1,0:T(8,128)(2,1)S(1)} %copy-done.24, bf16[1024,1024]{1,0:T(8,128)(2,1)S(1)} %copy-done.26, ...), custom_call_target="tpu_custom_call", output_to_operand_aliasing={{0}: (4, {}), {1}: (5, {}), {2}: (6, {})} | custom-call | flops 7000000000 | bytes 4194304 | tf_op jit(solution)/shard_map/attend/pallas_call | solution.py:696
  210.7 7.6 %attend.7 = (bf16[1024,1024]{1,0:T(8,128)(2,1)S(1)}, bf16[16,1024,128]{2,1,0:T(8,128)(2,1)S(1)}, bf16[16,1024,128]{2,1,0:T(8,128)(2,1)}) custom-call(s32[1024,1]{1,0:T(8,128)S(1)} %copy.57.seg_ref, bf16[1024,1024]{1,0:T(8,128)(2,1)S(1)} %copy-done.24, bf16[1024,1024]{1,0:T(8,128)(2,1)S(1)} %copy-done.26, ...), custom_call_target="tpu_custom_call", output_to_operand_aliasing={{0}: (4, {}), {1}: (5, {}), {2}: (6, {})} | custom-call | flops 7000000000 | bytes 4194304 | tf_op jit(solution)/shard_map/attend/pallas_call | solution.py:696
  220.2 8.2 %gather_up.1 = (bf16[1024,4096]{1,0:T(8,128)(2,1)S(1)}, bf16[1024,1024]{1,0:T(8,128)(2,1)S(1)}) custom-call(s32[2]{0:T(128)S(1)} %pad_add_fusion.place_ref, bf16[8,64,1280]{2,1,0:T(8,128)(2,1)S(1)} %pad_maximum_fusion.7.refs_0_, bf16[8,64,1280]{2,1,0:T(8,128)(2,1)} %collective-permute-done.30.refs_1_, bf16[8,64,1280]{2,1,0:T(8,128)(2,1)} %collective-permute-done.32.refs_2_, ...), custom_call_target="tpu_custom_call" | custom-call | bytes 20971520 | tf_op jit(solution)/shard_map/gather_up/pallas_call | solution.py:528
  246.5 18.7 %up_project.1 = (bf16[1024,4096]{1,0:T(8,128)(2,1)S(1)}, bf16[1024,4096]{1,0:T(8,128)(2,1)}) custom-call(bf16[1024,1024]{1,0:T(8,128)(2,1)S(1)} %fusion.1.x_ref, bf16[1024,4096]{1,0:T(8,128)(2,1)} %copy-done.10, f32[1,4096]{1,0:T(1,128)S(1)} %bitcast.129), custom_call_target="tpu_custom_call" | custom-call | flops 8589934592 | bytes 27262976 | tf_op jit(solution)/shard_map/up_project/pallas_call | solution.py:830
  274.1 15.5 %fusion.30 = (f32[1024]{0:T(1024)S(1)}, f32[1024,1024]{1,0:T(8,128)S(1)}) fusion(f32[1024]{0:T(1024)S(1)} %add.393, bf16[1024,4096]{1,0:T(8,128)(2,1)} %copy-done.32, bf16[1024,4096]{1,0:T(8,128)(2,1)S(1)} %gather_down.1, f32[1024]{0:T(1024)S(1)} %add.389, f32[1024]{0:T(1024)S(1)} %mul.140, f32[1024]{0:T(1024)S(1)} %add_rsqrt_fusion.1, ...), kind=kOutput, calls=%fused_computation.245 | convolution fusion | flops 8597273600 | bytes 25190400 | tf_op jit(solution)/shard_map/dot_general | solution.py:43
  304.1 9.8 %convolution_convert_fusion.1.refs_0_ = bf16[1024,4096]{1,0:T(8,128)(2,1)S(1)} fusion(bf16[1024,1024]{1,0:T(8,128)(2,1)S(1)} %convert_element_type.753, bf16[1024,4096]{1,0:T(8,128)(2,1)S(1)} %bitcast.133), kind=kOutput, calls=%fused_computation.3 | convolution fusion | flops 8594128896 | bytes 18874368 | tf_op jit(solution)/shard_map/dot_general | solution.py:37
  313.9 11.4 %scatter_down.1 = (bf16[16,64,1024]{2,1,0:T(8,128)(2,1)S(1)}, bf16[16,64,1024]{2,1,0:T(8,128)(2,1)}, bf16[16,64,1024]{2,1,0:T(8,128)(2,1)S(1)}, bf16[16,64,1024]{2,1,0:T(8,128)(2,1)}) custom-call(s32[2]{0:T(128)S(1)} %pad_add_fusion.place_ref, bf16[1024,4096]{1,0:T(8,128)(2,1)S(1)} %convolution_convert_fusion.1.refs_0_), custom_call_target="tpu_custom_call" | custom-call | bytes 16777216 | tf_op jit(solution)/shard_map/scatter_down/pallas_call | solution.py:528
  331.4 16.8 %convert_reduce_fusion = (f32[4096]{0:T(1024)}, bf16[1024,4096]{1,0:T(8,128)(2,1)}) fusion(bf16[1024,4096]{1,0:T(8,128)(2,1)} %get-tuple-element.175, bf16[1024,1024]{1,0:T(8,128)(2,1)} %copy-done.57, bf16[1024,4096]{1,0:T(8,128)(2,1)} %copy-done.2), kind=kOutput, calls=%fused_computation | convolution fusion | flops 8610902016 | bytes 27279360 | tf_op jit(solution)/shard_map/dot_general | solution.py:368
  357.8 11.6 %convolution_convert_fusion.refs_0_ = bf16[1024,4096]{1,0:T(8,128)(2,1)S(1)} fusion(bf16[1024,1024]{1,0:T(8,128)(2,1)S(1)} %fusion.1.x_ref, bf16[1024,4096]{1,0:T(8,128)(2,1)} %get-tuple-element.185), kind=kOutput, calls=%fused_computation.2 | convolution fusion | flops 8594128896 | bytes 18874368 | tf_op jit(solution)/shard_map/dot_general | solution.py:37
  369.5 11.3 %scatter_up.1 = (bf16[16,64,1024]{2,1,0:T(8,128)(2,1)S(1)}, bf16[16,64,1024]{2,1,0:T(8,128)(2,1)}, bf16[16,64,1024]{2,1,0:T(8,128)(2,1)S(1)}, bf16[16,64,1024]{2,1,0:T(8,128)(2,1)}) custom-call(s32[2]{0:T(128)S(1)} %pad_add_fusion.place_ref, bf16[1024,4096]{1,0:T(8,128)(2,1)S(1)} %convolution_convert_fusion.refs_0_), custom_call_target="tpu_custom_call" | custom-call | bytes 16777216 | tf_op jit(solution)/shard_map/scatter_up/pallas_call | solution.py:528
  388.8 15.3 %multiply_reduce_fusion.1 = (f32[1024]{0:T(1024)S(1)}, f32[1024]{0:T(1024)S(1)}, f32[1024]{0:T(1024)S(1)}, f32[1024]{0:T(1024)S(1)}, f32[1024,1024]{1,0:T(8,128)}) fusion(f32[1024,1024]{1,0:T(8,128)} %copy-done.33, f32[1024]{0:T(1024)S(1)} %add_rsqrt_fusion.1, f32[1024]{0:T(1024)S(1)} %broadcast_multiply_fusion.5, f32[1024]{0:T(1024)S(1)} %mul.140, ...), kind=kOutput, calls=%fused_computation.9 | convolution fusion | flops 8600416256 | bytes 29388800 | tf_op jit(solution)/shard_map/dot_general | solution.py:43
  432.6 17.2 %collective-permute-done.89 = bf16[1,64,1024]{2,1,0:T(8,128)(2,1)S(1)} collective-permute-done((bf16[1,64,1024]{2,1,0:T(8,128)(2,1)S(1)}, bf16[1,64,1024]{2,1,0:T(8,128)(2,1)S(1)}, u32[]{:S(2)}, u32[]{:S(2)}) %collective-permute-start.89) | collective-permute-done | bytes 131104 | tf_op jit(solution)/shard_map/ppermute | solution.py:376
  452.1 11.4 %attend_back.4 = (bf16[1024,512]{1,0:T(8,128)(2,1)S(1)}, bf16[1024,512]{1,0:T(8,128)(2,1)S(1)}, bf16[1024,512]{1,0:T(8,128)(2,1)S(1)}) custom-call(bf16[16,1024,128]{2,1,0:T(8,128)(2,1)S(1)} %copy-done.16, bf16[16,1024,128]{2,1,0:T(8,128)(2,1)} %get-tuple-element.169.kx_ref, bf16[1024,1024]{1,0:T(8,128)(2,1)S(1)} %copy-done.21, ...), custom_call_target="tpu_custom_call" | custom-call | flops 10000000000 | bytes 4194304 | tf_op jit(solution)/shard_map/attend_back/pallas_call | solution.py:787
  466.6 11.2 %attend_back.5 = (bf16[1024,512]{1,0:T(8,128)(2,1)S(1)}, bf16[1024,512]{1,0:T(8,128)(2,1)S(1)}, bf16[1024,512]{1,0:T(8,128)(2,1)S(1)}) custom-call(bf16[16,1024,128]{2,1,0:T(8,128)(2,1)S(1)} %copy-done.16, bf16[16,1024,128]{2,1,0:T(8,128)(2,1)} %get-tuple-element.169.kx_ref, ...), custom_call_target="tpu_custom_call", output_to_operand_aliasing={{0}: (5, {}), {1}: (6, {}), {2}: (7, {})} | custom-call | flops 10000000000 | bytes 4194304 | tf_op jit(solution)/shard_map/attend_back/pallas_call | solution.py:787
  496.2 11.4 %attend_back.6 = (bf16[1024,512]{1,0:T(8,128)(2,1)S(1)}, bf16[1024,512]{1,0:T(8,128)(2,1)S(1)}, bf16[1024,512]{1,0:T(8,128)(2,1)S(1)}) custom-call(bf16[16,1024,128]{2,1,0:T(8,128)(2,1)S(1)} %copy-done.16, bf16[16,1024,128]{2,1,0:T(8,128)(2,1)} %get-tuple-element.169.kx_ref, bf16[1024,1024]{1,0:T(8,128)(2,1)S(1)} %copy-done.22, ...), custom_call_target="tpu_custom_call" | custom-call | flops 10000000000 | bytes 4194304 | tf_op jit(solution)/shard_map/attend_back/pallas_call | solution.py:787
  512.7 7.5 %collective-permute-done.87 = bf16[1,64,1024]{2,1,0:T(8,128)(2,1)S(1)} collective-permute-done((bf16[1,64,1024]{2,1,0:T(8,128)(2,1)S(1)}, bf16[1,64,1024]{2,1,0:T(8,128)(2,1)S(1)}, u32[]{:S(2)}, u32[]{:S(2)}) %collective-permute-start.87) | collective-permute-done | bytes 131104 | tf_op jit(solution)/shard_map/ppermute | solution.py:376
  526.1 11.2 %attend_back.7 = (bf16[1024,512]{1,0:T(8,128)(2,1)S(1)}, bf16[1024,512]{1,0:T(8,128)(2,1)S(1)}, bf16[1024,512]{1,0:T(8,128)(2,1)S(1)}) custom-call(bf16[16,1024,128]{2,1,0:T(8,128)(2,1)S(1)} %copy-done.16, bf16[16,1024,128]{2,1,0:T(8,128)(2,1)} %get-tuple-element.169.kx_ref, ...), custom_call_target="tpu_custom_call", output_to_operand_aliasing={{0}: (5, {}), {1}: (6, {}), {2}: (7, {})} | custom-call | flops 10000000000 | bytes 4194304 | tf_op jit(solution)/shard_map/attend_back/pallas_call | solution.py:787
  (539 shorter events, 357.7 us)
Async XLA Ops:
  15.6 75.9 %collective-permute-start = (bf16[512,1024]{1,0:T(8,128)(2,1)}, bf16[512,1024]{1,0:T(8,128)(2,1)}, u32[]{:S(2)}, u32[]{:S(2)}) collective-permute-start(bf16[512,1024]{1,0:T(8,128)(2,1)} %dynamic-slice_bitcast_fusion.1), channel_id=1, source_target_pairs={{0,1},{1,0},{2,3},{3,2},{4,5},{5,4},{6,7},{7,6},{8,9},{9,8},{10,11... | collective-permute-start | bytes 3145736 | tf_op jit(solution)/shard_map/ppermute | solution.py:376
  54.7 32.4 %collective-permute-start.11 = (bf16[8,64,768]{2,1,0:T(8,128)(2,1)S(1)}, bf16[8,64,768]{2,1,0:T(8,128)(2,1)S(1)}, u32[]{:S(2)}, u32[]{:S(2)}) collective-permute-start(bf16[8,64,768]{2,1,0:T(8,128)(2,1)S(1)} %pad_maximum_fusion.11.refs_0_), channel_id=1, source_target_pairs={{0,4},{2,6},{4,0},{6,2},{8,12},{10,14},{12,8},{14,10},{16,20},{18,... | collective-permute-start | bytes 2359304 | tf_op jit(solution)/shard_map/ppermute | solution.py:376
  56.3 30.8 %collective-permute-start.14 = (bf16[8,64,768]{2,1,0:T(8,128)(2,1)S(1)}, bf16[8,64,768]{2,1,0:T(8,128)(2,1)S(1)}, u32[]{:S(2)}, u32[]{:S(2)}) collective-permute-start(bf16[8,64,768]{2,1,0:T(8,128)(2,1)S(1)} %pad_maximum_fusion.12.refs_4_), channel_id=1, source_target_pairs={{0,8},{2,10},{4,12},{6,14},{8,0},{10,2},{12,4},{14,6},{16,24},{18,... | collective-permute-start | bytes 2359304 | tf_op jit(solution)/shard_map/ppermute | solution.py:376
  92.9 32.5 %collective-permute-start.22 = (bf16[4,64,1280]{2,1,0:T(8,128)(2,1)}, bf16[4,64,1280]{2,1,0:T(8,128)(2,1)}, u32[]{:S(2)}, u32[]{:S(2)}) collective-permute-start(bf16[4,64,1280]{2,1,0:T(8,128)(2,1)} %pad_maximum_fusion.13), channel_id=1, source_target_pairs={{0,1},{1,0},{2,3},{3,2},{4,5},{5,4},{6,7},{7,6},{8,9},{9,8},{10,11... | collective-permute-start | bytes 1966088 | tf_op jit(solution)/shard_map/ppermute | solution.py:376
  135.0 28.9 %collective-permute-start.30 = (bf16[8,64,1280]{2,1,0:T(8,128)(2,1)S(1)}, bf16[8,64,1280]{2,1,0:T(8,128)(2,1)}, u32[]{:S(2)}, u32[]{:S(2)}) collective-permute-start(bf16[8,64,1280]{2,1,0:T(8,128)(2,1)S(1)} %pad_maximum_fusion.7.refs_0_), channel_id=1, source_target_pairs={{0,4},{2,6},{4,0},{6,2},{8,12},{10,14},{12,8},{14,10},{16,20},{18,... | collective-permute-start | bytes 3932168 | tf_op jit(solution)/shard_map/ppermute | solution.py:376
  135.6 28.5 %collective-permute-start.31 = (bf16[8,64,1280]{2,1,0:T(8,128)(2,1)S(1)}, bf16[8,64,1280]{2,1,0:T(8,128)(2,1)}, u32[]{:S(2)}, u32[]{:S(2)}) collective-permute-start(bf16[8,64,1280]{2,1,0:T(8,128)(2,1)S(1)} %pad_maximum_fusion.8.refs_4_), channel_id=1, source_target_pairs={{0,8},{2,10},{4,12},{6,14},{8,0},{10,2},{12,4},{14,6},{16,24},{18,... | collective-permute-start | bytes 3932168 | tf_op jit(solution)/shard_map/ppermute | solution.py:376
  136.4 59.1 %collective-permute-start.32 = (bf16[8,64,1280]{2,1,0:T(8,128)(2,1)S(1)}, bf16[8,64,1280]{2,1,0:T(8,128)(2,1)}, u32[]{:S(2)}, u32[]{:S(2)}) collective-permute-start(bf16[8,64,1280]{2,1,0:T(8,128)(2,1)S(1)} %pad_maximum_fusion.7.refs_0_), channel_id=1, source_target_pairs={{0,2},{2,0},{4,6},{6,4},{8,10},{10,8},{12,14},{14,12},{16,18},{18,... | collective-permute-start | bytes 3932168 | tf_op jit(solution)/shard_map/ppermute | solution.py:376
  136.4 59.7 %collective-permute-start.34 = (bf16[8,64,1280]{2,1,0:T(8,128)(2,1)S(1)}, bf16[8,64,1280]{2,1,0:T(8,128)(2,1)}, u32[]{:S(2)}, u32[]{:S(2)}) collective-permute-start(bf16[8,64,1280]{2,1,0:T(8,128)(2,1)S(1)} %pad_maximum_fusion.8.refs_4_), channel_id=1, source_target_pairs={{0,2},{2,0},{4,6},{6,4},{8,10},{10,8},{12,14},{14,12},{16,18},{18,... | collective-permute-start | bytes 3932168 | tf_op jit(solution)/shard_map/ppermute | solution.py:376
  164.1 32.0 %collective-permute-start.33 = (bf16[8,64,1280]{2,1,0:T(8,128)(2,1)}, bf16[8,64,1280]{2,1,0:T(8,128)(2,1)}, u32[]{:S(2)}, u32[]{:S(2)}) collective-permute-start(bf16[8,64,1280]{2,1,0:T(8,128)(2,1)} %collective-permute-done.30.refs_1_), channel_id=1, source_target_pairs={{0,2},{2,0},{4,6},{6,4},{8,10},{10,8},{12,14},{14,12},{16,18},{18,... | collective-permute-start | bytes 3932168 | tf_op jit(solution)/shard_map/ppermute | solution.py:376
  164.1 32.0 %collective-permute-start.35 = (bf16[8,64,1280]{2,1,0:T(8,128)(2,1)}, bf16[8,64,1280]{2,1,0:T(8,128)(2,1)}, u32[]{:S(2)}, u32[]{:S(2)}) collective-permute-start(bf16[8,64,1280]{2,1,0:T(8,128)(2,1)} %collective-permute-done.31.refs_5_), channel_id=1, source_target_pairs={{0,2},{2,0},{4,6},{6,4},{8,10},{10,8},{12,14},{14,12},{16,18},{18,... | collective-permute-start | bytes 3932168 | tf_op jit(solution)/shard_map/ppermute | solution.py:376
  191.8 46.0 %collective-permute-start.43 = (s32[512,1]{0,1:T(1,128)S(1)}, s32[512,1]{0,1:T(1,128)S(1)}, u32[]{:S(2)}, u32[]{:S(2)}) collective-permute-start(s32[512,1]{0,1:T(1,128)S(1)} %fusion.22), channel_id=1, source_target_pairs={{0,1},{1,0},{2,3},{3,2},{4,5},{5,4},{6,7},{7,6},{8,9},{9,8},{10,11... | collective-permute-start | bytes 6152 | tf_op jit(solution)/shard_map/ppermute | solution.py:376
  195.6 48.2 %collective-permute-start.44 = (bf16[512,1024]{1,0:T(8,128)(2,1)}, bf16[512,1024]{1,0:T(8,128)(2,1)}, u32[]{:S(2)}, u32[]{:S(2)}) collective-permute-start(bf16[512,1024]{1,0:T(8,128)(2,1)} %dynamic-slice_bitcast_fusion), channel_id=1, source_target_pairs={{0,1},{1,0},{2,3},{3,2},{4,5},{5,4},{6,7},{7,6},{8,9},{9,8},{10,11... | collective-permute-start | bytes 3145736 | tf_op jit(solution)/shard_map/ppermute | solution.py:376
  210.7 35.8 %collective-permute-start.38 = (bf16[8,64,1024]{2,1,0:T(8,128)(2,1)}, bf16[8,64,1024]{2,1,0:T(8,128)(2,1)}, u32[]{:S(2)}, u32[]{:S(2)}) collective-permute-start(bf16[8,64,1024]{2,1,0:T(8,128)(2,1)} %pad_maximum_fusion.9.refs_0_), channel_id=1, source_target_pairs={{0,2},{2,0},{4,6},{6,4},{8,10},{10,8},{12,14},{14,12},{16,18},{18,... | collective-permute-start | bytes 3145736 | tf_op jit(solution)/shard_map/ppermute | solution.py:376
  329.7 294.3 %collective-permute-start.42 = (bf16[512,1024]{1,0:T(8,128)(2,1)}, bf16[512,1024]{1,0:T(8,128)(2,1)}, u32[]{:S(2)}, u32[]{:S(2)}) collective-permute-start(bf16[512,1024]{1,0:T(8,128)(2,1)} %constant_dynamic-slice_fusion.3), channel_id=1, source_target_pairs={{0,1},{1,0},{2,3},{3,2},{4,5},{5,4},{6,7},{7,6},{8,9},{9,8},{10,11... | collective-permute-start | bytes 3145736 | tf_op jit(solution)/shard_map/ppermute | solution.py:376
  380.8 36.2 %collective-permute-start.49 = (bf16[16,64,1024]{2,1,0:T(8,128)(2,1)}, bf16[16,64,1024]{2,1,0:T(8,128)(2,1)}, u32[]{:S(2)}, u32[]{:S(2)}) collective-permute-start(bf16[16,64,1024]{2,1,0:T(8,128)(2,1)} %get-tuple-element.181), channel_id=1, source_target_pairs={{0,2},{2,0},{4,6},{6,4},{8,10},{10,8},{12,14},{14,12},{16,18},{18,... | collective-permute-start | bytes 6291464 | tf_op jit(solution)/shard_map/ppermute | solution.py:376
  380.9 36.1 %collective-permute-start.50 = (bf16[16,64,1024]{2,1,0:T(8,128)(2,1)}, bf16[16,64,1024]{2,1,0:T(8,128)(2,1)}, u32[]{:S(2)}, u32[]{:S(2)}) collective-permute-start(bf16[16,64,1024]{2,1,0:T(8,128)(2,1)} %get-tuple-element.182), channel_id=1, source_target_pairs={{0,2},{2,0},{4,6},{6,4},{8,10},{10,8},{12,14},{14,12},{16,18},{18,... | collective-permute-start | bytes 6291464 | tf_op jit(solution)/shard_map/ppermute | solution.py:376
  422.9 40.6 %collective-permute-start.53 = (bf16[8,64,1024]{2,1,0:T(8,128)(2,1)S(1)}, bf16[8,64,1024]{2,1,0:T(8,128)(2,1)S(1)}, u32[]{:S(2)}, u32[]{:S(2)}) collective-permute-start(bf16[8,64,1024]{2,1,0:T(8,128)(2,1)S(1)} %get-tuple-element.272), channel_id=1, source_target_pairs={{0,4},{2,6},{4,0},{6,2},{8,12},{10,14},{12,8},{14,10},{16,20},{18,... | collective-permute-start | bytes 3145736 | tf_op jit(solution)/shard_map/ppermute | solution.py:376
  423.5 40.1 %collective-permute-start.54 = (bf16[8,64,1024]{2,1,0:T(8,128)(2,1)}, bf16[8,64,1024]{2,1,0:T(8,128)(2,1)S(1)}, u32[]{:S(2)}, u32[]{:S(2)}) collective-permute-start(bf16[8,64,1024]{2,1,0:T(8,128)(2,1)} %get-tuple-element.270), channel_id=1, source_target_pairs={{0,8},{2,10},{4,12},{6,14},{8,0},{10,2},{12,4},{14,6},{16,24},{18,... | collective-permute-start | bytes 3145736 | tf_op jit(solution)/shard_map/ppermute | solution.py:376
  478.7 29.0 %collective-permute-start.59 = (bf16[2,64,1024]{2,1,0:T(8,128)(2,1)}, bf16[2,64,1024]{2,1,0:T(8,128)(2,1)}, u32[]{:S(2)}, u32[]{:S(2)}) collective-permute-start(bf16[2,64,1024]{2,1,0:T(8,128)(2,1)} %get-tuple-element.308), channel_id=1, source_target_pairs={{0,8},{2,10},{4,12},{6,14},{8,0},{10,2},{12,4},{14,6},{16,24},{18,... | collective-permute-start | bytes 786440 | tf_op jit(solution)/shard_map/ppermute | solution.py:376
  495.6 29.0 %collective-permute-start.61 = (bf16[16,64,640]{2,1,0:T(8,128)(2,1)S(1)}, bf16[16,64,640]{2,1,0:T(8,128)(2,1)S(1)}, u32[]{:S(2)}, u32[]{:S(2)}) collective-permute-start(bf16[16,64,640]{2,1,0:T(8,128)(2,1)S(1)} %get-tuple-element.208), channel_id=1, source_target_pairs={{0,2},{2,0},{4,6},{6,4},{8,10},{10,8},{12,14},{14,12},{16,18},{18,... | collective-permute-start | bytes 3932168 | tf_op jit(solution)/shard_map/ppermute | solution.py:376
  495.7 29.0 %collective-permute-start.62 = (bf16[16,64,640]{2,1,0:T(8,128)(2,1)S(1)}, bf16[16,64,640]{2,1,0:T(8,128)(2,1)S(1)}, u32[]{:S(2)}, u32[]{:S(2)}) collective-permute-start(bf16[16,64,640]{2,1,0:T(8,128)(2,1)S(1)} %get-tuple-element.209), channel_id=1, source_target_pairs={{0,2},{2,0},{4,6},{6,4},{8,10},{10,8},{12,14},{14,12},{16,18},{18,... | collective-permute-start | bytes 3932168 | tf_op jit(solution)/shard_map/ppermute | solution.py:376
  567.8 37.5 %collective-permute-start.77 = (bf16[16,64,384]{2,1,0:T(8,128)(2,1)S(1)}, bf16[16,64,384]{2,1,0:T(8,128)(2,1)}, u32[]{:S(2)}, u32[]{:S(2)}) collective-permute-start(bf16[16,64,384]{2,1,0:T(8,128)(2,1)S(1)} %get-tuple-element.229), channel_id=1, source_target_pairs={{0,2},{2,0},{4,6},{6,4},{8,10},{10,8},{12,14},{14,12},{16,18},{18,... | collective-permute-start | bytes 2359304 | tf_op jit(solution)/shard_map/ppermute | solution.py:376
  567.8 37.5 %collective-permute-start.78 = (bf16[16,64,384]{2,1,0:T(8,128)(2,1)S(1)}, bf16[16,64,384]{2,1,0:T(8,128)(2,1)}, u32[]{:S(2)}, u32[]{:S(2)}) collective-permute-start(bf16[16,64,384]{2,1,0:T(8,128)(2,1)S(1)} %get-tuple-element.230), channel_id=1, source_target_pairs={{0,2},{2,0},{4,6},{6,4},{8,10},{10,8},{12,14},{14,12},{16,18},{18,... | collective-permute-start | bytes 2359304 | tf_op jit(solution)/shard_map/ppermute | solution.py:376
  590.9 33.0 %collective-permute-start.72 = (bf16[512,1024]{1,0:T(8,128)(2,1)}, bf16[512,1024]{1,0:T(8,128)(2,1)S(1)}, u32[]{:S(2)}, u32[]{:S(2)}) collective-permute-start(bf16[512,1024]{1,0:T(8,128)(2,1)} %constant_dynamic-slice_fusion), channel_id=1, source_target_pairs={{0,1},{1,0},{2,3},{3,2},{4,5},{5,4},{6,7},{7,6},{8,9},{9,8},{10,11... | collective-permute-start | bytes 3145736 | tf_op jit(solution)/shard_map/ppermute | solution.py:376
  (148 other events, 1839.3 us)

commit v3 on v0

--- a/solution.py
+++ b/solution.py
@@ -4,6 +4,8 @@
 import jax
 import jax.numpy as jnp
 from jax import lax
+from jax.experimental import pallas as pl
+from jax.experimental.pallas import tpu as pltpu
 from jax.sharding import PartitionSpec as P
 
 HEAD_DIM = 64
@@ -140,7 +142,7 @@
     return (jnp.stack(query_rows), jnp.stack(key_rows), jnp.stack(value_rows))
 
 
-def on_device(
+def on_device_heads(
     inputs,
     segment_ids,
     valid_mask,
@@ -352,6 +354,1403 @@
     )
 
 
+BLOCK = 256
+LOG2E = math.log2(math.e)
+SHARD_ROWS_PARTS = 2
+
+
+def rows_plan_fits(mesh):
+    fsdp_count, tp_count = (mesh.shape["fsdp"], mesh.shape["tp"])
+    return tp_count == 2 and fsdp_count >= 8 and fsdp_count & (fsdp_count - 1) == 0
+
+
+def dot_plain(left_side, right_side):
+    return lax.dot_general(
+        left_side, right_side, (((1,), (0,)), ((), ())), preferred_element_type=jnp.float32
+    )
+
+
+def exchange(values, move):
+    tp_count = lax.axis_size("tp")
+    count = lax.axis_size("fsdp") * tp_count
+    flip = move[0] * tp_count + move[1]
+    if move[1] == 0:
+        return lax.ppermute(
+            values, "fsdp", [(at, at ^ move[0]) for at in range(lax.axis_size("fsdp"))]
+        )
+    return lax.ppermute(values, ("fsdp", "tp"), [(at, at ^ flip) for at in range(count)])
+
+
+ACROSS = (0, 1)
+CORE = (1, 0)
+SIDE = (2, 0)
+
+
+def far_moves():
+    places = lax.axis_size("fsdp").bit_length() - 1
+    return [(1 << place, 0) for place in range(places - 1, 1, -1)]
+
+
+def gather_steps():
+    far = far_moves()
+    return (tuple(far) + (ACROSS, SIDE), (far[0], ACROSS, SIDE) + tuple(far[1:]))
+
+
+def scatter_steps(kind):
+    far = list(reversed(far_moves()))
+    if kind == "late":
+        return ((SIDE,), (ACROSS,), tuple(reversed(far)))
+    moves = {
+        "across": [ACROSS, SIDE] + far,
+        "far": far[:1] + [ACROSS, SIDE] + far[1:],
+        "far_side": far[:1] + [SIDE] + far[1:] + [ACROSS],
+    }[kind]
+    return tuple((move,) for move in moves)
+
+
+def moves_of(step):
+    found = [(0, 0)]
+    for high, low in reversed(step):
+        found = found + [(one ^ high, two ^ low) for one, two in found]
+    return found
+
+
+def step_masks(steps):
+    masks = [(0, 0)]
+    for step in steps:
+        masks = [
+            (high ^ one, low ^ two) for one, two in moves_of(step) for high, low in masks
+        ]
+    return masks
+
+
+def tie(values, *others):
+    return lax.optimization_barrier((values, others))[0]
+
+
+class GatherChain:
+
+    def __init__(self, parts):
+        self.steps = gather_steps()
+        self.held = [part[None] for part in parts]
+        self.arrived = None
+        self.at = 0
+
+    def advance(self, *after):
+        if self.arrived is not None:
+            self.held, self.arrived = tie((self.held, self.arrived), *after)
+            self.held = [
+                jnp.concatenate(pair, axis=0) for pair in zip(self.held, self.arrived)
+            ]
+        else:
+            self.held = tie(self.held, *after)
+        self.arrived = [
+            exchange(held, steps[self.at]) for held, steps in zip(self.held, self.steps)
+        ]
+        self.at += 1
+
+    def finish(self, *after):
+        if after:
+            self.arrived = tie(self.arrived, *after)
+        self.pieces = []
+        for held, arrived in zip(self.held, self.arrived):
+            near = [held, arrived]
+            self.pieces.append(near + [exchange(piece, CORE) for piece in near])
+
+    def marks(self):
+        return self.held
+
+    def sources(self):
+        return [piece for part in self.pieces for piece in part]
+
+    def places(self):
+        found = []
+        for part, steps in enumerate(self.steps):
+            masks = step_masks([(move,) for move in steps])
+            size = len(masks) // 2
+            for at in range(4):
+                for place, (high, low) in enumerate(masks[at % 2 * size : (at % 2 + 1) * size]):
+                    flip = CORE[0] if at >= 2 else 0
+                    found.append((part, part * 4 + at, place, high ^ flip, low))
+        return found
+
+
+def scatter_places(kinds):
+    found = []
+    for part, kind in enumerate(kinds):
+        masks = step_masks(tuple(reversed(scatter_steps(kind))))
+        for at, flip in enumerate((0, CORE[0])):
+            for place, (high, low) in enumerate(masks):
+                found.append((part, part * 2 + at, place, high ^ flip, low))
+    return found
+
+
+class ScatterChain:
+
+    def __init__(self, kept, sent, kind):
+        self.steps = scatter_steps(kind)
+        self.sent = [sent]
+        self.terms = [kept, exchange(sent, CORE)]
+        self.size = kept.shape[0]
+        self.at = 0
+
+    def total(self, first):
+        terms = [term[first : first + self.size].astype(jnp.float32) for term in self.terms]
+        return sum(terms[1:], terms[0])
+
+    def advance(self, *after):
+        self.terms = tie(self.terms, *after)
+        moves = moves_of(self.steps[self.at])
+        self.size //= len(moves)
+        self.sent = [
+            self.total(at * self.size).astype(jnp.bfloat16) for at in range(1, len(moves))
+        ]
+        self.terms = self.terms + [
+            exchange(sent, move) for sent, move in zip(self.sent, moves[1:])
+        ]
+        self.at += 1
+
+    def finish(self, *after):
+        self.terms = tie(self.terms, *after)
+        return self.total(0)[0]
+
+    def marks(self):
+        return self.sent
+
+
+def advance_all(chains, *after):
+    terms = tie([chain.terms for chain in chains], *after)
+    for chain, found in zip(chains, terms):
+        chain.terms = found
+        chain.advance()
+
+
+ANYWHERE = pl.BlockSpec(memory_space=pl.ANY)
+SCALARS = pl.BlockSpec(memory_space=pltpu.SMEM)
+VMEM_LIMIT = 58 << 20
+
+
+def cost(flops, moved, transcendentals=0):
+    return pl.CostEstimate(flops=flops // 8, bytes_accessed=moved // 8, transcendentals=0)
+
+
+def low_shape(*shape):
+    return jax.ShapeDtypeStruct(shape, jnp.bfloat16)
+
+
+def wide_shape(*shape):
+    return jax.ShapeDtypeStruct(shape, jnp.float32)
+
+
+def whole(*shape):
+    return pl.BlockSpec(shape, lambda *step: (0,) * len(shape))
+
+
+def block_span(block, count):
+    reach = -(-WINDOW // BLOCK)
+    return max(0, block - reach), min(count - 1, block + reach)
+
+
+def split_three(values):
+    high = values.astype(jnp.bfloat16)
+    rest = values - high.astype(jnp.float32)
+    mid = rest.astype(jnp.bfloat16)
+    low = (rest - mid.astype(jnp.float32)).astype(jnp.bfloat16)
+    return high, mid, low
+
+
+def window_edge(tile, row_block, column_block):
+    if (abs(row_block - column_block) + 1) * BLOCK - 1 < WINDOW:
+        return tile
+    row = lax.broadcasted_iota(jnp.int32, tile.shape, 0) + row_block * BLOCK
+    column = lax.broadcasted_iota(jnp.int32, tile.shape, 1) + column_block * BLOCK
+    return jnp.where(jnp.abs(row - column) < WINDOW, tile, MASKED)
+
+
+def attend_kernel(seg_ref, q_ref, k_ref, v_ref, out_ref, qx_ref, kx_ref, held_ref):
+    length = q_ref.shape[0]
+    count = length // BLOCK
+    lane = lax.broadcasted_iota(jnp.int32, (length, 128), 1)
+    seg = seg_ref[...]
+    q_heads, k_heads, v_heads = ([], [], [])
+    for head in range(2):
+        own = (lane < 64) if head == 0 else (lane >= 64)
+        extra = lane - 64 if head == 0 else lane
+        same = extra == seg
+        q_extra = jnp.where(same, 1.0, 0.0).astype(jnp.bfloat16)
+        k_extra = jnp.where(
+            extra < 4, jnp.where(same, 0.0, MASKED), jnp.where(extra < 7, -1.0, 0.0)
+        ).astype(jnp.bfloat16)
+        v_extra = jnp.where(extra == 0, 1.0, 0.0).astype(jnp.bfloat16)
+        q_heads.append(jnp.where(own, q_ref[...], q_extra))
+        k_heads.append(jnp.where(own, k_ref[...], k_extra))
+        v_heads.append(jnp.where(own, v_ref[...], v_extra))
+        kx_ref[head] = k_heads[head]
+    units = [(head, block) for head in range(2) for block in range(count)]
+
+    def score(unit):
+        head, block = unit
+        low, high = block_span(block, count)
+        rows = slice(block * BLOCK, (block + 1) * BLOCK)
+        tile = dot_last(q_heads[head][rows], k_heads[head][low * BLOCK : (high + 1) * BLOCK])
+        return [
+            window_edge(tile[:, (at - low) * BLOCK : (at - low + 1) * BLOCK], block, at)
+            for at in range(low, high + 1)
+        ]
+
+    def finish(unit, tiles):
+        head, block = unit
+        low, high = block_span(block, count)
+        rows = slice(block * BLOCK, (block + 1) * BLOCK)
+        most = tiles[0]
+        for tile in tiles[1:]:
+            most = jnp.maximum(most, tile)
+        top = jnp.max(most, axis=1, keepdims=True)
+        raised = jnp.concatenate(
+            [jnp.exp2(tile - top).astype(jnp.bfloat16) for tile in tiles], axis=1
+        )
+        mixed = dot_plain(raised, v_heads[head][low * BLOCK : (high + 1) * BLOCK])
+        norm_sum = mixed[:, 64:65] if head == 0 else mixed[:, 0:1]
+        held_ref[head, rows, :] = mixed * (1.0 / norm_sum)
+        first, second, third = split_three(top + jnp.log2(norm_sum))
+        extra = lane[:BLOCK] - 64 if head == 0 else lane[:BLOCK]
+        qx_ref[head, rows, :] = jnp.where(
+            extra == 4,
+            first,
+            jnp.where(extra == 5, second, jnp.where(extra == 6, third, q_heads[head][rows])),
+        )
+
+    tiles = score(units[0])
+    for at, unit in enumerate(units):
+        following = score(units[at + 1]) if at + 1 < len(units) else None
+        finish(unit, tiles)
+        tiles = following
+    out_ref[...] = jnp.where(lane < 64, held_ref[0], held_ref[1]).astype(jnp.bfloat16)
+
+
+def attend(queries, keys, values, seg, first, count, earlier=None):
+    length, width = queries.shape
+    pair = pl.BlockSpec((length, 128), lambda step: (0, first + step))
+    padded = pl.BlockSpec((2, length, 128), lambda step: (first + step, 0, 0))
+    passed = 0 if earlier is None else 3
+    operands = (seg, queries, keys, values) + (earlier or ())
+
+    def kernel(seg_ref, q_ref, k_ref, v_ref, *refs):
+        attend_kernel(seg_ref, q_ref, k_ref, v_ref, *refs[passed:])
+
+    return pl.pallas_call(
+        kernel,
+        grid=(count,),
+        in_specs=[pl.BlockSpec((length, 1), lambda step: (0, 0)), pair, pair, pair]
+        + [pl.BlockSpec(memory_space=pl.ANY)] * passed,
+        out_specs=[pair, padded, padded],
+        out_shape=[
+            jax.ShapeDtypeStruct((length, width), jnp.bfloat16),
+            jax.ShapeDtypeStruct((width // HEAD_DIM, length, 128), jnp.bfloat16),
+            jax.ShapeDtypeStruct((width // HEAD_DIM, length, 128), jnp.bfloat16),
+        ],
+        scratch_shapes=[pltpu.VMEM((2, length, 128), jnp.float32)],
+        input_output_aliases={4 + at: at for at in range(passed)},
+        compiler_params=pltpu.CompilerParams(vmem_limit_bytes=VMEM_LIMIT),
+        cost_estimate=cost(3_500_000_000 * count, (2 << 20) * count),
+        name="attend",
+    )(*operands)
+
+
+def attend_back_kernel(qx_ref, kx_ref, v_ref, out_ref, grad_ref, dq_ref, dk_ref, dv_ref, held_ref):
+    length = v_ref.shape[0]
+    count = length // BLOCK
+    lane = lax.broadcasted_iota(jnp.int32, (length, 128), 1)
+    grad = grad_ref[...]
+    for head in range(2):
+        mine = slice(head * 64, (head + 1) * 64)
+        own = (lane < 64) if head == 0 else (lane >= 64)
+        extra = lane - 64 if head == 0 else lane
+        product = jnp.where(
+            own, grad.astype(jnp.float32) * out_ref[...].astype(jnp.float32), 0.0
+        )
+        first, second, third = split_three(-jnp.sum(product, axis=1, keepdims=True))
+        grad_head = jnp.where(
+            own,
+            grad,
+            jnp.where(
+                extra == 0,
+                first,
+                jnp.where(extra == 1, second, jnp.where(extra == 2, third, jnp.zeros_like(grad))),
+            ),
+        )
+        v_head = jnp.where(own, v_ref[...], jnp.where(extra < 3, 1.0, 0.0).astype(jnp.bfloat16))
+        q_head, k_head = (qx_ref[head], kx_ref[head])
+        k_turned = k_head.T[mine]
+        for block in range(count):
+            low, high = block_span(block, count)
+            keys = slice(block * BLOCK, (block + 1) * BLOCK)
+            span = slice(low * BLOCK, (high + 1) * BLOCK)
+            tile = dot_last(k_head[keys], q_head[span])
+            soft = jnp.concatenate(
+                [
+                    jnp.exp2(
+                        window_edge(tile[:, (at - low) * BLOCK : (at - low + 1) * BLOCK], block, at)
+                    )
+                    for at in range(low, high + 1)
+                ],
+                axis=1,
+            )
+            grad_soft = dot_last(v_head[keys], grad_head[span])
+            grad_score = (soft * grad_soft).astype(jnp.bfloat16)
+            grad_value = dot_plain(soft.astype(jnp.bfloat16), grad_head[span])
+            grad_key = dot_plain(grad_score, q_head[span]) * (1.0 / LOG2E)
+            dv_ref[keys, mine] = grad_value[:, mine].astype(jnp.bfloat16)
+            dk_ref[keys, mine] = grad_key[:, mine].astype(jnp.bfloat16)
+            grad_query = dot_plain(k_turned[:, keys], grad_score)
+            if block == 0:
+                held_ref[mine, span] = grad_query
+                if high + 1 < count:
+                    held_ref[mine, (high + 1) * BLOCK :] = jnp.zeros(
+                        (64, length - (high + 1) * BLOCK), jnp.float32
+                    )
+            else:
+                held_ref[mine, span] += grad_query
+    dq_ref[...] = (held_ref[...] * (1.0 / math.sqrt(HEAD_DIM))).T.astype(jnp.bfloat16)
+
+
+def attend_back(
+    q_padded, k_padded, values, mixed, grad_mixed, first, count, out_first, out_count, earlier=None
+):
+    length, width = values.shape
+    pair = pl.BlockSpec((length, 128), lambda step: (0, first + step))
+    out_pair = pl.BlockSpec((length, 128), lambda step: (0, first - out_first + step))
+    padded = pl.BlockSpec((2, length, 128), lambda step: (first + step, 0, 0))
+    passed = 0 if earlier is None else 3
+    operands = (q_padded, k_padded, values, mixed, grad_mixed) + tuple(earlier or ())
+
+    def kernel(qx_ref, kx_ref, v_ref, out_ref, grad_ref, *refs):
+        attend_back_kernel(qx_ref, kx_ref, v_ref, out_ref, grad_ref, *refs[passed:])
+
+    return pl.pallas_call(
+        kernel,
+        grid=(count,),
+        in_specs=[padded, padded, pair, pair, pair]
+        + [pl.BlockSpec(memory_space=pl.ANY)] * passed,
+        out_specs=[out_pair, out_pair, out_pair],
+        out_shape=[jax.ShapeDtypeStruct((length, 128 * out_count), jnp.bfloat16)] * 3,
+        scratch_shapes=[pltpu.VMEM((128, length), jnp.float32)],
+        input_output_aliases={5 + at: at for at in range(passed)},
+        compiler_params=pltpu.CompilerParams(vmem_limit_bytes=VMEM_LIMIT),
+        cost_estimate=cost(5_000_000_000 * count, (2 << 20) * count),
+        name="attend_back",
+    )(*operands)
+
+
+MASK_ROW = 16
+
+
+def shards_kernel(
+    place_ref, wq_ref, wk_ref, wv_ref, wo_ref, wu_ref, wd_ref, bq_ref, bv_ref, bu_ref, gain_ref,
+    shift_ref, mask_ref, first_ref, second_ref, wide_ref, low_ref, high_ref,
+):
+    rows, width = wq_ref.shape
+    half = width // 2
+    first_ref[:, :width] = wq_ref[...]
+    first_ref[:, width : width + half] = wk_ref[:, :half]
+    second_ref[:, :half] = wk_ref[:, half:]
+    second_ref[:, half:] = wv_ref[...]
+    lane = lax.broadcasted_iota(jnp.int32, (1, 128), 1)
+
+    def spread(ref):
+        values = ref[...].astype(jnp.float32)
+        size = values.shape[1]
+        lanes = jnp.concatenate([values] * (128 // size), axis=1)
+        return [
+            jnp.where((row * 128 + lane) // size == place_ref[0], lanes, 0.0)
+            for row in range(width // 128)
+        ]
+
+    def flat(ref):
+        values = ref[...].astype(jnp.float32)
+        return [
+            jnp.concatenate([values[at : at + 1], values[at + 1 : at + 2]], axis=1)
+            for at in range(0, values.shape[0], 2)
+        ]
+
+    count = jnp.sum(mask_ref[...].astype(jnp.float32))
+    high = jnp.floor(count / 256.0)
+    count_row = jnp.where(lane == 0, high, jnp.where(lane == 1, count - 256.0 * high, 0.0))
+    lines = spread(bq_ref) + spread(bv_ref) + [bu_ref[...].astype(jnp.float32)]
+    lines = lines + flat(gain_ref) + flat(shift_ref) + [count_row]
+    lines = lines + [jnp.zeros((1, 128), jnp.float32)] * (MASK_ROW - len(lines))
+    mask = mask_ref[...].astype(jnp.float32)
+    for row in range(mask.shape[0]):
+        lines = lines + [
+            mask[row : row + 1, at : at + 128] for at in range(0, mask.shape[1], 128)
+        ]
+    lines = lines + [jnp.zeros((1, 128), jnp.float32)] * (rows - len(lines))
+    first_ref[:, width + half :] = jnp.concatenate(lines, axis=0).astype(jnp.bfloat16)
+    wide_ref[:, : wu_ref.shape[1]] = wu_ref[...]
+    wide_ref[:, wu_ref.shape[1] :] = wo_ref[...]
+    cut = low_ref.shape[1]
+    low_ref[...] = wd_ref[:, :cut]
+    high_ref[...] = wd_ref[:, cut:]
+
+
+def shards(place, w_query, w_key, w_value, w_out, w_up, w_down, small):
+    rows, width = w_query.shape
+    hidden = w_up.shape[1]
+    operands = (w_query, w_key, w_value, w_out, w_up, w_down) + small
+    outs = [
+        low_shape(rows, width + width // 2 + 128),
+        low_shape(rows, width // 2 + width),
+        low_shape(rows, hidden + width),
+        low_shape(rows, hidden // 2),
+        low_shape(rows, hidden // 2),
+    ]
+    return pl.pallas_call(
+        shards_kernel,
+        in_specs=[SCALARS] + [whole(*operand.shape) for operand in operands],
+        out_specs=[whole(*out.shape) for out in outs],
+        out_shape=outs,
+        compiler_params=pltpu.CompilerParams(vmem_limit_bytes=VMEM_LIMIT),
+        cost_estimate=cost(0, 2 << 20),
+        name="shards",
+    )(place, *operands)
+
+
+def qkv_kernel(spans, places, place_ref, row_ref, *refs):
+    count = 1 + max(source for _, source, _, _, _ in places)
+    sources = refs[:count]
+    q_ref, k_ref, v_ref, full_ref, small_out, held, small, sems, out_sem = refs[count:]
+    me_fsdp, me_tp = (place_ref[0], place_ref[1])
+    rows = sources[0].shape[1]
+    width = q_ref.shape[1]
+    fsdp_count = held.shape[0] // rows
+    copies = {0: [], 1: [], 2: [], 3: []}
+    for part, source, place, high, low in places:
+        fsdp, tp = (me_fsdp ^ high, me_tp ^ low)
+        for start, size, target, per_tp, column in spans[part]:
+            if target == 3:
+                from_ref = sources[source].at[place, pl.ds(0, small.shape[1]), pl.ds(start, size)]
+                to_ref = small.at[tp * fsdp_count + fsdp]
+            else:
+                row = pl.multiple_of(fsdp * rows, rows)
+                lane = pl.multiple_of(tp * per_tp + column, 128)
+                from_ref = sources[source].at[place, :, pl.ds(start, size)]
+                to_ref = held.at[pl.ds(row, rows), pl.ds(lane, size)]
+            total = sum(len(group) for group in copies.values())
+            copies[target].append(pltpu.make_async_copy(from_ref, to_ref, sems.at[total]))
+            copies[target][-1].start()
+
+    def bias(first):
+        halves = [
+            jnp.sum(
+                small[tp * fsdp_count : (tp + 1) * fsdp_count].astype(jnp.float32), axis=0
+            )
+            for tp in range(2)
+        ]
+        count = width // 256
+        lanes = [
+            half[first + at : first + at + 1]
+            for group in (range(count - 1), (count - 1,))
+            for half in halves
+            for at in group
+        ]
+        return jnp.concatenate(lanes, axis=1)
+
+    scale = LOG2E / math.sqrt(HEAD_DIM)
+    for copy in copies[3]:
+        copy.wait()
+    out_copies = [pltpu.make_async_copy(small, small_out, out_sem.at[3])]
+    out_copies[0].start()
+    for target, out_ref in ((0, q_ref), (1, k_ref), (2, v_ref)):
+        for copy in copies[target]:
+            copy.wait()
+        span = pl.ds(target * width, width)
+        out_copies.append(
+            pltpu.make_async_copy(held.at[:, span], full_ref.at[:, span], out_sem.at[target])
+        )
+        out_copies[-1].start()
+        added = bias(0 if target == 0 else width // 256) if target != 1 else None
+        for block in range(row_ref.shape[0] // BLOCK):
+            lines = slice(block * BLOCK, (block + 1) * BLOCK)
+            found = dot_plain(row_ref[lines], held[:, target * width : (target + 1) * width])
+            if added is not None:
+                found = found + added
+            if target == 0:
+                found = found * scale
+            out_ref[lines] = found.astype(jnp.bfloat16)
+    for copy in out_copies:
+        copy.wait()
+
+
+def qkv_project(chain, spans, place, row_low, width, small_rows):
+    length, features = row_low.shape
+    sources = chain.sources()
+    places = chain.places()
+    devices = lax.axis_size("fsdp") * lax.axis_size("tp")
+    copies = sum(len(spans[entry[0]]) for entry in places)
+    return pl.pallas_call(
+        partial(qkv_kernel, spans, places),
+        in_specs=[SCALARS, whole(length, features)] + [ANYWHERE] * len(sources),
+        out_specs=[whole(length, width)] * 3 + [ANYWHERE] * 2,
+        out_shape=[low_shape(length, width)] * 3
+        + [low_shape(features, 3 * width), low_shape(devices, small_rows, 128)],
+        scratch_shapes=[
+            pltpu.VMEM((features, 3 * width), jnp.bfloat16),
+            pltpu.VMEM((devices, small_rows, 128), jnp.bfloat16),
+            pltpu.SemaphoreType.DMA((copies,)),
+            pltpu.SemaphoreType.DMA((4,)),
+        ],
+        compiler_params=pltpu.CompilerParams(vmem_limit_bytes=VMEM_LIMIT),
+        cost_estimate=cost(6 * length * features * width, 24 << 20),
+        name="qkv_project",
+    )(place, row_low, *sources)
+
+
+def unit_of(values):
+    centred = values - jnp.mean(values, axis=-1, keepdims=True)
+    inverse = lax.rsqrt(jnp.mean(centred * centred, axis=-1, keepdims=True) + EPSILON)
+    return centred * inverse, inverse
+
+
+def out_up_kernel(
+    mixed_ref, row_ref, out_w_ref, up_w_ref, vector_ref, b_ref,
+    active_ref, slope_ref, unit_ref, inverse_ref, hidden_ref, full_out_ref,
+):
+    length, features = row_ref.shape
+    late = out_w_ref.shape[3] // 4
+    early = 3 * late
+
+    @pl.when(pl.program_id(0) == 0)
+    def _():
+        for tp in range(2):
+            lanes = pl.ds(tp * early, early)
+            full_out_ref[:, lanes] = out_w_ref[:, tp, :, :early].reshape(features, early)
+            lanes = pl.ds(2 * early + tp * late, late)
+            full_out_ref[:, lanes] = out_w_ref[:, tp, :, early:].reshape(features, late)
+        for block in range(length // BLOCK):
+            lines = slice(block * BLOCK, (block + 1) * BLOCK)
+            before = (
+                row_ref[lines].astype(jnp.float32)
+                + dot_last(mixed_ref[lines], full_out_ref[...])
+                + vector_ref[0:1]
+            )
+            unit, inverse = unit_of(before)
+            unit_ref[lines] = unit
+            inverse_ref[lines] = inverse
+            hidden_ref[lines] = (unit * vector_ref[1:2] + vector_ref[2:3]).astype(jnp.bfloat16)
+
+    weight = up_w_ref[:, 0].reshape(features, up_w_ref.shape[3])
+
+    def product(block):
+        lines = slice(block * BLOCK, (block + 1) * BLOCK)
+        return dot_plain(hidden_ref[lines], weight) + b_ref[...]
+
+    up = product(0)
+    count = length // BLOCK
+    for block in range(count):
+        following = product(block + 1) if block + 1 < count else None
+        lines = slice(block * BLOCK, (block + 1) * BLOCK)
+        cumulative = 0.5 * (1.0 + lax.erf(up * math.sqrt(0.5)))
+        density = jnp.exp2(up * up * (-0.5 * LOG2E)) * (1.0 / math.sqrt(2.0 * math.pi))
+        active_ref[lines] = (up * cumulative).astype(jnp.bfloat16)
+        slope_ref[lines] = (cumulative + up * density).astype(jnp.bfloat16)
+        up = following
+
+
+def out_up_project(mixed, row_low, gathered, vectors, bias, local_hidden, local_width):
+    length, features = row_low.shape
+    fsdp_count, tp_count, rows, _ = gathered.shape
+    hidden_units = local_hidden * tp_count
+    block_width = math.gcd(math.gcd(local_hidden, 512), local_width)
+    each = local_hidden // block_width
+    column = pl.BlockSpec((length, block_width), lambda step: (0, step))
+    return pl.pallas_call(
+        out_up_kernel,
+        grid=(hidden_units // block_width,),
+        in_specs=[
+            whole(length, features),
+            whole(length, features),
+            pl.BlockSpec(
+                (fsdp_count, tp_count, rows, local_width),
+                lambda step: (0, 0, 0, local_hidden // local_width),
+            ),
+            pl.BlockSpec(
+                (fsdp_count, 1, rows, block_width),
+                lambda step: (0, step // each, 0, step % each),
+            ),
+            whole(*vectors.shape),
+            pl.BlockSpec((1, block_width), lambda step: (0, step)),
+        ],
+        out_specs=[column, column]
+        + [whole(length, features), whole(length, 1), whole(length, features)]
+        + [whole(features, features)],
+        out_shape=[
+            low_shape(length, hidden_units),
+            low_shape(length, hidden_units),
+            wide_shape(length, features),
+            wide_shape(length, 1),
+            low_shape(length, features),
+            low_shape(features, features),
+        ],
+        compiler_params=pltpu.CompilerParams(vmem_limit_bytes=VMEM_LIMIT),
+        cost_estimate=cost(
+            2 * length * features * (hidden_units + features),
+            36 << 20,
+            2 * length * hidden_units,
+        ),
+        name="out_up_project",
+    )(mixed, row_low, gathered, gathered, vectors, bias)
+
+
+def down_kernel(
+    places, place_ref, active_ref, unit_ref, teacher_ref, weight_ref, vector_ref, *refs
+):
+    count = 1 + max(source for _, source, _, _, _ in places)
+    sources = refs[:count]
+    out_ref, grad_ref, low_ref, sums_ref, full_ref, held, sems, out_sem = refs[count:]
+    rows = sources[0].shape[1]
+    part_width = sources[0].shape[2]
+    step = pl.program_id(0)
+    last = pl.num_programs(0) - 1
+    full_copy = pltpu.make_async_copy(held, full_ref, out_sem)
+
+    @pl.when(step == 0)
+    def _():
+        me_fsdp, me_tp = (place_ref[0], place_ref[1])
+        copies = []
+        for at, (part, source, place, high, low) in enumerate(places):
+            row = pl.multiple_of((me_fsdp ^ high) * rows, rows)
+            lane = (me_tp ^ low) * (2 * part_width) + part * part_width
+            lane = pl.multiple_of(lane, 128)
+            copies.append(
+                pltpu.make_async_copy(
+                    sources[source].at[place],
+                    held.at[pl.ds(row, rows), pl.ds(lane, part_width)],
+                    sems.at[at],
+                )
+            )
+            copies[-1].start()
+        for copy in copies:
+            copy.wait()
+        full_copy.start()
+        sums_ref[...] = jnp.zeros_like(sums_ref)
+
+    normed_first = unit_ref[...] * vector_ref[0:1] + vector_ref[1:2]
+    before = normed_first + dot_last(active_ref[...], held[...]) + vector_ref[2:3]
+    unit, inverse = unit_of(before)
+    gain = vector_ref[3:4]
+    result = unit * gain + vector_ref[4:5]
+    out_ref[...] = result.astype(jnp.bfloat16)
+    differ = result - teacher_ref[...].astype(jnp.float32)
+    grad = differ * weight_ref[...]
+    scaled = grad * gain
+    grad_before = inverse * (
+        scaled
+        - jnp.mean(scaled, axis=-1, keepdims=True)
+        - unit * jnp.mean(scaled * unit, axis=-1, keepdims=True)
+    )
+    grad_ref[...] = grad_before
+    low_ref[...] = grad_before.astype(jnp.bfloat16)
+    for at, term in enumerate((grad * unit, grad, grad_before, grad * differ)):
+        sums_ref[at : at + 1] += jnp.sum(term, axis=0, keepdims=True)
+
+    @pl.when(step == last)
+    def _():
+        full_copy.wait()
+
+
+def down_project(chain, place, active, unit, teacher, weight, vectors):
+    length, hidden_units = active.shape
+    features = unit.shape[1]
+    sources, places = (chain.sources(), chain.places())
+    line = lambda width: pl.BlockSpec((BLOCK, width), lambda step: (step, 0))
+    return pl.pallas_call(
+        partial(down_kernel, places),
+        grid=(length // BLOCK,),
+        in_specs=[SCALARS, line(hidden_units), line(features), line(features), line(1)]
+        + [whole(*vectors.shape)]
+        + [ANYWHERE] * len(sources),
+        out_specs=[line(features), line(features), line(features), whole(8, features), ANYWHERE],
+        out_shape=[
+            low_shape(length, features),
+            wide_shape(length, features),
+            low_shape(length, features),
+            wide_shape(8, features),
+            low_shape(features, hidden_units),
+        ],
+        scratch_shapes=[
+            pltpu.VMEM((features, hidden_units), jnp.bfloat16),
+            pltpu.SemaphoreType.DMA((len(places),)),
+            pltpu.SemaphoreType.DMA,
+        ],
+        compiler_params=pltpu.CompilerParams(vmem_limit_bytes=VMEM_LIMIT),
+        cost_estimate=cost(2 * length * features * hidden_units, 36 << 20),
+        name="down_project",
+    )(place, active, unit, teacher, weight, vectors, *sources)
+
+
+def column_copies(places, tp_places, each, block_width, me_fsdp, held, pieces, sems, at):
+    rows = pieces[0].shape[1]
+    found = []
+    for number, (_, output, place, high, low) in enumerate(places):
+        if low:
+            continue
+        row = pl.multiple_of((me_fsdp ^ high) * rows, rows)
+        lane = pl.multiple_of(at % each * block_width, 128)
+        found.append(
+            pltpu.make_async_copy(
+                held.at[at, pl.ds(row, rows)],
+                pieces[output].at[place + at // each * tp_places, :, pl.ds(lane, block_width)],
+                sems.at[at, number],
+            )
+        )
+    return found
+
+
+def down_back_kernel(
+    places, tp_places, each, place_ref, grad_ref, active_ref, kept_ref, sent_ref,
+    turned, held, sems,
+):
+    step = pl.program_id(0)
+
+    @pl.when(step == 0)
+    def _():
+        turned[...] = grad_ref[...].T
+
+    copies = partial(
+        column_copies, places, tp_places, each, active_ref.shape[1], place_ref[0], held,
+        (kept_ref, sent_ref), sems,
+    )
+    held[step] = dot_plain(turned[...], active_ref[...]).astype(jnp.bfloat16)
+    for copy in copies(step):
+        copy.start()
+
+    @pl.when(step == 2 * each - 1)
+    def _():
+        for at in range(2 * each):
+            for copy in copies(at):
+                copy.wait()
+
+
+def up_back_kernel(
+    places, tp_places, each, place_ref, grad_ref, hidden_ref, slope_ref, down_ref, up_ref,
+    total_ref, bias_ref, kept_ref, sent_ref, turned, held, sems,
+):
+    step = pl.program_id(0)
+    length, features = grad_ref.shape
+    block_width = slope_ref.shape[1]
+
+    @pl.when(step == 0)
+    def _():
+        turned[...] = hidden_ref[...].T
+        total_ref[...] = jnp.zeros_like(total_ref)
+
+    copies = partial(
+        column_copies, places, tp_places, each, block_width, place_ref[0], held,
+        (kept_ref, sent_ref), sems,
+    )
+    down_weight = down_ref[...]
+    up_weight = up_ref[:, 0].reshape(features, block_width)
+    spans = [slice(at * BLOCK, (at + 1) * BLOCK) for at in range(length // BLOCK)]
+    grads, bias = ([], jnp.zeros((1, block_width), jnp.float32))
+    found = dot_plain(grad_ref[spans[0]], down_weight)
+    for at, span in enumerate(spans):
+        following = (
+            dot_plain(grad_ref[spans[at + 1]], down_weight) if at + 1 < len(spans) else None
+        )
+        grad_up = found * slope_ref[span].astype(jnp.float32)
+        bias = bias + jnp.sum(grad_up, axis=0, keepdims=True)
+        grads.append(grad_up.astype(jnp.bfloat16))
+        found = following
+    bias_ref[...] = bias
+    grad_up = jnp.concatenate(grads, axis=0)
+    held[step] = dot_plain(turned[...], grad_up).astype(jnp.bfloat16)
+    for copy in copies(step):
+        copy.start()
+    total_ref[...] += dot_last(grad_up, up_weight)
+
+    @pl.when(step == 2 * each - 1)
+    def _():
+        for at in range(2 * each):
+            for copy in copies(at):
+                copy.wait()
+
+
+def column_plan(kind, local_hidden):
+    block_width = math.gcd(local_hidden, 512)
+    each = local_hidden // block_width
+    places = scatter_places([kind])
+    tp_places = next(place for _, at, place, high, low in places if at == 0 and low and not high)
+
+    def column(step, where):
+        return (where[1] ^ (step // each)) * each + step % each
+
+    return block_width, each, places, tp_places, column
+
+
+def keep(*shape):
+    return pl.BlockSpec(shape, lambda step, where: (0,) * len(shape))
+
+
+def column_scratch(features, length, each, block_width, places):
+    return [
+        pltpu.VMEM((features, length), jnp.bfloat16),
+        pltpu.VMEM((2 * each, features, block_width), jnp.bfloat16),
+        pltpu.SemaphoreType.DMA((2 * each, len(places))),
+    ]
+
+
+def down_back(place, grad_down, active, rows, local_hidden, kind):
+    length, features = grad_down.shape
+    block_width, each, places, tp_places, column = column_plan(kind, local_hidden)
+    piece = low_shape(len(places) // 2, rows, local_hidden)
+    return pl.pallas_call(
+        partial(down_back_kernel, places, tp_places, each),
+        grid_spec=pltpu.PrefetchScalarGridSpec(
+            num_scalar_prefetch=1,
+            grid=(2 * each,),
+            in_specs=[
+                keep(length, features),
+                pl.BlockSpec((length, block_width), lambda step, where: (0, column(step, where))),
+            ],
+            out_specs=[ANYWHERE] * 2,
+            scratch_shapes=column_scratch(features, length, each, block_width, places),
+        ),
+        out_shape=[piece] * 2,
+        compiler_params=pltpu.CompilerParams(vmem_limit_bytes=VMEM_LIMIT),
+        cost_estimate=cost(4 * length * features * local_hidden, 20 << 20),
+        name="down_back",
+    )(place, grad_down, active)
+
+
+def up_back(place, grad_down, hidden, slope, full_down, gathered, kind):
+    length, features = hidden.shape
+    fsdp_count, tp_count, rows, _ = gathered.shape
+    local_hidden = full_down.shape[1] // tp_count
+    block_width, each, places, tp_places, column = column_plan(kind, local_hidden)
+    piece = low_shape(len(places) // 2, rows, local_hidden)
+    block = pl.BlockSpec((length, block_width), lambda step, where: (0, column(step, where)))
+    return pl.pallas_call(
+        partial(up_back_kernel, places, tp_places, each),
+        grid_spec=pltpu.PrefetchScalarGridSpec(
+            num_scalar_prefetch=1,
+            grid=(2 * each,),
+            in_specs=[
+                keep(length, features),
+                keep(length, features),
+                block,
+                pl.BlockSpec((features, block_width), lambda step, where: (0, column(step, where))),
+                pl.BlockSpec(
+                    (fsdp_count, 1, rows, block_width),
+                    lambda step, where: (0, where[1] ^ (step // each), 0, step % each),
+                ),
+            ],
+            out_specs=[
+                keep(length, features),
+                pl.BlockSpec((1, block_width), lambda step, where: (0, column(step, where))),
+            ]
+            + [ANYWHERE] * 2,
+            scratch_shapes=column_scratch(features, length, each, block_width, places),
+        ),
+        out_shape=[wide_shape(length, features), wide_shape(1, local_hidden * tp_count)]
+        + [piece] * 2,
+        compiler_params=pltpu.CompilerParams(vmem_limit_bytes=VMEM_LIMIT),
+        cost_estimate=cost(12 * length * features * local_hidden, 40 << 20),
+        name="up_back",
+    )(place, grad_down, hidden, slope, full_down, gathered)
+
+
+def norm_back_kernel(
+    base_ref, grad_ref, unit_ref, inverse_ref, gain_ref, weight_ref, first_ref, low_ref, mixed_ref, sums_ref
+):
+    @pl.when(pl.program_id(0) == 0)
+    def _():
+        sums_ref[...] = jnp.zeros_like(sums_ref)
+
+    grad, unit = (base_ref[...] + grad_ref[...], unit_ref[...])
+    scaled = grad * gain_ref[...]
+    found = inverse_ref[...] * (
+        scaled
+        - jnp.mean(scaled, axis=-1, keepdims=True)
+        - unit * jnp.mean(scaled * unit, axis=-1, keepdims=True)
+    )
+    first_ref[...] = found
+    low = found.astype(jnp.bfloat16)
+    low_ref[...] = low
+    mixed_ref[...] = dot_plain(low, weight_ref[...]).astype(jnp.bfloat16)
+    for at, term in enumerate((grad * unit, grad, found)):
+        sums_ref[at : at + 1] += jnp.sum(term, axis=0, keepdims=True)
+
+
+def norm_back(grad_second, grad_hidden, unit, inverse, gain, full_out):
+    length, features = unit.shape
+    line = lambda width: pl.BlockSpec((BLOCK, width), lambda step: (step, 0))
+    return pl.pallas_call(
+        norm_back_kernel,
+        grid=(length // BLOCK,),
+        in_specs=[line(features)] * 3 + [line(1), whole(1, features)]
+        + [whole(*full_out.shape)],
+        out_specs=[line(features), line(features), line(full_out.shape[1]), whole(8, features)],
+        out_shape=[
+            wide_shape(length, features),
+            low_shape(length, features),
+            low_shape(length, full_out.shape[1]),
+            wide_shape(8, features),
+        ],
+        compiler_params=pltpu.CompilerParams(vmem_limit_bytes=VMEM_LIMIT),
+        cost_estimate=cost(2 * length * features * features, 22 << 20),
+        name="norm_back",
+    )(grad_second, grad_hidden, unit, inverse, gain, full_out)
+
+
+def weight_grad_kernel(products, spans, places, extra, place_ref, *refs):
+    lefts = 1 + max(left for left, _ in products)
+    rights = 1 + max(right for _, right in products)
+    left_refs, right_refs = (refs[:lefts], refs[lefts : lefts + rights])
+    refs = refs[lefts + rights :]
+    if extra:
+        extra_ref, refs = (refs[0], refs[1:])
+    parts = 2 * len(spans)
+    pieces, scratch = (refs[:parts], refs[parts:])
+    turned, held, sems = (scratch[:lefts], scratch[lefts:-1], scratch[-1])
+    me_fsdp, me_tp = (place_ref[0], place_ref[1])
+    rows = pieces[0].shape[1]
+    started = []
+
+    def start(target):
+        for part, output, place, high, low in places:
+            fsdp, tp = (me_fsdp ^ high, me_tp ^ low)
+            for begin, size, which, per_tp, column in spans[part]:
+                if which != target:
+                    continue
+                if target == len(products):
+                    fsdp_count = extra_ref.shape[0] // 2
+                    from_ref = extra_ref.at[tp * fsdp_count + fsdp]
+                    row_span = pl.ds(0, extra_ref.shape[1])
+                else:
+                    row = pl.multiple_of(fsdp * rows, rows)
+                    lane = pl.multiple_of(tp * per_tp + column, 128)
+                    from_ref = held[target].at[pl.ds(row, rows), pl.ds(lane, size)]
+                    row_span = pl.ds(0, rows)
+                copy = pltpu.make_async_copy(
+                    from_ref,
+                    pieces[output].at[place, row_span, pl.ds(begin, size)],
+                    sems.at[len(started)],
+                )
+                copy.start()
+                started.append(copy)
+
+    if extra:
+        start(len(products))
+    for at, left in enumerate(left_refs):
+        turned[at][...] = left[...].T
+    for target, (left, right) in enumerate(products):
+        features = held[target].shape[0]
+        for block in range(features // BLOCK):
+            lines = slice(block * BLOCK, (block + 1) * BLOCK)
+            held[target][lines] = dot_plain(turned[left][lines], right_refs[right][...]).astype(
+                jnp.bfloat16
+            )
+        start(target)
+    for copy in started:
+        copy.wait()
+
+
+def weight_grads(place, lefts, rights, products, spans, kinds, rows, part_widths, extra=None):
+    length, features = lefts[0].shape
+    places = scatter_places(kinds)
+    copies = sum(len(spans[entry[0]]) for entry in places)
+    devices = lax.axis_size("fsdp") * lax.axis_size("tp")
+    outs = [low_shape(devices // 2, rows, part_widths[at // 2]) for at in range(2 * len(spans))]
+    operands = list(lefts) + list(rights) + ([] if extra is None else [extra])
+    flops = sum(2 * length * features * rights[right].shape[1] for _, right in products)
+    return pl.pallas_call(
+        partial(weight_grad_kernel, products, spans, places, extra is not None),
+        in_specs=[SCALARS] + [whole(*operand.shape) for operand in operands],
+        out_specs=[ANYWHERE] * len(outs),
+        out_shape=outs,
+        scratch_shapes=[pltpu.VMEM((features, length), jnp.bfloat16) for _ in lefts]
+        + [pltpu.VMEM((features, rights[right].shape[1]), jnp.bfloat16) for _, right in products]
+        + [pltpu.SemaphoreType.DMA((copies,))],
+        compiler_params=pltpu.CompilerParams(vmem_limit_bytes=VMEM_LIMIT),
+        cost_estimate=cost(flops, 16 << 20),
+        name="weight_grads",
+    )(place, *operands)
+
+
+def input_grad_kernel(flip, place_ref, base_ref, *refs):
+    grads, weight_ref, out_ref = (refs[:-2], refs[-2], refs[-1])
+    total = base_ref[...]
+    at = 0
+    for grad in grads:
+        width = grad.shape[1]
+        total = total + dot_last(grad[...], weight_ref[:, at : at + width])
+        at += width
+    out_ref[...] = total.astype(jnp.bfloat16)
+
+
+def input_grad(place, base, grads, full_qkv, flip):
+    length, features = base.shape
+    half = length // 2
+    each = half // BLOCK
+    line = lambda width: pl.BlockSpec(
+        (BLOCK, width), lambda step, where: ((where[1] ^ flip) * each + step, 0)
+    )
+    return pl.pallas_call(
+        partial(input_grad_kernel, flip),
+        grid_spec=pltpu.PrefetchScalarGridSpec(
+            num_scalar_prefetch=1,
+            grid=(each,),
+            in_specs=[line(features)]
+            + [line(grad.shape[1]) for grad in grads]
+            + [pl.BlockSpec(full_qkv.shape, lambda step, where: (0, 0))],
+            out_specs=pl.BlockSpec((BLOCK, features), lambda step, where: (step, 0)),
+        ),
+        out_shape=low_shape(half, features),
+        compiler_params=pltpu.CompilerParams(vmem_limit_bytes=VMEM_LIMIT),
+        cost_estimate=cost(2 * half * features * full_qkv.shape[1], 14 << 20),
+        name="input_grad",
+    )(place, base, *grads, full_qkv)
+
+
+def swap_in(pieces, tp_rank, *after):
+    mine = lax.dynamic_index_in_dim(pieces, tp_rank, 0, keepdims=False)
+    theirs = lax.dynamic_index_in_dim(pieces, 1 - tp_rank, 0, keepdims=False)
+    if after:
+        theirs = tie(theirs, *after)
+    arrived = exchange(theirs, ACROSS)
+    first = tp_rank == 0
+    return jnp.concatenate(
+        [jnp.where(first, mine, arrived), jnp.where(first, arrived, mine)], axis=0
+    )
+
+
+def both_rows(mine, arrived, tp_rank):
+    first = tp_rank == 0
+    return jnp.stack([jnp.where(first, mine, arrived), jnp.where(first, arrived, mine)])
+
+
+def on_device_rows(
+    inputs,
+    segment_ids,
+    valid_mask,
+    teacher,
+    w_query,
+    w_key,
+    w_value,
+    w_out,
+    b_query,
+    b_value,
+    w_up,
+    b_up,
+    w_down,
+    ln_gains,
+    ln_shifts,
+):
+    seq_count, piece_len, features = inputs.shape
+    fsdp_count, tp_count = (lax.axis_size("fsdp"), lax.axis_size("tp"))
+    fsdp_rank, tp_rank = (lax.axis_index("fsdp"), lax.axis_index("tp"))
+    devices = fsdp_count * tp_count
+    assert seq_count == tp_count
+    total_tokens = seq_count * piece_len * tp_count * fsdp_count
+    shard_rows, local_width = w_query.shape
+    local_hidden = w_up.shape[1]
+    width = local_width * tp_count
+    late_width = local_width // 4
+    early_width = 3 * late_width
+    half = local_width // 2
+    pairs = width // 128
+    late_pairs = pairs // 4
+    early_pairs = pairs - late_pairs
+    place = jnp.stack([fsdp_rank, tp_rank]).astype(jnp.int32)
+
+    late_at = 2 * early_width
+    qkv_spans = [
+        [
+            (0, early_width, 0, early_width, 0),
+            (early_width, late_width, 0, late_width, late_at),
+            (local_width, half, 1, early_width, width),
+            (local_width + half, 128, 3, 0, 0),
+        ],
+        [
+            (0, early_width - half, 1, early_width, width + half),
+            (early_width - half, late_width, 1, late_width, width + late_at),
+            (half, early_width, 2, early_width, 2 * width),
+            (half + early_width, late_width, 2, late_width, 2 * width + late_at),
+        ],
+    ]
+    small_rows = 32
+    small = (
+        b_query[None],
+        b_value[None],
+        b_up[None],
+        ln_gains,
+        ln_shifts,
+        valid_mask,
+    )
+    up_cut = (local_hidden + local_width) // 2
+    up_rest = local_hidden - up_cut
+    up_spans = [
+        [(0, up_cut, 0, local_hidden, 0)],
+        [
+            (0, up_rest, 0, local_hidden, up_cut),
+            (up_rest, early_width, 1, early_width, 0),
+            (up_rest + early_width, late_width, 1, late_width, late_at),
+        ],
+    ]
+    qkv_first, qkv_second, up_shard, down_first, down_second = shards(
+        place, w_query, w_key, w_value, w_out.T, w_up, w_down.T, small
+    )
+    chain_qkv = GatherChain([qkv_first, qkv_second])
+    chain_down = GatherChain([down_first, down_second])
+    row_low = swap_in(inputs, tp_rank)
+    seg = lax.dynamic_index_in_dim(segment_ids, tp_rank, 0, keepdims=False)[:, None]
+    chain_qkv.advance()
+    chain_qkv.advance()
+    chain_qkv.advance(row_low)
+    chain_qkv.advance()
+    gathered = lax.all_gather(
+        tie(up_shard, chain_qkv.marks()), ("fsdp", "tp"), axis=0, tiled=False
+    ).reshape(fsdp_count, tp_count, shard_rows, local_hidden + local_width)
+    chain_qkv.finish()
+    chain_down.advance(chain_qkv.arrived)
+    queries, keys, values, full_qkv, small_all = qkv_project(
+        chain_qkv, qkv_spans, tie(place, chain_down.marks()), row_low, width, small_rows
+    )
+    valid_row = (
+        lax.dynamic_slice(
+            small_all.reshape(tp_count, fsdp_count, small_rows, 128),
+            (0, fsdp_rank, MASK_ROW + tp_rank * (piece_len // 128), 0),
+            (tp_count, 1, piece_len // 128, 128),
+        )
+        .reshape(-1)
+        .astype(jnp.float32)
+    )
+    small_all = small_all.astype(jnp.float32)
+    small_at = 2 * (local_width // 128)
+    bias_up = small_all[:, small_at].reshape(1, -1)
+
+    def feature_rows(columns, rows):
+        return (
+            columns[:fsdp_count]
+            .reshape(fsdp_count, rows, features // fsdp_count)
+            .transpose(1, 0, 2)
+            .reshape(rows, features)
+        )
+
+    gains = feature_rows(small_all[:, small_at + 1], 2)
+    shifts = feature_rows(small_all[:, small_at + 2 : small_at + 4], 4)
+    valid_count = jnp.sum(small_all[:, small_at + 4, 0] * 256.0 + small_all[:, small_at + 4, 1])
+
+    chain_down.advance(queries)
+    queries = tie(queries, chain_down.marks())
+    attended = attend(queries, keys, values, seg, 0, pairs // 2)
+    chain_down.advance(attended)
+    mixed, q_padded, k_padded = attend(
+        queries, keys, tie(values, chain_down.marks()), seg, pairs // 2, pairs // 2, attended
+    )
+    teacher_row = swap_in(teacher, tp_rank, attended)
+    chain_down.advance(mixed)
+    vectors = jnp.stack([shifts[2], gains[0], shifts[0]])
+    active, slope, unit_first, inverse_first, hidden_low, full_out = out_up_project(
+        tie(mixed, chain_down.marks()),
+        row_low,
+        gathered,
+        vectors,
+        bias_up,
+        local_hidden,
+        local_width,
+    )
+    chain_down.finish(active)
+    weight = (valid_row * (total_tokens / valid_count))[:, None]
+    vectors = jnp.stack([gains[0], shifts[0], shifts[3], gains[1], shifts[1]])
+    result_low, grad_second, grad_down, sums_second, full_down = down_project(
+        chain_down, place, active, unit_first, teacher_row, weight, vectors
+    )
+
+    chain_down = ScatterChain(
+        *down_back(place, grad_down, active, shard_rows, local_hidden, "across"), "across"
+    )
+    grad_hidden, grad_b_up, kept, sent = up_back(
+        place, tie(grad_down, chain_down.marks()), hidden_low, slope, full_down, gathered, "far"
+    )
+    chain_up = ScatterChain(kept, sent, "far")
+    chain_down.advance(grad_hidden)
+    grad_first, grad_attend, grad_mixed, sums_first = norm_back(
+        grad_second, tie(grad_hidden, chain_down.marks(), chain_up.marks()), unit_first, inverse_first, gains[:1], full_out
+    )
+    mine = lax.dynamic_slice_in_dim(result_low, tp_rank * piece_len, piece_len, 0)
+    theirs = lax.dynamic_slice_in_dim(result_low, (1 - tp_rank) * piece_len, piece_len, 0)
+    back = partial(attend_back, q_padded, k_padded, values, mixed)
+    chain_up.advance(grad_mixed)
+    early_grads = back(tie(grad_mixed, chain_up.marks()), 0, early_pairs // 2, 0, early_pairs)
+    early_grads = back(
+        grad_mixed, early_pairs // 2, early_pairs // 2, 0, early_pairs, early_grads
+    )
+    chain_down.advance(early_grads)
+    early_spans = [
+        [
+            (0, early_width, 0, early_width, 0),
+            (early_width, late_width, 0, late_width, late_at),
+            (local_width, early_width, 1, early_width, 0),
+        ],
+        [(0, early_width, 2, early_width, 0), (early_width, early_width, 3, early_width, 0)],
+    ]
+    early_first = local_width + early_width
+    early_kinds = ["across", "far_side"]
+    pieces = weight_grads(
+        place,
+        [grad_attend, tie(row_low, chain_down.marks())],
+        [mixed] + list(early_grads),
+        [(0, 0), (1, 1), (1, 2), (1, 3)],
+        early_spans,
+        early_kinds,
+        shard_rows,
+        [early_first, 2 * early_width],
+    )
+    early_chains = [
+        ScatterChain(pieces[2 * at], pieces[2 * at + 1], kind)
+        for at, kind in enumerate(early_kinds)
+    ]
+    chain_up.advance(pieces)
+    chain_down.advance(pieces)
+    arrived_out = exchange(tie(theirs, grad_mixed), ACROSS)
+    late_grads = back(
+        tie(grad_mixed, chain_up.marks(), chain_down.marks(), arrived_out),
+        early_pairs,
+        late_pairs,
+        early_pairs,
+        late_pairs,
+    )
+    advance_all([chain_up, chain_down] + early_chains, late_grads)
+    def feature_pieces(rows):
+        pieces = rows.reshape(rows.shape[0], fsdp_count, -1).transpose(1, 0, 2)
+        pieces = pieces.reshape(fsdp_count, -1, 128)
+        return jnp.concatenate([pieces] * tp_count, axis=0)
+
+    def bias_pieces(early, late):
+        sums = [
+            jnp.sum(part.astype(jnp.float32), axis=0).reshape(tp_count, -1) for part in (early, late)
+        ]
+        return jnp.concatenate(sums, axis=1).reshape(devices, -1)
+
+    bias_pair = jnp.concatenate(
+        [bias_pieces(early_grads[0], late_grads[0]), bias_pieces(early_grads[2], late_grads[2])],
+        axis=1,
+    )
+    bias_pair = jnp.pad(bias_pair, ((0, 0), (0, 128 - bias_pair.shape[1])))
+    squares = jnp.sum(sums_second[3]) * (valid_count / total_tokens)
+    lane = lax.broadcasted_iota(jnp.int32, (1, 128), 1)
+    square_rows = jnp.concatenate(
+        [
+            jnp.where(lane == tp_rank * fsdp_count + fsdp_rank, term.astype(jnp.float32), 0.0)
+            for term in split_three(squares)
+        ],
+        axis=0,
+    )
+    small = jnp.concatenate(
+        [
+            bias_pair[:, None],
+            grad_b_up.reshape(devices, 1, 128),
+            feature_pieces(
+                jnp.stack(
+                    [
+                        sums_first[0],
+                        sums_second[0],
+                        sums_first[1],
+                        sums_second[1],
+                        sums_first[2],
+                        sums_second[2],
+                    ]
+                )
+            ),
+            jnp.broadcast_to(square_rows[None], (devices, 3, 128)),
+        ],
+        axis=1,
+    )
+    small = jnp.pad(small, ((0, 0), (0, 16 - small.shape[1]), (0, 0)))
+    late_spans = [
+        [(at * late_width, late_width, at, late_width, 0) for at in range(3)]
+        + [(3 * late_width, 128, 3, 0, 0)]
+    ]
+    chain_late = ScatterChain(
+        *weight_grads(
+            place,
+            [
+                tie(
+                    row_low,
+                    chain_up.marks(),
+                    chain_down.marks(),
+                    [chain.marks() for chain in early_chains],
+                )
+            ],
+            list(late_grads),
+            [(0, 0), (0, 1), (0, 2)],
+            late_spans,
+            ["late"],
+            shard_rows,
+            [3 * late_width + 128],
+            small.astype(jnp.bfloat16),
+        ),
+        "late",
+    )
+    grads = [part for pair in zip(early_grads, late_grads) for part in pair]
+    input_theirs = input_grad(
+        place, tie(grad_first, chain_late.marks()), grads, full_qkv, 1
+    )
+    arrived_inputs = exchange(input_theirs, ACROSS)
+    advance_all([chain_late, chain_up] + early_chains, input_theirs)
+    input_mine = input_grad(
+        place,
+        tie(grad_first, chain_late.marks(), [chain.marks() for chain in early_chains]),
+        grads,
+        full_qkv,
+        0,
+    )
+    grad_inputs = both_rows(input_mine, arrived_inputs, tp_rank)
+    hidden_out = both_rows(mine, tie(arrived_out, input_mine), tp_rank)
+    advance_all([chain_late] + early_chains, input_mine)
+    waiting = [chain_late] + early_chains
+    while waiting:
+        advance_all(waiting)
+        waiting = [chain for chain in waiting if chain.at < len(chain.steps)]
+    for chain in [chain_up, chain_down] + early_chains:
+        assert chain.at == len(chain.steps)
+    grad_w_down, grad_w_up = (chain_down.finish(input_mine), chain_up.finish(input_mine))
+    early_one, early_two = [chain.finish() for chain in early_chains]
+    late = chain_late.finish()
+    early_qkv = (
+        early_one[:, local_width:],
+        early_two[:, :early_width],
+        early_two[:, early_width:],
+    )
+    grad_w_query, grad_w_key, grad_w_value = [
+        jnp.concatenate([early, late[:, at * late_width : (at + 1) * late_width]], axis=1)
+        for at, early in enumerate(early_qkv)
+    ]
+    own = late[:, 3 * late_width :]
+    bias_size, row = (b_query.shape[0], 2)
+    gain_rows = ln_gains.size // 128
+    shift_rows = ln_shifts.size // 128
+    loss_row = row + gain_rows + shift_rows
+    loss_value = jnp.sum(own[loss_row : loss_row + 3]) / (features * valid_count)
+    return (
+        hidden_out,
+        loss_value,
+        grad_inputs,
+        grad_w_query,
+        grad_w_key,
+        grad_w_value,
+        early_one[:, :local_width].T,
+        own[0, :bias_size],
+        own[0, bias_size : 2 * bias_size],
+        grad_w_up,
+        own[1],
+        grad_w_down.T,
+        own[row : row + gain_rows].reshape(ln_gains.shape),
+        own[row + gain_rows : loss_row].reshape(ln_shifts.shape),
+    )
+
+
 def solution(mesh):
     in_specs = (
         P("fsdp", "tp", None),
@@ -386,6 +1785,7 @@
         P(None, "fsdp"),
         P(None, "fsdp"),
     )
+    rows_plan = rows_plan_fits(mesh)
     return jax.shard_map(
-        on_device, mesh=mesh, in_specs=in_specs, out_specs=out_specs, check_vma=False
-    )
+        on_device_rows if rows_plan else on_device_heads, mesh=mesh, in_specs=in_specs, out_specs=out_specs, check_vma=False
+    )

time: 1550 us -> 513 us (0.33)
  waiting for transfers between devices: 761 us -> 86.4 us
  matrix products: 332 us -> 0 us
  Pallas kernels: 0 us -> 246 us
  blocking collectives: 211 us -> 0 us
  other arithmetic: 134 us -> 70.3 us
  local copies, waits for them, and re-layouts: 86.6 us -> 23.5 us
  starting transfers between devices: 1.38 us -> 58.8 us
    dot_general x42 -> x0, matrix products: 332 us -> none  [the longest x4 56.9 us: attention_backward(): jnp.einsum('qhd,khd->hqk', grad_part, value_all[row_index], preferred_ele...]
    pallas_call x0 -> x16, Pallas kernels: none -> 246 us  [the longest x3 46 us: attend_back(): pl.pallas_call(kernel, grid=(count,), in_specs=[padded, padded, pair, pai...]
    reduce_scatter x5 -> x0, waiting for transfers between devices: 219 us -> none  [the longest x1 74 us: on_device(): lax.psum_scatter(weight_up.astype(jnp.bfloat16), 'fsdp', scatter_dimensio...]
    unnamed x25 -> x1, waiting for transfers between devices: 192 us -> 0.02 us
    all_gather x8 -> x1, waiting for transfers between devices: 195 us -> 5.13 us  [on_device_rows(): lax.all_gather(tie(up_shard, chain_qkv.marks()), ('fsdp', 'tp'), axis=0,...]
    psum x2 -> x0, waiting for transfers between devices: 155 us -> none  [the longest x1 107 us: on_device(): lax.psum(hidden_part.astype(jnp.bfloat16), 'tp').astype(jnp.float32)]
    psum x3 -> x0, blocking collectives: 88.7 us -> none  [the longest x2 81 us: on_device(): lax.psum((jnp.sum(mask_float * differ * differ), jnp.sum(mask_float)), ('...]
    ppermute x0 -> x54, waiting for transfers between devices: none -> 81.3 us  [the longest x41 69.8 us: exchange(): lax.ppermute(values, 'fsdp', [(at, at ^ move[0]) for at in range(lax.axis...]
  transfers between devices with their start and end apart: 20 -> 55, of which waited for: 16 -> 20; matrix products, arithmetic and copies ran while one was open for 16% -> 14% of each run, Pallas kernels for 0% -> 40%
where the time goes in v3:
time: 513 us; the launch traced here: 505 us
  Pallas kernels  246 us (48%)
  waiting for transfers between devices  86.4 us (17%)
  other arithmetic  70.3 us (14%)
  starting transfers between devices  58.8 us (11%)
  local copies, waits for them, and re-layouts  23.5 us (5%)
  between operations  19.6 us (4%)
    ppermute x41, waiting for transfers between devices, exchange(): lax.ppermute(values, 'fsdp', [(at, at ^ move[0]) for at in range(lax.axis...  69.8 us
    pallas_call x3, Pallas kernels, attend_back(): pl.pallas_call(kernel, grid=(count,), in_specs=[padded, padded, pair, pai...  46 us
    convert_element_type x19, other arithmetic, advance(): self.total(at * self.size).astype(jnp.bfloat16)  42.3 us
    ppermute x41, starting transfers between devices, exchange(): lax.ppermute(values, 'fsdp', [(at, at ^ move[0]) for at in range(lax.axis...  40.4 us
    pallas_call x1, Pallas kernels, up_back(): pl.pallas_call(partial(up_back_kernel, places, tp_places, each), grid_spe...  38.3 us
    pallas_call x2, Pallas kernels, attend(): pl.pallas_call(kernel, grid=(count,), in_specs=[pl.BlockSpec((length, 1),...  28.5 us
    pallas_call x1, Pallas kernels, out_up_project(): pl.pallas_call(out_up_kernel, grid=(hidden_units // block_width,), in_spe...  25.7 us
    pallas_call x1, Pallas kernels, down_project(): pl.pallas_call(partial(down_kernel, places), grid=(length // BLOCK,), in_...  22 us
  transfers between devices with their start and end apart: 55, of which 20 were waited for; matrix products, arithmetic and copies ran while one was open for 14% of the time, Pallas kernels for 40%

profile of v3, /device:TPU:0, one launch (start us, length us, event | category | flops | bytes accessed | tf_op | source)
XLA Modules:
  0.0 504.6 jit_solution(3829579131555580168)
XLA Ops:
  18.2 9.5 %collective-permute-done.1 = bf16[1,64,768]{2,1,0:T(8,128)(2,1)S(1)} collective-permute-done((bf16[1,64,768]{2,1,0:T(8,128)(2,1)}, bf16[1,64,768]{2,1,0:T(8,128)(2,1)S(1)}, u32[]{:S(2)}, u32[]{:S(2)}) %collective-permute-start.1) | collective-permute-done | bytes 98336 | tf_op jit(solution)/shard_map/ppermute | solution.py:378
  30.9 5.9 %collective-permute-done.4 = bf16[512,1024]{1,0:T(8,128)(2,1)S(1)} collective-permute-done((bf16[512,1024]{1,0:T(8,128)(2,1)}, bf16[512,1024]{1,0:T(8,128)(2,1)S(1)}, u32[]{:S(2)}, u32[]{:S(2)}) %collective-permute-start.4) | collective-permute-done | bytes 1048608 | tf_op jit(solution)/shard_map/ppermute | solution.py:381
  43.7 8.2 %collective-permute-done.6 = bf16[4,64,768]{2,1,0:T(8,128)(2,1)S(1)} collective-permute-done((bf16[4,64,768]{2,1,0:T(8,128)(2,1)S(1)}, bf16[4,64,768]{2,1,0:T(8,128)(2,1)S(1)}, u32[]{:S(2)}, u32[]{:S(2)}) %collective-permute-start.6) | collective-permute-done | bytes 393248 | tf_op jit(solution)/shard_map/ppermute | solution.py:378
  55.4 19.9 %collective-permute-done.7.refs_1_ = bf16[8,64,896]{2,1,0:T(8,128)(2,1)S(1)} collective-permute-done((bf16[8,64,896]{2,1,0:T(8,128)(2,1)S(1)}, bf16[8,64,896]{2,1,0:T(8,128)(2,1)S(1)}, u32[]{:S(2)}, u32[]{:S(2)}) %collective-permute-start.7) | collective-permute-done | bytes 917536 | tf_op jit(solution)/shard_map/ppermute | solution.py:378
  83.2 16.0 %qkv_project.1 = (bf16[1024,1024]{1,0:T(8,128)(2,1)}, bf16[1024,1024]{1,0:T(8,128)(2,1)}, bf16[1024,1024]{1,0:T(8,128)(2,1)}, bf16[1024,3072]{1,0:T(8,128)(2,1)}, bf16[32,32,128]{2,1,0:T(8,128)(2,1)}) custom-call(s32[2]{0:T(128)} %pad_add_fusion.place_ref, bf16[1024,1024]{1,0:T(8,128)(2,1)} %pad_maximum_fusion.row_ref.refs_1_.refs_0_, ...), custom_call_target="tpu_custom_call" | custom-call | flops 805306368 | bytes 3145728 | tf_op jit(solution)/shard_map/qkv_project/pallas_call | solution.py:890
  99.2 4.3 collective-permute-done.14
  111.6 14.2 %attend.2 = (bf16[1024,1024]{1,0:T(8,128)(2,1)}, bf16[16,1024,128]{2,1,0:T(8,128)(2,1)}, bf16[16,1024,128]{2,1,0:T(8,128)(2,1)}) custom-call(s32[1024,1]{1,0:T(8,128)} %copy.40.seg_ref, bf16[1024,1024]{1,0:T(8,128)(2,1)} %get-tuple-element.285.q_ref, bf16[1024,1024]{1,0:T(8,128)(2,1)} %get-tuple-element.286.k_ref, bf16[1024,1024]{1,0:T(8,128)(2,1)} %get-tuple-element.295.v_ref), custom_call_target="tpu_custom_call" | custom-call | flops 1750000000 | bytes 1048576 | tf_op jit(solution)/shard_map/attend/pallas_call | solution.py:641
  128.7 14.3 %attend.3 = (bf16[1024,1024]{1,0:T(8,128)(2,1)}, bf16[16,1024,128]{2,1,0:T(8,128)(2,1)}, bf16[16,1024,128]{2,1,0:T(8,128)(2,1)}) custom-call(s32[1024,1]{1,0:T(8,128)} %copy.40.seg_ref, bf16[1024,1024]{1,0:T(8,128)(2,1)} %get-tuple-element.285.q_ref, ...), custom_call_target="tpu_custom_call", output_to_operand_aliasing={{0}: (4, {}), {1}: (5, {}), {2}: (6, {})} | custom-call | flops 1750000000 | bytes 1048576 | tf_op jit(solution)/shard_map/attend/pallas_call | solution.py:641
  151.6 5.1 %all-gather.3.cloned.1.call-done = bf16[2048,2560]{1,0:T(8,128)(2,1)} async-done(((bf16[64,2560]{1,0:T(8,128)(2,1)}), bf16[2048,2560]{1,0:T(8,128)(2,1)}) %all-gather.3.cloned.1.call-update) | async-done | bytes 10485776 | tf_op jit(solution)/shard_map/all_gather | solution.py:1511
  156.8 25.7 %out_up_project.1 = (bf16[1024,4096]{1,0:T(8,128)(2,1)}, bf16[1024,4096]{1,0:T(8,128)(2,1)}, f32[1024,1024]{1,0:T(8,128)}, f32[1024,1]{1,0:T(8,128)}, bf16[1024,...) custom-call(bf16[1024,1024]{1,0:T(8,128)(2,1)} %get-tuple-element.301.mixed_ref.out_ref.refs_2_, ...), custom_call_target="tpu_custom_call" | custom-call | flops 1342177280 | bytes 4718592 | tf_op jit(solution)/shard_map/out_up_project/pallas_call | solution.py:966
  190.6 22.0 %down_project.1 = (bf16[1024,1024]{1,0:T(8,128)(2,1)}, f32[1024,1024]{1,0:T(8,128)}, bf16[1024,1024]{1,0:T(8,128)(2,1)}, f32[8,1024]{1,0:T(8,128)}, bf16[1024,4096]{1,0:T(8,128)(2,1)}) custom-call(s32[2]{0:T(128)} %pad_add_fusion.place_ref, bf16[1024,4096]{1,0:T(8,128)(2,1)} %get-tuple-element.305.active_ref, f32[1024,1024]{1,0:T(8,128)} %get-tuple-element.306.unit_ref, ...), custom_call_target="tpu_custom_call" | custom-call | flops 1073741824 | bytes 4718592 | tf_op jit(solution)/shard_map/down_project/pallas_call | solution.py:1066
  212.6 17.9 %down_back.1 = (bf16[16,64,2048]{2,1,0:T(8,128)(2,1)}, bf16[16,64,2048]{2,1,0:T(8,128)(2,1)}) custom-call(s32[2]{0:T(128)} %pad_add_fusion.place_ref, bf16[1024,1024]{1,0:T(8,128)(2,1)} %get-tuple-element.314.grad_ref, bf16[1024,4096]{1,0:T(8,128)(2,1)} %get-tuple-element.305.active_ref), custom_call_target="tpu_custom_call" | custom-call | flops 1073741824 | bytes 2621440 | tf_op jit(solution)/shard_map/down_back/pallas_call | solution.py:1206
  230.9 38.3 %up_back.1 = (f32[1024,1024]{1,0:T(8,128)}, f32[1,4096]{1,0:T(1,128)}, bf16[16,64,2048]{2,1,0:T(8,128)(2,1)}, bf16[16,64,2048]{2,1,0:T(8,128)(2,1)}) custom-call(s32[2]{0:T(128)} %pad_add_fusion.place_ref, bf16[1024,1024]{1,0:T(8,128)(2,1)} %get-tuple-element.314.grad_ref, bf16[1024,1024]{1,0:T(8,128)(2,1)} %get-tuple-element.315.hidden_ref, ...), custom_call_target="tpu_custom_call" | custom-call | flops 3221225472 | bytes 5242880 | tf_op jit(solution)/shard_map/up_back/pallas_call | solution.py:1232
  277.5 10.9 %norm_back.1 = (f32[1024,1024]{1,0:T(8,128)}, bf16[1024,1024]{1,0:T(8,128)(2,1)}, bf16[1024,1024]{1,0:T(8,128)(2,1)}, f32[8,1024]{1,0:T(8,128)}) custom-call(f32[1024,1024]{1,0:T(8,128)} %get-tuple-element.311.base_ref, f32[1024,1024]{1,0:T(8,128)} %get-tuple-element.323.grad_ref, f32[1024,1024]{1,0:T(8,128)} %get-tuple-element.306.unit_ref, ...), custom_call_target="tpu_custom_call" | custom-call | flops 268435456 | bytes 2883584 | tf_op jit(solution)/shard_map/norm_back/pallas_call | solution.py:1287
  288.4 4.0 add_convert_fusion
  296.2 16.9 %attend_back.3 = (bf16[1024,768]{1,0:T(8,128)(2,1)}, bf16[1024,768]{1,0:T(8,128)(2,1)}, bf16[1024,768]{1,0:T(8,128)(2,1)}) custom-call(bf16[16,1024,128]{2,1,0:T(8,128)(2,1)} %get-tuple-element.333.qx_ref, bf16[16,1024,128]{2,1,0:T(8,128)(2,1)} %get-tuple-element.334.kx_ref, bf16[1024,1024]{1,0:T(8,128)(2,1)} %get-tuple-element.295.v_ref, ...), custom_call_target="tpu_custom_call" | custom-call | flops 1875000064 | bytes 786432 | tf_op jit(solution)/shard_map/attend_back/pallas_call | solution.py:730
  313.1 17.0 %attend_back.4 = (bf16[1024,768]{1,0:T(8,128)(2,1)}, bf16[1024,768]{1,0:T(8,128)(2,1)}, bf16[1024,768]{1,0:T(8,128)(2,1)}) custom-call(bf16[16,1024,128]{2,1,0:T(8,128)(2,1)} %get-tuple-element.333.qx_ref, bf16[16,1024,128]{2,1,0:T(8,128)(2,1)} %get-tuple-element.334.kx_ref, ...), custom_call_target="tpu_custom_call", output_to_operand_aliasing={{0}: (5, {}), {1}: (6, {}), {2}: (7, {})} | custom-call | flops 1875000064 | bytes 786432 | tf_op jit(solution)/shard_map/attend_back/pallas_call | solution.py:730
  334.4 14.1 %weight_grads.2 = (bf16[16,64,896]{2,1,0:T(8,128)(2,1)}, bf16[16,64,896]{2,1,0:T(8,128)(2,1)}, bf16[16,64,768]{2,1,0:T(8,128)(2,1)}, bf16[16,64,768]{2,1,0:T(8,128)(2,1)}) custom-call(s32[2]{0:T(128)} %pad_add_fusion.place_ref, bf16[1024,1024]{1,0:T(8,128)(2,1)} %get-tuple-element.332.refs_0_, bf16[1024,1024]{1,0:T(8,128)(2,1)} %pad_maximum_fusion.row_ref.refs_1_.refs_0_, ...), custom_call_target="tpu_custom_call" | custom-call | flops 872415232 | bytes 2097152 | tf_op jit(solution)/shard_map/weight_grads/pallas_call | solution.py:1366
  362.7 12.1 %attend_back.5 = (bf16[1024,256]{1,0:T(8,128)(2,1)}, bf16[1024,256]{1,0:T(8,128)(2,1)}, bf16[1024,256]{1,0:T(8,128)(2,1)}) custom-call(bf16[16,1024,128]{2,1,0:T(8,128)(2,1)} %get-tuple-element.333.qx_ref, bf16[16,1024,128]{2,1,0:T(8,128)(2,1)} %get-tuple-element.334.kx_ref, bf16[1024,1024]{1,0:T(8,128)(2,1)} %get-tuple-element.295.v_ref, ...), custom_call_target="tpu_custom_call" | custom-call | flops 1250000000 | bytes 524288 | tf_op jit(solution)/shard_map/attend_back/pallas_call | solution.py:730
  391.5 5.9 %weight_grads.3 = (bf16[16,64,512]{2,1,0:T(8,128)(2,1)}, bf16[16,64,512]{2,1,0:T(8,128)(2,1)}) custom-call(s32[2]{0:T(128)} %pad_add_fusion.place_ref, bf16[1024,1024]{1,0:T(8,128)(2,1)} %pad_maximum_fusion.row_ref.refs_1_.refs_0_, bf16[1024,256]{1,0:T(8,128)(2,1)} %get-tuple-element.358.refs_1_, bf16[1024,256]{1,0:T(8,128)(2,1)} %get-tuple-element.359.refs_2_.refs_3_, ...), custom_call_target="tpu_custom_call" | custom-call | flops 201326592 | bytes 2097152 | tf_op jit(solution)/shard_map/weight_grads/pallas_call | solution.py:1366
  403.0 9.2 %input_grad.2 = bf16[512,1024]{1,0:T(8,128)(2,1)} custom-call(s32[2]{0:T(128)} %pad_add_fusion.place_ref, f32[1024,1024]{1,0:T(8,128)} %get-tuple-element.411.base_ref, bf16[1024,768]{1,0:T(8,128)(2,1)} %get-tuple-element.339.refs_3_.refs_0_, bf16[1024,256]{1,0:T(8,128)(2,1)} %get-tuple-element.358.refs_1_, ...), custom_call_target="tpu_custom_call" | custom-call | flops 402653184 | bytes 1835008 | tf_op jit(solution)/shard_map/input_grad/pallas_call | solution.py:1398
  414.0 9.3 %collective-permute-done.39 = bf16[8,64,768]{2,1,0:T(8,128)(2,1)} collective-permute-done((bf16[8,64,768]{2,1,0:T(8,128)(2,1)}, bf16[8,64,768]{2,1,0:T(8,128)(2,1)}, u32[]{:S(2)}, u32[]{:S(2)}) %collective-permute-start.39) | collective-permute-done | bytes 786464 | tf_op jit(solution)/shard_map/ppermute | solution.py:378
  432.6 9.5 %input_grad.3 = bf16[512,1024]{1,0:T(8,128)(2,1)} custom-call(s32[2]{0:T(128)} %pad_add_fusion.place_ref, f32[1024,1024]{1,0:T(8,128)} %get-tuple-element.411.base_ref, bf16[1024,768]{1,0:T(8,128)(2,1)} %get-tuple-element.339.refs_3_.refs_0_, bf16[1024,256]{1,0:T(8,128)(2,1)} %get-tuple-element.358.refs_1_, ...), custom_call_target="tpu_custom_call" | custom-call | flops 402653184 | bytes 1835008 | tf_op jit(solution)/shard_map/input_grad/pallas_call | solution.py:1398
  451.7 4.7 collective-permute-done.52
  (298 shorter events, 170.2 us)
Async XLA Ops:
  7.2 149.6 %all-gather.3.cloned.1.call-start = ((), (), s32[]{:S(2)}) async-start(), calls=%async_computation | async-start | bytes 10813440 | tf_op jit(solution)/shard_map/all_gather | solution.py:1511
  9.7 27.1 %collective-permute-start.4 = (bf16[512,1024]{1,0:T(8,128)(2,1)}, bf16[512,1024]{1,0:T(8,128)(2,1)S(1)}, u32[]{:S(2)}, u32[]{:S(2)}) collective-permute-start(bf16[512,1024]{1,0:T(8,128)(2,1)} %dynamic-slice_bitcast_fusion.1), channel_id=1, source_target_pairs={{0,1},{1,0},{2,3},{3,2},{4,5},{5,4},{6,7},{7,6},{8,9},{9,8},{10,11... | collective-permute-start | bytes 3145736 | tf_op jit(solution)/shard_map/ppermute | solution.py:381
  55.4 25.7 %collective-permute-start.9 = (bf16[8,64,896]{2,1,0:T(8,128)(2,1)S(1)}, bf16[8,64,896]{2,1,0:T(8,128)(2,1)S(1)}, u32[]{:S(2)}, u32[]{:S(2)}) collective-permute-start(bf16[8,64,896]{2,1,0:T(8,128)(2,1)S(1)} %constant_dynamic-update-slice_fusion.8.refs_0_), channel_id=1, source_target_pairs={{0,2},{2,0},{4,6},{6,4},{8,10},{10,8},{12,14},{14,12},{16,18},{18,... | collective-permute-start | bytes 2752520 | tf_op jit(solution)/shard_map/ppermute | solution.py:378
  145.6 36.9 %collective-permute-start.21 = (bf16[8,64,1024]{2,1,0:T(8,128)(2,1)S(1)}, bf16[8,64,1024]{2,1,0:T(8,128)(2,1)S(1)}, u32[]{:S(2)}, u32[]{:S(2)}) collective-permute-start(bf16[8,64,1024]{2,1,0:T(8,128)(2,1)S(1)} %constant_dynamic-update-slice_fusion.22.refs_4_), channel_id=1, source_target_pairs={{0,8},{2,10},{4,12},{6,14},{8,0},{10,2},{12,4},{14,6},{16,24},{18,... | collective-permute-start | bytes 3145736 | tf_op jit(solution)/shard_map/ppermute | solution.py:378
  147.2 35.3 %collective-permute-start.20 = (bf16[8,64,1024]{2,1,0:T(8,128)(2,1)S(1)}, bf16[8,64,1024]{2,1,0:T(8,128)(2,1)}, u32[]{:S(2)}, u32[]{:S(2)}) collective-permute-start(bf16[8,64,1024]{2,1,0:T(8,128)(2,1)S(1)} %constant_dynamic-update-slice_fusion.20.refs_0_), channel_id=1, source_target_pairs={{0,4},{2,6},{4,0},{6,2},{8,12},{10,14},{12,8},{14,10},{16,20},{18,... | collective-permute-start | bytes 3145736 | tf_op jit(solution)/shard_map/ppermute | solution.py:378
  149.5 37.9 %collective-permute-start.19 = (bf16[512,1024]{1,0:T(8,128)(2,1)}, bf16[512,1024]{1,0:T(8,128)(2,1)}, u32[]{:S(2)}, u32[]{:S(2)}) collective-permute-start(bf16[512,1024]{1,0:T(8,128)(2,1)} %dynamic-slice_bitcast_fusion), channel_id=1, source_target_pairs={{0,1},{1,0},{2,3},{3,2},{4,5},{5,4},{6,7},{7,6},{8,9},{9,8},{10,11... | collective-permute-start | bytes 3145736 | tf_op jit(solution)/shard_map/ppermute | solution.py:381
  151.1 39.5 %collective-permute-start.24 = (bf16[8,64,1024]{2,1,0:T(8,128)(2,1)S(1)}, bf16[8,64,1024]{2,1,0:T(8,128)(2,1)}, u32[]{:S(2)}, u32[]{:S(2)}) collective-permute-start(bf16[8,64,1024]{2,1,0:T(8,128)(2,1)S(1)} %constant_dynamic-update-slice_fusion.22.refs_4_), channel_id=1, source_target_pairs={{0,2},{2,0},{4,6},{6,4},{8,10},{10,8},{12,14},{14,12},{16,18},{18,... | collective-permute-start | bytes 3145736 | tf_op jit(solution)/shard_map/ppermute | solution.py:378
  151.1 39.5 %collective-permute-start.22 = (bf16[8,64,1024]{2,1,0:T(8,128)(2,1)S(1)}, bf16[8,64,1024]{2,1,0:T(8,128)(2,1)}, u32[]{:S(2)}, u32[]{:S(2)}) collective-permute-start(bf16[8,64,1024]{2,1,0:T(8,128)(2,1)S(1)} %constant_dynamic-update-slice_fusion.20.refs_0_), channel_id=1, source_target_pairs={{0,2},{2,0},{4,6},{6,4},{8,10},{10,8},{12,14},{14,12},{16,18},{18,... | collective-permute-start | bytes 3145736 | tf_op jit(solution)/shard_map/ppermute | solution.py:378
  230.5 39.0 %collective-permute-start.26 = (bf16[16,64,2048]{2,1,0:T(8,128)(2,1)}, bf16[16,64,2048]{2,1,0:T(8,128)(2,1)}, u32[]{:S(2)}, u32[]{:S(2)}) collective-permute-start(bf16[16,64,2048]{2,1,0:T(8,128)(2,1)} %get-tuple-element.313), channel_id=1, source_target_pairs={{0,2},{2,0},{4,6},{6,4},{8,10},{10,8},{12,14},{14,12},{16,18},{18,... | collective-permute-start | bytes 12582920 | tf_op jit(solution)/shard_map/ppermute | solution.py:378
  273.3 56.8 %collective-permute-start.30 = (bf16[8,64,2048]{2,1,0:T(8,128)(2,1)}, bf16[8,64,2048]{2,1,0:T(8,128)(2,1)}, u32[]{:S(2)}, u32[]{:S(2)}) collective-permute-start(bf16[8,64,2048]{2,1,0:T(8,128)(2,1)} %add_convert_fusion.1), channel_id=1, source_target_pairs={{0,1},{1,0},{2,3},{3,2},{4,5},{5,4},{6,7},{7,6},{8,9},{9,8},{10,11... | collective-permute-start | bytes 6291464 | tf_op jit(solution)/shard_map/ppermute | solution.py:381
  292.5 57.9 %collective-permute-start.29 = (bf16[8,64,2048]{2,1,0:T(8,128)(2,1)}, bf16[8,64,2048]{2,1,0:T(8,128)(2,1)}, u32[]{:S(2)}, u32[]{:S(2)}) collective-permute-start(bf16[8,64,2048]{2,1,0:T(8,128)(2,1)} %add_convert_fusion), channel_id=1, source_target_pairs={{0,8},{2,10},{4,12},{6,14},{8,0},{10,2},{12,4},{14,6},{16,24},{18,... | collective-permute-start | bytes 6291464 | tf_op jit(solution)/shard_map/ppermute | solution.py:378
  333.7 25.1 %collective-permute-start.32 = (bf16[4,64,2048]{2,1,0:T(8,128)(2,1)}, bf16[4,64,2048]{2,1,0:T(8,128)(2,1)}, u32[]{:S(2)}, u32[]{:S(2)}) collective-permute-start(bf16[4,64,2048]{2,1,0:T(8,128)(2,1)} %add_convert_fusion.3), channel_id=1, source_target_pairs={{0,4},{2,6},{4,0},{6,2},{8,12},{10,14},{12,8},{14,10},{16,20},{18,... | collective-permute-start | bytes 3145736 | tf_op jit(solution)/shard_map/ppermute | solution.py:378
  334.3 27.4 %collective-permute-start.27 = (bf16[512,1024]{1,0:T(8,128)(2,1)}, bf16[512,1024]{1,0:T(8,128)(2,1)S(1)}, u32[]{:S(2)}, u32[]{:S(2)}) collective-permute-start(bf16[512,1024]{1,0:T(8,128)(2,1)} %constant_dynamic-slice_fusion), channel_id=1, source_target_pairs={{0,1},{1,0},{2,3},{3,2},{4,5},{5,4},{6,7},{7,6},{8,9},{9,8},{10,11... | collective-permute-start | bytes 3145736 | tf_op jit(solution)/shard_map/ppermute | solution.py:381
  348.5 33.4 %collective-permute-start.34 = (bf16[16,64,896]{2,1,0:T(8,128)(2,1)}, bf16[16,64,896]{2,1,0:T(8,128)(2,1)}, u32[]{:S(2)}, u32[]{:S(2)}) collective-permute-start(bf16[16,64,896]{2,1,0:T(8,128)(2,1)} %get-tuple-element.347), channel_id=1, source_target_pairs={{0,2},{2,0},{4,6},{6,4},{8,10},{10,8},{12,14},{14,12},{16,18},{18,... | collective-permute-start | bytes 5505032 | tf_op jit(solution)/shard_map/ppermute | solution.py:378
  349.8 32.2 %collective-permute-start.35 = (bf16[16,64,768]{2,1,0:T(8,128)(2,1)}, bf16[16,64,768]{2,1,0:T(8,128)(2,1)}, u32[]{:S(2)}, u32[]{:S(2)}) collective-permute-start(bf16[16,64,768]{2,1,0:T(8,128)(2,1)} %get-tuple-element.349), channel_id=1, source_target_pairs={{0,2},{2,0},{4,6},{6,4},{8,10},{10,8},{12,14},{14,12},{16,18},{18,... | collective-permute-start | bytes 4718600 | tf_op jit(solution)/shard_map/ppermute | solution.py:378
  353.8 28.2 %collective-permute-start.31 = (bf16[4,64,2048]{2,1,0:T(8,128)(2,1)}, bf16[4,64,2048]{2,1,0:T(8,128)(2,1)}, u32[]{:S(2)}, u32[]{:S(2)}) collective-permute-start(bf16[4,64,2048]{2,1,0:T(8,128)(2,1)} %add_convert_fusion.2), channel_id=1, source_target_pairs={{0,1},{1,0},{2,3},{3,2},{4,5},{5,4},{6,7},{7,6},{8,9},{9,8},{10,11... | collective-permute-start | bytes 3145736 | tf_op jit(solution)/shard_map/ppermute | solution.py:381
  397.4 26.0 %collective-permute-start.36 = (bf16[16,64,512]{2,1,0:T(8,128)(2,1)}, bf16[16,64,512]{2,1,0:T(8,128)(2,1)}, u32[]{:S(2)}, u32[]{:S(2)}) collective-permute-start(bf16[16,64,512]{2,1,0:T(8,128)(2,1)} %get-tuple-element.392), channel_id=1, source_target_pairs={{0,2},{2,0},{4,6},{6,4},{8,10},{10,8},{12,14},{14,12},{16,18},{18,... | collective-permute-start | bytes 3145736 | tf_op jit(solution)/shard_map/ppermute | solution.py:378
  397.5 25.9 %collective-permute-start.38 = (bf16[8,64,896]{2,1,0:T(8,128)(2,1)}, bf16[8,64,896]{2,1,0:T(8,128)(2,1)}, u32[]{:S(2)}, u32[]{:S(2)}) collective-permute-start(bf16[8,64,896]{2,1,0:T(8,128)(2,1)} %add_convert_fusion.4), channel_id=1, source_target_pairs={{0,1},{1,0},{2,3},{3,2},{4,5},{5,4},{6,7},{7,6},{8,9},{9,8},{10,11... | collective-permute-start | bytes 2752520 | tf_op jit(solution)/shard_map/ppermute | solution.py:381
  397.8 25.5 %collective-permute-start.39 = (bf16[8,64,768]{2,1,0:T(8,128)(2,1)}, bf16[8,64,768]{2,1,0:T(8,128)(2,1)}, u32[]{:S(2)}, u32[]{:S(2)}) collective-permute-start(bf16[8,64,768]{2,1,0:T(8,128)(2,1)} %add_convert_fusion.5), channel_id=1, source_target_pairs={{0,8},{2,10},{4,12},{6,14},{8,0},{10,2},{12,4},{14,6},{16,24},{18,... | collective-permute-start | bytes 2359304 | tf_op jit(solution)/shard_map/ppermute | solution.py:378
  400.5 41.6 %collective-permute-start.53 = (bf16[1,64,2048]{2,1,0:T(8,128)(2,1)}, bf16[1,64,2048]{2,1,0:T(8,128)(2,1)}, u32[]{:S(2)}, u32[]{:S(2)}) collective-permute-start(bf16[1,64,2048]{2,1,0:T(8,128)(2,1)} %add_convert_fusion.13), channel_id=1, source_target_pairs={{0,16},{2,18},{4,20},{6,22},{8,24},{10,26},{12,28},{14,30},{16,0},... | collective-permute-start | bytes 786440 | tf_op jit(solution)/shard_map/ppermute | solution.py:378
  412.2 34.0 %collective-permute-start.49 = (bf16[512,1024]{1,0:T(8,128)(2,1)}, bf16[512,1024]{1,0:T(8,128)(2,1)S(1)}, u32[]{:S(2)}, u32[]{:S(2)}) collective-permute-start(bf16[512,1024]{1,0:T(8,128)(2,1)} %input_grad.2), channel_id=1, source_target_pairs={{0,1},{1,0},{2,3},{3,2},{4,5},{5,4},{6,7},{7,6},{8,9},{9,8},{10,11... | collective-permute-start | bytes 3145736 | tf_op jit(solution)/shard_map/ppermute | solution.py:381
  425.4 31.0 %collective-permute-start.42 = (bf16[4,64,768]{2,1,0:T(8,128)(2,1)}, bf16[4,64,768]{2,1,0:T(8,128)(2,1)}, u32[]{:S(2)}, u32[]{:S(2)}) collective-permute-start(bf16[4,64,768]{2,1,0:T(8,128)(2,1)} %add_convert_fusion.10), channel_id=1, source_target_pairs={{0,4},{2,6},{4,0},{6,2},{8,12},{10,14},{12,8},{14,10},{16,20},{18,... | collective-permute-start | bytes 1179656 | tf_op jit(solution)/shard_map/ppermute | solution.py:378
  429.3 27.1 %collective-permute-start.41 = (bf16[4,64,896]{2,1,0:T(8,128)(2,1)}, bf16[4,64,896]{2,1,0:T(8,128)(2,1)}, u32[]{:S(2)}, u32[]{:S(2)}) collective-permute-start(bf16[4,64,896]{2,1,0:T(8,128)(2,1)} %add_convert_fusion.9), channel_id=1, source_target_pairs={{0,4},{2,6},{4,0},{6,2},{8,12},{10,14},{12,8},{14,10},{16,20},{18,... | collective-permute-start | bytes 1376264 | tf_op jit(solution)/shard_map/ppermute | solution.py:378
  430.8 26.4 %collective-permute-start.40 = (bf16[8,64,512]{2,1,0:T(8,128)(2,1)S(1)}, bf16[8,64,512]{2,1,0:T(8,128)(2,1)}, u32[]{:S(2)}, u32[]{:S(2)}) collective-permute-start(bf16[8,64,512]{2,1,0:T(8,128)(2,1)S(1)} %add_convert_fusion.6), channel_id=1, source_target_pairs={{0,4},{2,6},{4,0},{6,2},{8,12},{10,14},{12,8},{14,10},{16,20},{18,... | collective-permute-start | bytes 1572872 | tf_op jit(solution)/shard_map/ppermute | solution.py:378
  (68 other events, 990.0 us)
Sparse Core Ops, SparseCore 0:
  52.4 104.3 all-gather.2

commit v4 on v3

--- a/solution.py
+++ b/solution.py
@@ -402,6 +402,7 @@
         return ((SIDE,), (ACROSS,), tuple(reversed(far)))
     moves = {
         "across": [ACROSS, SIDE] + far,
+        "side": [SIDE, ACROSS] + far,
         "far": far[:1] + [ACROSS, SIDE] + far[1:],
         "far_side": far[:1] + [SIDE] + far[1:] + [ACROSS],
     }[kind]
@@ -531,7 +532,7 @@
 
 
 def cost(flops, moved, transcendentals=0):
-    return pl.CostEstimate(flops=flops // 8, bytes_accessed=moved // 8, transcendentals=0)
+    return pl.CostEstimate(flops=flops // 2000, bytes_accessed=moved // 2000, transcendentals=0)
 
 
 def low_shape(*shape):
@@ -801,8 +802,8 @@
         low_shape(rows, width + width // 2 + 128),
         low_shape(rows, width // 2 + width),
         low_shape(rows, hidden + width),
-        low_shape(rows, hidden // 2),
-        low_shape(rows, hidden // 2),
+        low_shape(rows, hidden // 2 + 128),
+        low_shape(rows, hidden // 2 - 128),
     ]
     return pl.pallas_call(
         shards_kernel,
@@ -1001,41 +1002,62 @@
     )(mixed, row_low, gathered, gathered, vectors, bias)
 
 
+def piece_lanes(place_ref, sources, group):
+    part, low = group
+    widths = [sources[0].shape[2], sources[4].shape[2]]
+    return (place_ref[1] ^ low) * sum(widths) + sum(widths[:part]), widths[part]
+
+
+def piece_copies(places, place_ref, sources, held, sems, group):
+    rows = sources[0].shape[1]
+    found = []
+    for at, (part, source, place, high, low) in enumerate(places):
+        if (part, low) != group:
+            continue
+        row = pl.multiple_of((place_ref[0] ^ high) * rows, rows)
+        lane, part_width = piece_lanes(place_ref, sources, group)
+        found.append(
+            pltpu.make_async_copy(
+                sources[source].at[place],
+                held.at[pl.ds(row, rows), pl.ds(pl.multiple_of(lane, 128), part_width)],
+                sems.at[at],
+            )
+        )
+    return found
+
+
+PIECE_GROUPS = [(part, low) for low in range(2) for part in range(2)]
+
+
 def down_kernel(
     places, place_ref, active_ref, unit_ref, teacher_ref, weight_ref, vector_ref, *refs
 ):
     count = 1 + max(source for _, source, _, _, _ in places)
     sources = refs[:count]
-    out_ref, grad_ref, low_ref, sums_ref, full_ref, held, sems, out_sem = refs[count:]
-    rows = sources[0].shape[1]
-    part_width = sources[0].shape[2]
+    out_ref, grad_ref, low_ref, sums_ref, held, sems = refs[count:]
     step = pl.program_id(0)
-    last = pl.num_programs(0) - 1
-    full_copy = pltpu.make_async_copy(held, full_ref, out_sem)
+    copies = partial(piece_copies, places, place_ref, sources, held, sems)
 
     @pl.when(step == 0)
     def _():
-        me_fsdp, me_tp = (place_ref[0], place_ref[1])
-        copies = []
-        for at, (part, source, place, high, low) in enumerate(places):
-            row = pl.multiple_of((me_fsdp ^ high) * rows, rows)
-            lane = (me_tp ^ low) * (2 * part_width) + part * part_width
-            lane = pl.multiple_of(lane, 128)
-            copies.append(
-                pltpu.make_async_copy(
-                    sources[source].at[place],
-                    held.at[pl.ds(row, rows), pl.ds(lane, part_width)],
-                    sems.at[at],
-                )
-            )
-            copies[-1].start()
-        for copy in copies:
-            copy.wait()
-        full_copy.start()
+        for group in PIECE_GROUPS:
+            for copy in copies(group):
+                copy.start()
         sums_ref[...] = jnp.zeros_like(sums_ref)
 
     normed_first = unit_ref[...] * vector_ref[0:1] + vector_ref[1:2]
-    before = normed_first + dot_last(active_ref[...], held[...]) + vector_ref[2:3]
+    before = normed_first + vector_ref[2:3]
+    for group in PIECE_GROUPS:
+
+        @pl.when(step == 0)
+        def _(group=group):
+            for copy in copies(group):
+                copy.wait()
+
+        lane, part_width = piece_lanes(place_ref, sources, group)
+        span = pl.ds(pl.multiple_of(lane, 128), part_width)
+        before = before + dot_last(active_ref[:, span], held[:, span])
+
     unit, inverse = unit_of(before)
     gain = vector_ref[3:4]
     result = unit * gain + vector_ref[4:5]
@@ -1053,10 +1075,6 @@
     for at, term in enumerate((grad * unit, grad, grad_before, grad * differ)):
         sums_ref[at : at + 1] += jnp.sum(term, axis=0, keepdims=True)
 
-    @pl.when(step == last)
-    def _():
-        full_copy.wait()
-
 
 def down_project(chain, place, active, unit, teacher, weight, vectors):
     length, hidden_units = active.shape
@@ -1069,18 +1087,16 @@
         in_specs=[SCALARS, line(hidden_units), line(features), line(features), line(1)]
         + [whole(*vectors.shape)]
         + [ANYWHERE] * len(sources),
-        out_specs=[line(features), line(features), line(features), whole(8, features), ANYWHERE],
+        out_specs=[line(features), line(features), line(features), whole(8, features)],
         out_shape=[
             low_shape(length, features),
             wide_shape(length, features),
             low_shape(length, features),
             wide_shape(8, features),
-            low_shape(features, hidden_units),
         ],
         scratch_shapes=[
             pltpu.VMEM((features, hidden_units), jnp.bfloat16),
             pltpu.SemaphoreType.DMA((len(places),)),
-            pltpu.SemaphoreType.DMA,
         ],
         compiler_params=pltpu.CompilerParams(vmem_limit_bytes=VMEM_LIMIT),
         cost_estimate=cost(2 * length * features * hidden_units, 36 << 20),
@@ -1132,23 +1148,38 @@
 
 
 def up_back_kernel(
-    places, tp_places, each, place_ref, grad_ref, hidden_ref, slope_ref, down_ref, up_ref,
-    total_ref, bias_ref, kept_ref, sent_ref, turned, held, sems,
+    places, tp_places, each, down_places, place_ref, grad_ref, hidden_ref, slope_ref, up_ref, *refs
 ):
+    count = 1 + max(source for _, source, _, _, _ in down_places)
+    sources = refs[:count]
+    total_ref, bias_ref, kept_ref, sent_ref, turned, held, sems, down_held, down_sems = refs[count:]
     step = pl.program_id(0)
+    down_copies = partial(piece_copies, down_places, place_ref, sources, down_held, down_sems)
     length, features = grad_ref.shape
     block_width = slope_ref.shape[1]
 
     @pl.when(step == 0)
     def _():
+        for group in PIECE_GROUPS:
+            for copy in down_copies(group):
+                copy.start()
         turned[...] = hidden_ref[...].T
         total_ref[...] = jnp.zeros_like(total_ref)
+
+    for at, group in enumerate(PIECE_GROUPS):
+
+        @pl.when(step == at * (each // 2))
+        def _(group=group):
+            for copy in down_copies(group):
+                copy.wait()
 
     copies = partial(
         column_copies, places, tp_places, each, block_width, place_ref[0], held,
         (kept_ref, sent_ref), sems,
     )
-    down_weight = down_ref[...]
+    column = (place_ref[1] ^ (step // each)) * each + step % each
+    lane = pl.multiple_of(column * block_width, block_width)
+    down_weight = down_held[:, pl.ds(lane, block_width)]
     up_weight = up_ref[:, 0].reshape(features, block_width)
     spans = [slice(at * BLOCK, (at + 1) * BLOCK) for at in range(length // BLOCK)]
     grads, bias = ([], jnp.zeros((1, block_width), jnp.float32))
@@ -1222,15 +1253,16 @@
     )(place, grad_down, active)
 
 
-def up_back(place, grad_down, hidden, slope, full_down, gathered, kind):
+def up_back(place, grad_down, hidden, slope, chain, gathered, kind):
     length, features = hidden.shape
     fsdp_count, tp_count, rows, _ = gathered.shape
-    local_hidden = full_down.shape[1] // tp_count
+    local_hidden = slope.shape[1] // tp_count
+    sources, down_places = (chain.sources(), chain.places())
     block_width, each, places, tp_places, column = column_plan(kind, local_hidden)
     piece = low_shape(len(places) // 2, rows, local_hidden)
     block = pl.BlockSpec((length, block_width), lambda step, where: (0, column(step, where)))
     return pl.pallas_call(
-        partial(up_back_kernel, places, tp_places, each),
+        partial(up_back_kernel, places, tp_places, each, down_places),
         grid_spec=pltpu.PrefetchScalarGridSpec(
             num_scalar_prefetch=1,
             grid=(2 * each,),
@@ -1238,25 +1270,29 @@
                 keep(length, features),
                 keep(length, features),
                 block,
-                pl.BlockSpec((features, block_width), lambda step, where: (0, column(step, where))),
                 pl.BlockSpec(
                     (fsdp_count, 1, rows, block_width),
                     lambda step, where: (0, where[1] ^ (step // each), 0, step % each),
                 ),
-            ],
+            ]
+            + [ANYWHERE] * len(sources),
             out_specs=[
                 keep(length, features),
                 pl.BlockSpec((1, block_width), lambda step, where: (0, column(step, where))),
             ]
             + [ANYWHERE] * 2,
-            scratch_shapes=column_scratch(features, length, each, block_width, places),
+            scratch_shapes=column_scratch(features, length, each, block_width, places)
+            + [
+                pltpu.VMEM((features, slope.shape[1]), jnp.bfloat16),
+                pltpu.SemaphoreType.DMA((len(down_places),)),
+            ],
         ),
         out_shape=[wide_shape(length, features), wide_shape(1, local_hidden * tp_count)]
         + [piece] * 2,
         compiler_params=pltpu.CompilerParams(vmem_limit_bytes=VMEM_LIMIT),
         cost_estimate=cost(12 * length * features * local_hidden, 40 << 20),
         name="up_back",
-    )(place, grad_down, hidden, slope, full_down, gathered)
+    )(place, grad_down, hidden, slope, gathered, *sources)
 
 
 def norm_back_kernel(
@@ -1418,15 +1454,16 @@
     if after:
         theirs = tie(theirs, *after)
     arrived = exchange(theirs, ACROSS)
-    first = tp_rank == 0
-    return jnp.concatenate(
-        [jnp.where(first, mine, arrived), jnp.where(first, arrived, mine)], axis=0
-    )
+    length = mine.shape[0]
+    row = jnp.zeros((2 * length,) + mine.shape[1:], mine.dtype)
+    row = lax.dynamic_update_slice_in_dim(row, mine, tp_rank * length, 0)
+    return lax.dynamic_update_slice_in_dim(row, arrived, (1 - tp_rank) * length, 0)
 
 
 def both_rows(mine, arrived, tp_rank):
-    first = tp_rank == 0
-    return jnp.stack([jnp.where(first, mine, arrived), jnp.where(first, arrived, mine)])
+    rows = jnp.zeros((2,) + mine.shape, mine.dtype)
+    rows = lax.dynamic_update_slice_in_dim(rows, mine[None], tp_rank, 0)
+    return lax.dynamic_update_slice_in_dim(rows, arrived[None], 1 - tp_rank, 0)
 
 
 def on_device_rows(
@@ -1507,14 +1544,15 @@
     chain_qkv.advance()
     chain_qkv.advance()
     chain_qkv.advance(row_low)
-    chain_qkv.advance()
     gathered = lax.all_gather(
         tie(up_shard, chain_qkv.marks()), ("fsdp", "tp"), axis=0, tiled=False
     ).reshape(fsdp_count, tp_count, shard_rows, local_hidden + local_width)
+    teacher_row = swap_in(teacher, tp_rank, chain_qkv.marks())
+    chain_qkv.advance()
     chain_qkv.finish()
     chain_down.advance(chain_qkv.arrived)
     queries, keys, values, full_qkv, small_all = qkv_project(
-        chain_qkv, qkv_spans, tie(place, chain_down.marks()), row_low, width, small_rows
+        chain_qkv, qkv_spans, tie(place, chain_down.marks(), teacher_row), row_low, width, small_rows
     )
     valid_row = (
         lax.dynamic_slice(
@@ -1548,11 +1586,11 @@
     mixed, q_padded, k_padded = attend(
         queries, keys, tie(values, chain_down.marks()), seg, pairs // 2, pairs // 2, attended
     )
-    teacher_row = swap_in(teacher, tp_rank, attended)
+    weight = (valid_row * (total_tokens / valid_count))[:, None]
     chain_down.advance(mixed)
     vectors = jnp.stack([shifts[2], gains[0], shifts[0]])
     active, slope, unit_first, inverse_first, hidden_low, full_out = out_up_project(
-        tie(mixed, chain_down.marks()),
+        tie(mixed, chain_down.marks(), weight),
         row_low,
         gathered,
         vectors,
@@ -1561,81 +1599,46 @@
         local_width,
     )
     chain_down.finish(active)
-    weight = (valid_row * (total_tokens / valid_count))[:, None]
     vectors = jnp.stack([gains[0], shifts[0], shifts[3], gains[1], shifts[1]])
-    result_low, grad_second, grad_down, sums_second, full_down = down_project(
+    result_low, grad_second, grad_down, sums_second = down_project(
         chain_down, place, active, unit_first, teacher_row, weight, vectors
     )
 
+    weight_chain = chain_down
     chain_down = ScatterChain(
         *down_back(place, grad_down, active, shard_rows, local_hidden, "across"), "across"
     )
+    mine = lax.dynamic_slice_in_dim(result_low, tp_rank * piece_len, piece_len, 0)
+    theirs = lax.dynamic_slice_in_dim(result_low, (1 - tp_rank) * piece_len, piece_len, 0)
+    arrived_out = exchange(theirs, ACROSS)
     grad_hidden, grad_b_up, kept, sent = up_back(
-        place, tie(grad_down, chain_down.marks()), hidden_low, slope, full_down, gathered, "far"
+        place, tie(grad_down, chain_down.marks(), arrived_out), hidden_low, slope, weight_chain, gathered, "far"
     )
     chain_up = ScatterChain(kept, sent, "far")
     chain_down.advance(grad_hidden)
     grad_first, grad_attend, grad_mixed, sums_first = norm_back(
         grad_second, tie(grad_hidden, chain_down.marks(), chain_up.marks()), unit_first, inverse_first, gains[:1], full_out
     )
-    mine = lax.dynamic_slice_in_dim(result_low, tp_rank * piece_len, piece_len, 0)
-    theirs = lax.dynamic_slice_in_dim(result_low, (1 - tp_rank) * piece_len, piece_len, 0)
     back = partial(attend_back, q_padded, k_padded, values, mixed)
     chain_up.advance(grad_mixed)
-    early_grads = back(tie(grad_mixed, chain_up.marks()), 0, early_pairs // 2, 0, early_pairs)
-    early_grads = back(
-        grad_mixed, early_pairs // 2, early_pairs // 2, 0, early_pairs, early_grads
-    )
-    chain_down.advance(early_grads)
-    early_spans = [
-        [
-            (0, early_width, 0, early_width, 0),
-            (early_width, late_width, 0, late_width, late_at),
-            (local_width, early_width, 1, early_width, 0),
-        ],
-        [(0, early_width, 2, early_width, 0), (early_width, early_width, 3, early_width, 0)],
-    ]
-    early_first = local_width + early_width
-    early_kinds = ["across", "far_side"]
-    pieces = weight_grads(
-        place,
-        [grad_attend, tie(row_low, chain_down.marks())],
-        [mixed] + list(early_grads),
-        [(0, 0), (1, 1), (1, 2), (1, 3)],
-        early_spans,
-        early_kinds,
-        shard_rows,
-        [early_first, 2 * early_width],
-    )
-    early_chains = [
-        ScatterChain(pieces[2 * at], pieces[2 * at + 1], kind)
-        for at, kind in enumerate(early_kinds)
-    ]
-    chain_up.advance(pieces)
-    chain_down.advance(pieces)
-    arrived_out = exchange(tie(theirs, grad_mixed), ACROSS)
-    late_grads = back(
-        tie(grad_mixed, chain_up.marks(), chain_down.marks(), arrived_out),
-        early_pairs,
-        late_pairs,
-        early_pairs,
-        late_pairs,
-    )
-    advance_all([chain_up, chain_down] + early_chains, late_grads)
+    attend_grads = back(tie(grad_mixed, chain_up.marks()), 0, pairs, 0, pairs)
+    advance_all([chain_up], attend_grads)
+
     def feature_pieces(rows):
         pieces = rows.reshape(rows.shape[0], fsdp_count, -1).transpose(1, 0, 2)
         pieces = pieces.reshape(fsdp_count, -1, 128)
         return jnp.concatenate([pieces] * tp_count, axis=0)
 
-    def bias_pieces(early, late):
+    def bias_pieces(grad):
+        sums = jnp.sum(grad.astype(jnp.float32), axis=0)
         sums = [
-            jnp.sum(part.astype(jnp.float32), axis=0).reshape(tp_count, -1) for part in (early, late)
+            sums[:late_at].reshape(tp_count, -1),
+            sums[late_at:].reshape(tp_count, -1),
         ]
         return jnp.concatenate(sums, axis=1).reshape(devices, -1)
 
     bias_pair = jnp.concatenate(
-        [bias_pieces(early_grads[0], late_grads[0]), bias_pieces(early_grads[2], late_grads[2])],
-        axis=1,
+        [bias_pieces(attend_grads[0]), bias_pieces(attend_grads[2])], axis=1
     )
     bias_pair = jnp.pad(bias_pair, ((0, 0), (0, 128 - bias_pair.shape[1])))
     squares = jnp.sum(sums_second[3]) * (valid_count / total_tokens)
@@ -1668,66 +1671,67 @@
         axis=1,
     )
     small = jnp.pad(small, ((0, 0), (0, 16 - small.shape[1]), (0, 0)))
-    late_spans = [
-        [(at * late_width, late_width, at, late_width, 0) for at in range(3)]
-        + [(3 * late_width, 128, 3, 0, 0)]
+    def spans_of(start, target):
+        return [
+            (start, early_width, target, early_width, 0),
+            (start + early_width, late_width, target, late_width, late_at),
+        ]
+
+    grad_spans = [
+        spans_of(0, 0) + spans_of(local_width, 1) + [(2 * local_width, 128, 4, 0, 0)],
+        spans_of(0, 2) + spans_of(local_width, 3),
     ]
-    chain_late = ScatterChain(
-        *weight_grads(
-            place,
-            [
-                tie(
-                    row_low,
-                    chain_up.marks(),
-                    chain_down.marks(),
-                    [chain.marks() for chain in early_chains],
-                )
-            ],
-            list(late_grads),
-            [(0, 0), (0, 1), (0, 2)],
-            late_spans,
-            ["late"],
-            shard_rows,
-            [3 * late_width + 128],
-            small.astype(jnp.bfloat16),
-        ),
-        "late",
-    )
-    grads = [part for pair in zip(early_grads, late_grads) for part in pair]
+    grad_kinds = ["side", "far_side"]
+    pieces = weight_grads(
+        place,
+        [grad_attend, tie(row_low, chain_up.marks())],
+        [mixed] + list(attend_grads),
+        [(0, 0), (1, 1), (1, 2), (1, 3)],
+        grad_spans,
+        grad_kinds,
+        shard_rows,
+        [2 * local_width + 128, 2 * local_width],
+        small.astype(jnp.bfloat16),
+    )
+    attend_chains = [
+        ScatterChain(pieces[2 * at], pieces[2 * at + 1], kind)
+        for at, kind in enumerate(grad_kinds)
+    ]
+    advance_all([chain_down], pieces)
     input_theirs = input_grad(
-        place, tie(grad_first, chain_late.marks()), grads, full_qkv, 1
+        place,
+        tie(grad_first, chain_down.marks(), attend_chains[0].sent),
+        attend_grads,
+        full_qkv,
+        1,
     )
     arrived_inputs = exchange(input_theirs, ACROSS)
-    advance_all([chain_late, chain_up] + early_chains, input_theirs)
+    advance_all(attend_chains, input_theirs)
     input_mine = input_grad(
         place,
-        tie(grad_first, chain_late.marks(), [chain.marks() for chain in early_chains]),
-        grads,
+        tie(grad_first, [chain.marks() for chain in attend_chains]),
+        attend_grads,
         full_qkv,
         0,
     )
+    advance_all([chain_up, chain_down], input_mine)
+    mine, arrived_out = tie((mine, arrived_out), chain_up.marks())
+    hidden_out = both_rows(mine, arrived_out, tp_rank)
+    advance_all(attend_chains, hidden_out)
+    sent = [chain.marks() for chain in attend_chains]
+    advance_all([chain_up, chain_down], sent)
+    arrived_inputs = tie(arrived_inputs, sent)
     grad_inputs = both_rows(input_mine, arrived_inputs, tp_rank)
-    hidden_out = both_rows(mine, tie(arrived_out, input_mine), tp_rank)
-    advance_all([chain_late] + early_chains, input_mine)
-    waiting = [chain_late] + early_chains
-    while waiting:
-        advance_all(waiting)
-        waiting = [chain for chain in waiting if chain.at < len(chain.steps)]
-    for chain in [chain_up, chain_down] + early_chains:
-        assert chain.at == len(chain.steps)
-    grad_w_down, grad_w_up = (chain_down.finish(input_mine), chain_up.finish(input_mine))
-    early_one, early_two = [chain.finish() for chain in early_chains]
-    late = chain_late.finish()
-    early_qkv = (
-        early_one[:, local_width:],
-        early_two[:, :early_width],
-        early_two[:, early_width:],
-    )
-    grad_w_query, grad_w_key, grad_w_value = [
-        jnp.concatenate([early, late[:, at * late_width : (at + 1) * late_width]], axis=1)
-        for at, early in enumerate(early_qkv)
-    ]
-    own = late[:, 3 * late_width :]
+    while attend_chains[0].at < len(attend_chains[0].steps):
+        advance_all(attend_chains, grad_inputs)
+    sent = [chain.marks() for chain in attend_chains]
+    grad_w_down = chain_down.finish(sent)
+    grad_w_up = chain_up.finish(sent)
+    first, second = [chain.finish() for chain in attend_chains]
+    grad_w_out = first[:, :local_width].T
+    grad_w_query = first[:, local_width : 2 * local_width]
+    grad_w_key, grad_w_value = (second[:, :local_width], second[:, local_width:])
+    own = first[:, 2 * local_width :]
     bias_size, row = (b_query.shape[0], 2)
     gain_rows = ln_gains.size // 128
     shift_rows = ln_shifts.size // 128
@@ -1740,7 +1744,7 @@
         grad_w_query,
         grad_w_key,
         grad_w_value,
-        early_one[:, :local_width].T,
+        grad_w_out,
         own[0, :bias_size],
         own[0, bias_size : 2 * bias_size],
         grad_w_up,

time: 513 us -> 510 us (level)
  waiting for transfers between devices: 86.4 us -> 116 us
  other arithmetic: 70.3 us -> 48.5 us
  starting transfers between devices: 58.8 us -> 44.6 us
  local copies, waits for them, and re-layouts: 23.5 us -> 31.4 us
    ppermute x41 -> x36, waiting for transfers between devices: 69.8 us -> 98.8 us  [exchange(): lax.ppermute(values, 'fsdp', [(at, at ^ move[0]) for at in range(lax.axis...]
    ppermute x41 -> x36, starting transfers between devices: 40.4 us -> 28.4 us  [exchange(): lax.ppermute(values, 'fsdp', [(at, at ^ move[0]) for at in range(lax.axis...]
    convert_element_type x19 -> x16, other arithmetic: 42.3 us -> 33.8 us  [advance(): self.total(at * self.size).astype(jnp.bfloat16)]
    concatenate x5 -> x0, other arithmetic: 6.47 us -> none  [the longest x3 3.52 us: on_device_rows(): jnp.concatenate([early, late[:, at * late_width:(at + 1) * late_width]],...]
    ppermute x13 -> x12, waiting for transfers between devices: 11.5 us -> 16.8 us  [exchange(): lax.ppermute(values, ('fsdp', 'tp'), [(at, at ^ flip) for at in range(cou...]
    all_gather x1, waiting for transfers between devices: 5.13 us -> 0.01 us  [on_device_rows(): lax.all_gather(tie(up_shard, chain_qkv.marks()), ('fsdp', 'tp'), axis=0,...]
    pallas_call x3 -> x1, Pallas kernels: 46 us -> 41.2 us  [attend_back(): pl.pallas_call(kernel, grid=(count,), in_specs=[padded, padded, pair, pai...]
    pallas_call x2 -> x1, Pallas kernels: 20 us -> 17.5 us  [weight_grads(): pl.pallas_call(partial(weight_grad_kernel, products, spans, places, extra...]
  transfers between devices with their start and end apart: 55 -> 49, of which waited for: 20 -> 19; matrix products, arithmetic and copies ran while one was open for 14% -> 12% of each run, Pallas kernels for 40% -> 44%
where the time goes in v4:
time: 510 us; the launch traced here: 501 us
  Pallas kernels  241 us (47%)
  waiting for transfers between devices  116 us (23%)
  other arithmetic  48.5 us (10%)
  starting transfers between devices  44.6 us (9%)
  local copies, waits for them, and re-layouts  31.4 us (6%)
  between operations  19.9 us (4%)
    ppermute x36, waiting for transfers between devices, exchange(): lax.ppermute(values, 'fsdp', [(at, at ^ move[0]) for at in range(lax.axis...  98.8 us
    pallas_call x1, Pallas kernels, attend_back(): pl.pallas_call(kernel, grid=(count,), in_specs=[padded, padded, pair, pai...  41.2 us
    pallas_call x1, Pallas kernels, up_back(): pl.pallas_call(partial(up_back_kernel, places, tp_places, each, down_plac...  39.3 us
    convert_element_type x16, other arithmetic, advance(): self.total(at * self.size).astype(jnp.bfloat16)  33.8 us
    pallas_call x2, Pallas kernels, attend(): pl.pallas_call(kernel, grid=(count,), in_specs=[pl.BlockSpec((length, 1),...  28.5 us
    ppermute x36, starting transfers between devices, exchange(): lax.ppermute(values, 'fsdp', [(at, at ^ move[0]) for at in range(lax.axis...  28.4 us
    pallas_call x1, Pallas kernels, out_up_project(): pl.pallas_call(out_up_kernel, grid=(hidden_units // block_width,), in_spe...  25.8 us
    pallas_call x1, Pallas kernels, down_project(): pl.pallas_call(partial(down_kernel, places), grid=(length // BLOCK,), in_...  23.1 us
  transfers between devices with their start and end apart: 49, of which 19 were waited for; matrix products, arithmetic and copies ran while one was open for 12% of the time, Pallas kernels for 44%

profile of v4, /device:TPU:0, one launch (start us, length us, event | category | flops | bytes accessed | tf_op | source)
XLA Modules:
  0.0 501.2 jit_solution(14830699269450602023)
XLA Ops:
  18.0 9.5 %collective-permute-done.1 = bf16[1,64,768]{2,1,0:T(8,128)(2,1)S(1)} collective-permute-done((bf16[1,64,768]{2,1,0:T(8,128)(2,1)}, bf16[1,64,768]{2,1,0:T(8,128)(2,1)S(1)}, u32[]{:S(2)}, u32[]{:S(2)}) %collective-permute-start.1) | collective-permute-done | bytes 98336 | tf_op jit(solution)/shard_map/ppermute | solution.py:378
  46.6 8.2 %collective-permute-done.6 = bf16[4,64,768]{2,1,0:T(8,128)(2,1)S(1)} collective-permute-done((bf16[4,64,768]{2,1,0:T(8,128)(2,1)S(1)}, bf16[4,64,768]{2,1,0:T(8,128)(2,1)S(1)}, u32[]{:S(2)}, u32[]{:S(2)}) %collective-permute-start.6) | collective-permute-done | bytes 393248 | tf_op jit(solution)/shard_map/ppermute | solution.py:378
  62.9 18.4 %collective-permute-done.7.refs_1_ = bf16[8,64,896]{2,1,0:T(8,128)(2,1)} collective-permute-done((bf16[8,64,896]{2,1,0:T(8,128)(2,1)S(1)}, bf16[8,64,896]{2,1,0:T(8,128)(2,1)}, u32[]{:S(2)}, u32[]{:S(2)}) %collective-permute-start.7) | collective-permute-done | bytes 917536 | tf_op jit(solution)/shard_map/ppermute | solution.py:378
  81.3 7.7 %collective-permute-done.8.refs_5_ = bf16[8,64,768]{2,1,0:T(8,128)(2,1)} collective-permute-done((bf16[8,64,768]{2,1,0:T(8,128)(2,1)}, bf16[8,64,768]{2,1,0:T(8,128)(2,1)}, u32[]{:S(2)}, u32[]{:S(2)}) %collective-permute-start.8) | collective-permute-done | bytes 786464 | tf_op jit(solution)/shard_map/ppermute | solution.py:378
  98.2 17.5 %qkv_project.1 = (bf16[1024,1024]{1,0:T(8,128)(2,1)}, bf16[1024,1024]{1,0:T(8,128)(2,1)}, bf16[1024,1024]{1,0:T(8,128)(2,1)}, bf16[1024,3072]{1,0:T(8,128)(2,1)}, bf16[32,32,128]{2,1,0:T(8,128)(2,1)}) custom-call(s32[2]{0:T(128)} %pad_add_fusion.place_ref, bf16[1024,1024]{1,0:T(8,128)(2,1)} %copy-done.3, bf16[8,64,896]{2,1,0:T(8,128)(2,1)} %copy-done.14, ...), custom_call_target="tpu_custom_call" | custom-call | flops 3221225 | bytes 12582 | tf_op jit(solution)/shard_map/qkv_project/pallas_call | solution.py:891
  119.3 14.3 %attend.2 = (bf16[1024,1024]{1,0:T(8,128)(2,1)}, bf16[16,1024,128]{2,1,0:T(8,128)(2,1)}, bf16[16,1024,128]{2,1,0:T(8,128)(2,1)}) custom-call(s32[1024,1]{1,0:T(8,128)} %copy.37.seg_ref, bf16[1024,1024]{1,0:T(8,128)(2,1)} %get-tuple-element.261.q_ref, bf16[1024,1024]{1,0:T(8,128)(2,1)} %get-tuple-element.262.k_ref, bf16[1024,1024]{1,0:T(8,128)(2,1)} %get-tuple-element.271.v_ref), custom_call_target="tpu_custom_call" | custom-call | flops 7000000 | bytes 4194 | tf_op jit(solution)/shard_map/attend/pallas_call | solution.py:642
  133.6 4.7 collective-permute-done.16
  143.1 14.2 %attend.3 = (bf16[1024,1024]{1,0:T(8,128)(2,1)}, bf16[16,1024,128]{2,1,0:T(8,128)(2,1)}, bf16[16,1024,128]{2,1,0:T(8,128)(2,1)}) custom-call(s32[1024,1]{1,0:T(8,128)} %copy.37.seg_ref, bf16[1024,1024]{1,0:T(8,128)(2,1)} %get-tuple-element.261.q_ref, ...), custom_call_target="tpu_custom_call", output_to_operand_aliasing={{0}: (4, {}), {1}: (5, {}), {2}: (6, {})} | custom-call | flops 7000000 | bytes 4194 | tf_op jit(solution)/shard_map/attend/pallas_call | solution.py:642
  161.7 25.8 %out_up_project.1 = (bf16[1024,4096]{1,0:T(8,128)(2,1)}, bf16[1024,4096]{1,0:T(8,128)(2,1)}, f32[1024,1024]{1,0:T(8,128)}, f32[1024,1]{1,0:T(8,128)}, bf16[1024,...) custom-call(bf16[1024,1024]{1,0:T(8,128)(2,1)} %get-tuple-element.278.mixed_ref.out_ref.refs_2_, ...), custom_call_target="tpu_custom_call" | custom-call | flops 5368709 | bytes 18874 | tf_op jit(solution)/shard_map/out_up_project/pallas_call | solution.py:967
  193.5 23.1 %down_project.1 = (bf16[1024,1024]{1,0:T(8,128)(2,1)}, f32[1024,1024]{1,0:T(8,128)}, bf16[1024,1024]{1,0:T(8,128)(2,1)}, f32[8,1024]{1,0:T(8,128)}) custom-call(s32[2]{0:T(128)} %pad_add_fusion.place_ref, bf16[1024,4096]{1,0:T(8,128)(2,1)} %get-tuple-element.281.active_ref, f32[1024,1024]{1,0:T(8,128)} %get-tuple-element.282.unit_ref, ...), custom_call_target="tpu_custom_call" | custom-call | flops 4294967 | bytes 18874 | tf_op jit(solution)/shard_map/down_project/pallas_call | solution.py:1084
  219.2 17.9 %down_back.1 = (bf16[16,64,2048]{2,1,0:T(8,128)(2,1)}, bf16[16,64,2048]{2,1,0:T(8,128)(2,1)}) custom-call(s32[2]{0:T(128)} %pad_add_fusion.place_ref, bf16[1024,1024]{1,0:T(8,128)(2,1)} %get-tuple-element.288.grad_ref, bf16[1024,4096]{1,0:T(8,128)(2,1)} %get-tuple-element.281.active_ref), custom_call_target="tpu_custom_call" | custom-call | flops 4294967 | bytes 10485 | tf_op jit(solution)/shard_map/down_back/pallas_call | solution.py:1237
  237.2 6.7 %collective-permute-done.26 = bf16[512,1024]{1,0:T(8,128)(2,1)S(1)} collective-permute-done((bf16[512,1024]{1,0:T(8,128)(2,1)S(1)}, bf16[512,1024]{1,0:T(8,128)(2,1)S(1)}, u32[]{:S(2)}, u32[]{:S(2)}) %collective-permute-start.26) | collective-permute-done | bytes 1048608 | tf_op jit(solution)/shard_map/ppermute | solution.py:381
  243.8 39.3 %up_back.1 = (f32[1024,1024]{1,0:T(8,128)}, f32[1,4096]{1,0:T(1,128)}, bf16[16,64,2048]{2,1,0:T(8,128)(2,1)}, bf16[16,64,2048]{2,1,0:T(8,128)(2,1)}) custom-call(s32[2]{0:T(128)} %pad_add_fusion.place_ref, bf16[1024,1024]{1,0:T(8,128)(2,1)} %get-tuple-element.288.grad_ref, bf16[1024,1024]{1,0:T(8,128)(2,1)} %get-tuple-element.289.hidden_ref, ...), custom_call_target="tpu_custom_call" | custom-call | flops 12884901 | bytes 20971 | tf_op jit(solution)/shard_map/up_back/pallas_call | solution.py:1264
  287.7 10.4 %norm_back.1 = (f32[1024,1024]{1,0:T(8,128)}, bf16[1024,1024]{1,0:T(8,128)(2,1)}, bf16[1024,1024]{1,0:T(8,128)(2,1)}, f32[8,1024]{1,0:T(8,128)}) custom-call(f32[1024,1024]{1,0:T(8,128)} %get-tuple-element.293.base_ref, f32[1024,1024]{1,0:T(8,128)} %get-tuple-element.298.grad_ref, f32[1024,1024]{1,0:T(8,128)} %get-tuple-element.282.unit_ref, ...), custom_call_target="tpu_custom_call" | custom-call | flops 1073741 | bytes 11534 | tf_op jit(solution)/shard_map/norm_back/pallas_call | solution.py:1323
  308.6 41.2 %attend_back.1 = (bf16[1024,1024]{1,0:T(8,128)(2,1)}, bf16[1024,1024]{1,0:T(8,128)(2,1)}, bf16[1024,1024]{1,0:T(8,128)(2,1)}) custom-call(bf16[16,1024,128]{2,1,0:T(8,128)(2,1)} %get-tuple-element.304.qx_ref, bf16[16,1024,128]{2,1,0:T(8,128)(2,1)} %get-tuple-element.305.kx_ref, bf16[1024,1024]{1,0:T(8,128)(2,1)} %get-tuple-element.271.v_ref, ...), custom_call_target="tpu_custom_call" | custom-call | flops 20000000 | bytes 8388 | tf_op jit(solution)/shard_map/attend_back/pallas_call | solution.py:731
  356.9 17.5 %weight_grads.1 = (bf16[16,64,1152]{2,1,0:T(8,128)(2,1)}, bf16[16,64,1152]{2,1,0:T(8,128)(2,1)}, bf16[16,64,1024]{2,1,0:T(8,128)(2,1)}, bf16[16,64,1024]{2,1,0:T(8,128)(2,1)}) custom-call(s32[2]{0:T(128)} %pad_add_fusion.place_ref, bf16[1024,1024]{1,0:T(8,128)(2,1)} %get-tuple-element.316.refs_0_, bf16[1024,1024]{1,0:T(8,128)(2,1)} %copy-done.3, ...), custom_call_target="tpu_custom_call" | custom-call | flops 4294967 | bytes 8388 | tf_op jit(solution)/shard_map/weight_grads/pallas_call | solution.py:1402
  381.4 9.2 %input_grad.2 = bf16[512,1024]{1,0:T(8,128)(2,1)} custom-call(s32[2]{0:T(128)} %pad_add_fusion.place_ref, f32[1024,1024]{1,0:T(8,128)} %get-tuple-element.342.base_ref, bf16[1024,1024]{1,0:T(8,128)(2,1)} %get-tuple-element.307.refs_3_.refs_0_, bf16[1024,1024]{1,0:T(8,128)(2,1)} %get-tuple-element.308.refs_4_.refs_1_, ...), custom_call_target="tpu_custom_call" | custom-call | flops 1610612 | bytes 7340 | tf_op jit(solution)/shard_map/input_grad/pallas_call | solution.py:1434
  396.7 8.9 %input_grad.3 = bf16[512,1024]{1,0:T(8,128)(2,1)} custom-call(s32[2]{0:T(128)} %pad_add_fusion.place_ref, f32[1024,1024]{1,0:T(8,128)} %get-tuple-element.342.base_ref, bf16[1024,1024]{1,0:T(8,128)(2,1)} %get-tuple-element.307.refs_3_.refs_0_, bf16[1024,1024]{1,0:T(8,128)(2,1)} %get-tuple-element.308.refs_4_.refs_1_, ...), custom_call_target="tpu_custom_call" | custom-call | flops 1610612 | bytes 7340 | tf_op jit(solution)/shard_map/input_grad/pallas_call | solution.py:1434
  414.2 6.5 %collective-permute-done.36 = bf16[8,64,1024]{2,1,0:T(8,128)(2,1)} collective-permute-done((bf16[8,64,1024]{2,1,0:T(8,128)(2,1)}, bf16[8,64,1024]{2,1,0:T(8,128)(2,1)}, u32[]{:S(2)}, u32[]{:S(2)}) %collective-permute-start.36) | collective-permute-done | bytes 1048608 | tf_op jit(solution)/shard_map/ppermute | solution.py:378
  420.7 9.3 %collective-permute-done.35 = bf16[8,64,1152]{2,1,0:T(8,128)(2,1)} collective-permute-done((bf16[8,64,1152]{2,1,0:T(8,128)(2,1)}, bf16[8,64,1152]{2,1,0:T(8,128)(2,1)}, u32[]{:S(2)}, u32[]{:S(2)}) %collective-permute-start.35) | collective-permute-done | bytes 1179680 | tf_op jit(solution)/shard_map/ppermute | solution.py:378
  435.3 5.8 %collective-permute-done.44 = bf16[2,64,2048]{2,1,0:T(8,128)(2,1)S(1)} collective-permute-done((bf16[2,64,2048]{2,1,0:T(8,128)(2,1)S(1)}, bf16[2,64,2048]{2,1,0:T(8,128)(2,1)S(1)}, u32[]{:S(2)}, u32[]{:S(2)}) %collective-permute-start.44) | collective-permute-done | bytes 524320 | tf_op jit(solution)/shard_map/ppermute | solution.py:378
  445.0 6.5 %collective-permute-done.38 = bf16[4,64,1024]{2,1,0:T(8,128)(2,1)S(1)} collective-permute-done((bf16[4,64,1024]{2,1,0:T(8,128)(2,1)S(1)}, bf16[4,64,1024]{2,1,0:T(8,128)(2,1)S(1)}, u32[]{:S(2)}, u32[]{:S(2)}) %collective-permute-start.38) | collective-permute-done | bytes 524320 | tf_op jit(solution)/shard_map/ppermute | solution.py:378
  458.5 9.3 %collective-permute-done.41 = bf16[2,64,1024]{2,1,0:T(8,128)(2,1)S(1)} collective-permute-done((bf16[2,64,1024]{2,1,0:T(8,128)(2,1)S(1)}, bf16[2,64,1024]{2,1,0:T(8,128)(2,1)S(1)}, u32[]{:S(2)}, u32[]{:S(2)}) %collective-permute-start.41) | collective-permute-done | bytes 262176 | tf_op jit(solution)/shard_map/ppermute | solution.py:378
  473.0 8.2 %collective-permute-done.46 = bf16[1,64,2048]{2,1,0:T(8,128)(2,1)S(1)} collective-permute-done((bf16[1,64,2048]{2,1,0:T(8,128)(2,1)S(1)}, bf16[1,64,2048]{2,1,0:T(8,128)(2,1)S(1)}, u32[]{:S(2)}, u32[]{:S(2)}) %collective-permute-start.46) | collective-permute-done | bytes 262176 | tf_op jit(solution)/shard_map/ppermute | solution.py:378
  (264 shorter events, 141.4 us)
Async XLA Ops:
  7.2 154.5 %all-gather.3.cloned.1.call-start = ((), (), s32[]{:S(2)}) async-start(), calls=%async_computation | async-start | bytes 10813440 | tf_op jit(solution)/shard_map/all_gather | solution.py:1547
  9.5 27.1 %collective-permute-start.4 = (bf16[512,1024]{1,0:T(8,128)(2,1)}, bf16[512,1024]{1,0:T(8,128)(2,1)S(1)}, u32[]{:S(2)}, u32[]{:S(2)}) collective-permute-start(bf16[512,1024]{1,0:T(8,128)(2,1)} %dynamic-slice_bitcast_fusion.1), channel_id=1, source_target_pairs={{0,1},{1,0},{2,3},{3,2},{4,5},{5,4},{6,7},{7,6},{8,9},{9,8},{10,11... | collective-permute-start | bytes 3145736 | tf_op jit(solution)/shard_map/ppermute | solution.py:381
  55.1 26.2 %collective-permute-start.7 = (bf16[8,64,896]{2,1,0:T(8,128)(2,1)S(1)}, bf16[8,64,896]{2,1,0:T(8,128)(2,1)}, u32[]{:S(2)}, u32[]{:S(2)}) collective-permute-start(bf16[8,64,896]{2,1,0:T(8,128)(2,1)S(1)} %constant_dynamic-update-slice_fusion.8.refs_0_), channel_id=1, source_target_pairs={{0,4},{2,6},{4,0},{6,2},{8,12},{10,14},{12,8},{14,10},{16,20},{18,... | collective-permute-start | bytes 2752520 | tf_op jit(solution)/shard_map/ppermute | solution.py:378
  59.2 29.9 %collective-permute-start.8 = (bf16[8,64,768]{2,1,0:T(8,128)(2,1)}, bf16[8,64,768]{2,1,0:T(8,128)(2,1)}, u32[]{:S(2)}, u32[]{:S(2)}) collective-permute-start(bf16[8,64,768]{2,1,0:T(8,128)(2,1)} %constant_dynamic-update-slice_fusion.10.refs_4_), channel_id=1, source_target_pairs={{0,8},{2,10},{4,12},{6,14},{8,0},{10,2},{12,4},{14,6},{16,24},{18,... | collective-permute-start | bytes 2359304 | tf_op jit(solution)/shard_map/ppermute | solution.py:378
  60.8 32.0 %collective-permute-start.9 = (bf16[512,1024]{1,0:T(8,128)(2,1)S(1)}, bf16[512,1024]{1,0:T(8,128)(2,1)}, u32[]{:S(2)}, u32[]{:S(2)}) collective-permute-start(bf16[512,1024]{1,0:T(8,128)(2,1)S(1)} %dynamic-slice_bitcast_fusion), channel_id=1, source_target_pairs={{0,1},{1,0},{2,3},{3,2},{4,5},{5,4},{6,7},{7,6},{8,9},{9,8},{10,11... | collective-permute-start | bytes 3145736 | tf_op jit(solution)/shard_map/ppermute | solution.py:381
  62.4 34.1 %collective-permute-start.12 = (bf16[8,64,768]{2,1,0:T(8,128)(2,1)}, bf16[8,64,768]{2,1,0:T(8,128)(2,1)}, u32[]{:S(2)}, u32[]{:S(2)}) collective-permute-start(bf16[8,64,768]{2,1,0:T(8,128)(2,1)} %constant_dynamic-update-slice_fusion.10.refs_4_), channel_id=1, source_target_pairs={{0,2},{2,0},{4,6},{6,4},{8,10},{10,8},{12,14},{14,12},{16,18},{18,... | collective-permute-start | bytes 2359304 | tf_op jit(solution)/shard_map/ppermute | solution.py:378
  62.4 35.8 %collective-permute-start.10 = (bf16[8,64,896]{2,1,0:T(8,128)(2,1)S(1)}, bf16[8,64,896]{2,1,0:T(8,128)(2,1)}, u32[]{:S(2)}, u32[]{:S(2)}) collective-permute-start(bf16[8,64,896]{2,1,0:T(8,128)(2,1)S(1)} %constant_dynamic-update-slice_fusion.8.refs_0_), channel_id=1, source_target_pairs={{0,2},{2,0},{4,6},{6,4},{8,10},{10,8},{12,14},{14,12},{16,18},{18,... | collective-permute-start | bytes 2752520 | tf_op jit(solution)/shard_map/ppermute | solution.py:378
  92.9 23.9 %collective-permute-start.14 = (bf16[1,64,1152]{2,1,0:T(8,128)(2,1)S(1)}, bf16[1,64,1152]{2,1,0:T(8,128)(2,1)S(1)}, u32[]{:S(2)}, u32[]{:S(2)}) collective-permute-start(bf16[1,64,1152]{2,1,0:T(8,128)(2,1)S(1)} %bitcast.80), channel_id=1, source_target_pairs={{0,16},{2,18},{4,20},{6,22},{8,24},{10,26},{12,28},{14,30},{16,0},... | collective-permute-start | bytes 442376 | tf_op jit(solution)/shard_map/ppermute | solution.py:378
  158.2 29.3 %collective-permute-start.20 = (bf16[8,64,1152]{2,1,0:T(8,128)(2,1)S(1)}, bf16[8,64,1152]{2,1,0:T(8,128)(2,1)S(1)}, u32[]{:S(2)}, u32[]{:S(2)}) collective-permute-start(bf16[8,64,1152]{2,1,0:T(8,128)(2,1)S(1)} %constant_dynamic-update-slice_fusion.20.refs_0_), channel_id=1, source_target_pairs={{0,4},{2,6},{4,0},{6,2},{8,12},{10,14},{12,8},{14,10},{16,20},{18,... | collective-permute-start | bytes 3538952 | tf_op jit(solution)/shard_map/ppermute | solution.py:378
  159.3 28.1 %collective-permute-start.21 = (bf16[8,64,896]{2,1,0:T(8,128)(2,1)S(1)}, bf16[8,64,896]{2,1,0:T(8,128)(2,1)}, u32[]{:S(2)}, u32[]{:S(2)}) collective-permute-start(bf16[8,64,896]{2,1,0:T(8,128)(2,1)S(1)} %constant_dynamic-update-slice_fusion.22.refs_4_), channel_id=1, source_target_pairs={{0,8},{2,10},{4,12},{6,14},{8,0},{10,2},{12,4},{14,6},{16,24},{18,... | collective-permute-start | bytes 2752520 | tf_op jit(solution)/shard_map/ppermute | solution.py:378
  161.7 31.7 %collective-permute-start.22 = (bf16[8,64,1152]{2,1,0:T(8,128)(2,1)S(1)}, bf16[8,64,1152]{2,1,0:T(8,128)(2,1)}, u32[]{:S(2)}, u32[]{:S(2)}) collective-permute-start(bf16[8,64,1152]{2,1,0:T(8,128)(2,1)S(1)} %constant_dynamic-update-slice_fusion.20.refs_0_), channel_id=1, source_target_pairs={{0,2},{2,0},{4,6},{6,4},{8,10},{10,8},{12,14},{14,12},{16,18},{18,... | collective-permute-start | bytes 3538952 | tf_op jit(solution)/shard_map/ppermute | solution.py:378
  218.3 25.5 %collective-permute-start.26 = (bf16[512,1024]{1,0:T(8,128)(2,1)S(1)}, bf16[512,1024]{1,0:T(8,128)(2,1)S(1)}, u32[]{:S(2)}, u32[]{:S(2)}) collective-permute-start(bf16[512,1024]{1,0:T(8,128)(2,1)S(1)} %get-tuple-element.454), channel_id=1, source_target_pairs={{0,1},{1,0},{2,3},{3,2},{4,5},{5,4},{6,7},{7,6},{8,9},{9,8},{10,11... | collective-permute-start | bytes 3145736 | tf_op jit(solution)/shard_map/ppermute | solution.py:381
  237.0 46.2 %collective-permute-start.28 = (bf16[16,64,2048]{2,1,0:T(8,128)(2,1)}, bf16[16,64,2048]{2,1,0:T(8,128)(2,1)}, u32[]{:S(2)}, u32[]{:S(2)}) collective-permute-start(bf16[16,64,2048]{2,1,0:T(8,128)(2,1)} %get-tuple-element.287), channel_id=1, source_target_pairs={{0,2},{2,0},{4,6},{6,4},{8,10},{10,8},{12,14},{14,12},{16,18},{18,... | collective-permute-start | bytes 12582920 | tf_op jit(solution)/shard_map/ppermute | solution.py:378
  302.6 50.8 %collective-permute-start.29 = (bf16[8,64,2048]{2,1,0:T(8,128)(2,1)}, bf16[8,64,2048]{2,1,0:T(8,128)(2,1)}, u32[]{:S(2)}, u32[]{:S(2)}) collective-permute-start(bf16[8,64,2048]{2,1,0:T(8,128)(2,1)} %add_convert_fusion), channel_id=1, source_target_pairs={{0,8},{2,10},{4,12},{6,14},{8,0},{10,2},{12,4},{14,6},{16,24},{18,... | collective-permute-start | bytes 6291464 | tf_op jit(solution)/shard_map/ppermute | solution.py:378
  306.6 68.3 %collective-permute-start.31 = (bf16[8,64,2048]{2,1,0:T(8,128)(2,1)}, bf16[8,64,2048]{2,1,0:T(8,128)(2,1)}, u32[]{:S(2)}, u32[]{:S(2)}) collective-permute-start(bf16[8,64,2048]{2,1,0:T(8,128)(2,1)} %add_convert_fusion.1), channel_id=1, source_target_pairs={{0,1},{1,0},{2,3},{3,2},{4,5},{5,4},{6,7},{7,6},{8,9},{9,8},{10,11... | collective-permute-start | bytes 6291464 | tf_op jit(solution)/shard_map/ppermute | solution.py:381
  378.4 27.2 %collective-permute-start.32 = (bf16[4,64,2048]{2,1,0:T(8,128)(2,1)}, bf16[4,64,2048]{2,1,0:T(8,128)(2,1)}, u32[]{:S(2)}, u32[]{:S(2)}) collective-permute-start(bf16[4,64,2048]{2,1,0:T(8,128)(2,1)} %add_convert_fusion.4), channel_id=1, source_target_pairs={{0,4},{2,6},{4,0},{6,2},{8,12},{10,14},{12,8},{14,10},{16,20},{18,... | collective-permute-start | bytes 3145736 | tf_op jit(solution)/shard_map/ppermute | solution.py:378
  379.1 26.5 %collective-permute-start.30 = (bf16[4,64,2048]{2,1,0:T(8,128)(2,1)}, bf16[4,64,2048]{2,1,0:T(8,128)(2,1)}, u32[]{:S(2)}, u32[]{:S(2)}) collective-permute-start(bf16[4,64,2048]{2,1,0:T(8,128)(2,1)} %add_convert_fusion.5), channel_id=1, source_target_pairs={{0,1},{1,0},{2,3},{3,2},{4,5},{5,4},{6,7},{7,6},{8,9},{9,8},{10,11... | collective-permute-start | bytes 3145736 | tf_op jit(solution)/shard_map/ppermute | solution.py:381
  390.6 53.1 %collective-permute-start.39 = (bf16[512,1024]{1,0:T(8,128)(2,1)}, bf16[512,1024]{1,0:T(8,128)(2,1)}, u32[]{:S(2)}, u32[]{:S(2)}) collective-permute-start(bf16[512,1024]{1,0:T(8,128)(2,1)} %input_grad.2), channel_id=1, source_target_pairs={{0,1},{1,0},{2,3},{3,2},{4,5},{5,4},{6,7},{7,6},{8,9},{9,8},{10,11... | collective-permute-start | bytes 3145736 | tf_op jit(solution)/shard_map/ppermute | solution.py:381
  394.2 26.4 %collective-permute-start.36 = (bf16[8,64,1024]{2,1,0:T(8,128)(2,1)}, bf16[8,64,1024]{2,1,0:T(8,128)(2,1)}, u32[]{:S(2)}, u32[]{:S(2)}) collective-permute-start(bf16[8,64,1024]{2,1,0:T(8,128)(2,1)} %add_convert_fusion.3), channel_id=1, source_target_pairs={{0,8},{2,10},{4,12},{6,14},{8,0},{10,2},{12,4},{14,6},{16,24},{18,... | collective-permute-start | bytes 3145736 | tf_op jit(solution)/shard_map/ppermute | solution.py:378
  395.6 34.4 %collective-permute-start.35 = (bf16[8,64,1152]{2,1,0:T(8,128)(2,1)}, bf16[8,64,1152]{2,1,0:T(8,128)(2,1)}, u32[]{:S(2)}, u32[]{:S(2)}) collective-permute-start(bf16[8,64,1152]{2,1,0:T(8,128)(2,1)} %add_convert_fusion.2), channel_id=1, source_target_pairs={{0,4},{2,6},{4,0},{6,2},{8,12},{10,14},{12,8},{14,10},{16,20},{18,... | collective-permute-start | bytes 3538952 | tf_op jit(solution)/shard_map/ppermute | solution.py:378
  407.5 27.8 %collective-permute-start.45 = (bf16[2,64,2048]{2,1,0:T(8,128)(2,1)S(1)}, bf16[2,64,2048]{2,1,0:T(8,128)(2,1)S(1)}, u32[]{:S(2)}, u32[]{:S(2)}) collective-permute-start(bf16[2,64,2048]{2,1,0:T(8,128)(2,1)S(1)} %add_convert_fusion.7), channel_id=1, source_target_pairs={{0,8},{2,10},{4,12},{6,14},{8,0},{10,2},{12,4},{14,6},{16,24},{18,... | collective-permute-start | bytes 1572872 | tf_op jit(solution)/shard_map/ppermute | solution.py:378
  411.4 29.7 %collective-permute-start.44 = (bf16[2,64,2048]{2,1,0:T(8,128)(2,1)S(1)}, bf16[2,64,2048]{2,1,0:T(8,128)(2,1)S(1)}, u32[]{:S(2)}, u32[]{:S(2)}) collective-permute-start(bf16[2,64,2048]{2,1,0:T(8,128)(2,1)S(1)} %add_convert_fusion.9), channel_id=1, source_target_pairs={{0,4},{2,6},{4,0},{6,2},{8,12},{10,14},{12,8},{14,10},{16,20},{18,... | collective-permute-start | bytes 1572872 | tf_op jit(solution)/shard_map/ppermute | solution.py:378
  442.5 30.6 %collective-permute-start.47 = (bf16[1,64,2048]{2,1,0:T(8,128)(2,1)S(1)}, bf16[1,64,2048]{2,1,0:T(8,128)(2,1)S(1)}, u32[]{:S(2)}, u32[]{:S(2)}) collective-permute-start(bf16[1,64,2048]{2,1,0:T(8,128)(2,1)S(1)} %add_convert_fusion.11), channel_id=1, source_target_pairs={{0,16},{2,18},{4,20},{6,22},{8,24},{10,26},{12,28},{14,30},{16,0},... | collective-permute-start | bytes 786440 | tf_op jit(solution)/shard_map/ppermute | solution.py:378
  458.4 22.8 %collective-permute-start.46 = (bf16[1,64,2048]{2,1,0:T(8,128)(2,1)S(1)}, bf16[1,64,2048]{2,1,0:T(8,128)(2,1)S(1)}, u32[]{:S(2)}, u32[]{:S(2)}) collective-permute-start(bf16[1,64,2048]{2,1,0:T(8,128)(2,1)S(1)} %add_convert_fusion.12), channel_id=1, source_target_pairs={{0,16},{2,18},{4,20},{6,22},{8,24},{10,26},{12,28},{14,30},{16,0},... | collective-permute-start | bytes 786440 | tf_op jit(solution)/shard_map/ppermute | solution.py:378
  (55 other events, 921.2 us)
Sparse Core Ops, SparseCore 0:
  43.3 108.5 all-gather.2

commit v5 on v4

--- a/solution.py
+++ b/solution.py
@@ -1547,12 +1547,11 @@
     gathered = lax.all_gather(
         tie(up_shard, chain_qkv.marks()), ("fsdp", "tp"), axis=0, tiled=False
     ).reshape(fsdp_count, tp_count, shard_rows, local_hidden + local_width)
-    teacher_row = swap_in(teacher, tp_rank, chain_qkv.marks())
     chain_qkv.advance()
     chain_qkv.finish()
     chain_down.advance(chain_qkv.arrived)
     queries, keys, values, full_qkv, small_all = qkv_project(
-        chain_qkv, qkv_spans, tie(place, chain_down.marks(), teacher_row), row_low, width, small_rows
+        chain_qkv, qkv_spans, tie(place, chain_down.marks()), row_low, width, small_rows
     )
     valid_row = (
         lax.dynamic_slice(
@@ -1582,6 +1581,7 @@
     chain_down.advance(queries)
     queries = tie(queries, chain_down.marks())
     attended = attend(queries, keys, values, seg, 0, pairs // 2)
+    teacher_row = swap_in(teacher, tp_rank, attended)
     chain_down.advance(attended)
     mixed, q_padded, k_padded = attend(
         queries, keys, tie(values, chain_down.marks()), seg, pairs // 2, pairs // 2, attended

time: 510 us -> 517 us (1.014)
  starting transfers between devices: 44.6 us -> 52.5 us
    ppermute x36, starting transfers between devices: 28.4 us -> 36 us  [exchange(): lax.ppermute(values, 'fsdp', [(at, at ^ move[0]) for at in range(lax.axis...]
  transfers between devices with their start and end apart: 49 -> 49, of which waited for: 19 -> 17; matrix products, arithmetic and copies ran while one was open for 12% -> 13% of each run, Pallas kernels for 44% -> 43%
where the time goes in v5:
time: 517 us; the launch traced here: 508 us
  Pallas kernels  240 us (46%)
  waiting for transfers between devices  111 us (21%)
  starting transfers between devices  52.5 us (10%)
  other arithmetic  48.2 us (9%)
  local copies, waits for them, and re-layouts  35.6 us (7%)
  between operations  19.8 us (4%)
    ppermute x36, waiting for transfers between devices, exchange(): lax.ppermute(values, 'fsdp', [(at, at ^ move[0]) for at in range(lax.axis...  98.9 us
    pallas_call x1, Pallas kernels, attend_back(): pl.pallas_call(kernel, grid=(count,), in_specs=[padded, padded, pair, pai...  41.2 us
    pallas_call x1, Pallas kernels, up_back(): pl.pallas_call(partial(up_back_kernel, places, tp_places, each, down_plac...  39.5 us
    ppermute x36, starting transfers between devices, exchange(): lax.ppermute(values, 'fsdp', [(at, at ^ move[0]) for at in range(lax.axis...  36 us
    convert_element_type x16, other arithmetic, advance(): self.total(at * self.size).astype(jnp.bfloat16)  33.6 us
    pallas_call x2, Pallas kernels, attend(): pl.pallas_call(kernel, grid=(count,), in_specs=[pl.BlockSpec((length, 1),...  28.4 us
    pallas_call x1, Pallas kernels, out_up_project(): pl.pallas_call(out_up_kernel, grid=(hidden_units // block_width,), in_spe...  25.9 us
    pallas_call x1, Pallas kernels, down_project(): pl.pallas_call(partial(down_kernel, places), grid=(length // BLOCK,), in_...  23 us
  transfers between devices with their start and end apart: 49, of which 17 were waited for; matrix products, arithmetic and copies ran while one was open for 13% of the time, Pallas kernels for 43%

profile of v5, /device:TPU:0, one launch (start us, length us, event | category | flops | bytes accessed | tf_op | source)
XLA Modules:
  0.0 507.9 jit_solution(6904993740760011982)
XLA Ops:
  18.0 9.5 %collective-permute-done.1 = bf16[1,64,768]{2,1,0:T(8,128)(2,1)S(1)} collective-permute-done((bf16[1,64,768]{2,1,0:T(8,128)(2,1)}, bf16[1,64,768]{2,1,0:T(8,128)(2,1)S(1)}, u32[]{:S(2)}, u32[]{:S(2)}) %collective-permute-start.1) | collective-permute-done | bytes 98336 | tf_op jit(solution)/shard_map/ppermute | solution.py:378
  46.5 8.2 %collective-permute-done.6 = bf16[4,64,768]{2,1,0:T(8,128)(2,1)S(1)} collective-permute-done((bf16[4,64,768]{2,1,0:T(8,128)(2,1)S(1)}, bf16[4,64,768]{2,1,0:T(8,128)(2,1)S(1)}, u32[]{:S(2)}, u32[]{:S(2)}) %collective-permute-start.6) | collective-permute-done | bytes 393248 | tf_op jit(solution)/shard_map/ppermute | solution.py:378
  60.3 20.6 %collective-permute-done.7.refs_1_ = bf16[8,64,896]{2,1,0:T(8,128)(2,1)} collective-permute-done((bf16[8,64,896]{2,1,0:T(8,128)(2,1)S(1)}, bf16[8,64,896]{2,1,0:T(8,128)(2,1)}, u32[]{:S(2)}, u32[]{:S(2)}) %collective-permute-start.7) | collective-permute-done | bytes 917536 | tf_op jit(solution)/shard_map/ppermute | solution.py:378
  80.9 10.1 %collective-permute-done.8.refs_5_ = bf16[8,64,768]{2,1,0:T(8,128)(2,1)} collective-permute-done((bf16[8,64,768]{2,1,0:T(8,128)(2,1)}, bf16[8,64,768]{2,1,0:T(8,128)(2,1)}, u32[]{:S(2)}, u32[]{:S(2)}) %collective-permute-start.8) | collective-permute-done | bytes 786464 | tf_op jit(solution)/shard_map/ppermute | solution.py:378
  99.5 16.5 %qkv_project.1 = (bf16[1024,1024]{1,0:T(8,128)(2,1)}, bf16[1024,1024]{1,0:T(8,128)(2,1)}, bf16[1024,1024]{1,0:T(8,128)(2,1)}, bf16[1024,3072]{1,0:T(8,128)(2,1)}, bf16[32,32,128]{2,1,0:T(8,128)(2,1)}) custom-call(s32[2]{0:T(128)} %pad_add_fusion.place_ref, bf16[1024,1024]{1,0:T(8,128)(2,1)} %copy-done.3, bf16[8,64,896]{2,1,0:T(8,128)(2,1)} %copy-done.12, ...), custom_call_target="tpu_custom_call" | custom-call | flops 3221225 | bytes 12582 | tf_op jit(solution)/shard_map/qkv_project/pallas_call | solution.py:891
  119.0 5.7 %collective-permute-start.15 = (bf16[2,64,1152]{2,1,0:T(8,128)(2,1)S(1)}, bf16[2,64,1152]{2,1,0:T(8,128)(2,1)S(1)}, u32[]{:S(2)}, u32[]{:S(2)}) collective-permute-start(bf16[2,64,1152]{2,1,0:T(8,128)(2,1)S(1)} %constant_dynamic-update-slice_fusion.12), channel_id=1, source_target_pairs={{0,8},{2,10},{4,12},{6,14},{8,0},{10,2},{12,4},{14,6},{16,24},{18,... | collective-permute-start | bytes 884744 | tf_op jit(solution)/shard_map/ppermute | solution.py:378
  125.8 14.3 %attend.2 = (bf16[1024,1024]{1,0:T(8,128)(2,1)}, bf16[16,1024,128]{2,1,0:T(8,128)(2,1)}, bf16[16,1024,128]{2,1,0:T(8,128)(2,1)}) custom-call(s32[1024,1]{1,0:T(8,128)} %copy.37.seg_ref, bf16[1024,1024]{1,0:T(8,128)(2,1)} %get-tuple-element.260.q_ref, bf16[1024,1024]{1,0:T(8,128)(2,1)} %get-tuple-element.261.k_ref, bf16[1024,1024]{1,0:T(8,128)(2,1)} %get-tuple-element.270.v_ref), custom_call_target="tpu_custom_call" | custom-call | flops 7000000 | bytes 4194 | tf_op jit(solution)/shard_map/attend/pallas_call | solution.py:642
  147.2 14.1 %attend.3 = (bf16[1024,1024]{1,0:T(8,128)(2,1)}, bf16[16,1024,128]{2,1,0:T(8,128)(2,1)}, bf16[16,1024,128]{2,1,0:T(8,128)(2,1)}) custom-call(s32[1024,1]{1,0:T(8,128)} %copy.37.seg_ref, bf16[1024,1024]{1,0:T(8,128)(2,1)} %get-tuple-element.260.q_ref, ...), custom_call_target="tpu_custom_call", output_to_operand_aliasing={{0}: (4, {}), {1}: (5, {}), {2}: (6, {})} | custom-call | flops 7000000 | bytes 4194 | tf_op jit(solution)/shard_map/attend/pallas_call | solution.py:642
  166.2 25.9 %out_up_project.1 = (bf16[1024,4096]{1,0:T(8,128)(2,1)}, bf16[1024,4096]{1,0:T(8,128)(2,1)}, f32[1024,1024]{1,0:T(8,128)}, f32[1024,1]{1,0:T(8,128)}, bf16[1024,...) custom-call(bf16[1024,1024]{1,0:T(8,128)(2,1)} %get-tuple-element.277.mixed_ref.out_ref.refs_2_, ...), custom_call_target="tpu_custom_call" | custom-call | flops 5368709 | bytes 18874 | tf_op jit(solution)/shard_map/out_up_project/pallas_call | solution.py:967
  198.3 23.0 %down_project.1 = (bf16[1024,1024]{1,0:T(8,128)(2,1)}, f32[1024,1024]{1,0:T(8,128)}, bf16[1024,1024]{1,0:T(8,128)(2,1)}, f32[8,1024]{1,0:T(8,128)}) custom-call(s32[2]{0:T(128)} %pad_add_fusion.place_ref, bf16[1024,4096]{1,0:T(8,128)(2,1)} %get-tuple-element.280.active_ref, f32[1024,1024]{1,0:T(8,128)} %get-tuple-element.281.unit_ref, ...), custom_call_target="tpu_custom_call" | custom-call | flops 4294967 | bytes 18874 | tf_op jit(solution)/shard_map/down_project/pallas_call | solution.py:1084
  224.7 17.8 %down_back.1 = (bf16[16,64,2048]{2,1,0:T(8,128)(2,1)}, bf16[16,64,2048]{2,1,0:T(8,128)(2,1)}) custom-call(s32[2]{0:T(128)} %pad_add_fusion.place_ref, bf16[1024,1024]{1,0:T(8,128)(2,1)} %get-tuple-element.288.grad_ref, bf16[1024,4096]{1,0:T(8,128)(2,1)} %get-tuple-element.280.active_ref), custom_call_target="tpu_custom_call" | custom-call | flops 4294967 | bytes 10485 | tf_op jit(solution)/shard_map/down_back/pallas_call | solution.py:1237
  242.8 5.8 %collective-permute-done.26 = bf16[512,1024]{1,0:T(8,128)(2,1)S(1)} collective-permute-done((bf16[512,1024]{1,0:T(8,128)(2,1)S(1)}, bf16[512,1024]{1,0:T(8,128)(2,1)S(1)}, u32[]{:S(2)}, u32[]{:S(2)}) %collective-permute-start.26) | collective-permute-done | bytes 1048608 | tf_op jit(solution)/shard_map/ppermute | solution.py:381
  248.7 39.5 %up_back.1 = (f32[1024,1024]{1,0:T(8,128)}, f32[1,4096]{1,0:T(1,128)}, bf16[16,64,2048]{2,1,0:T(8,128)(2,1)}, bf16[16,64,2048]{2,1,0:T(8,128)(2,1)}) custom-call(s32[2]{0:T(128)} %pad_add_fusion.place_ref, bf16[1024,1024]{1,0:T(8,128)(2,1)} %get-tuple-element.288.grad_ref, bf16[1024,1024]{1,0:T(8,128)(2,1)} %get-tuple-element.289.hidden_ref, ...), custom_call_target="tpu_custom_call" | custom-call | flops 12884901 | bytes 20971 | tf_op jit(solution)/shard_map/up_back/pallas_call | solution.py:1264
  292.7 10.2 %norm_back.1 = (f32[1024,1024]{1,0:T(8,128)}, bf16[1024,1024]{1,0:T(8,128)(2,1)}, bf16[1024,1024]{1,0:T(8,128)(2,1)}, f32[8,1024]{1,0:T(8,128)}) custom-call(f32[1024,1024]{1,0:T(8,128)} %get-tuple-element.293.base_ref, f32[1024,1024]{1,0:T(8,128)} %get-tuple-element.298.grad_ref, f32[1024,1024]{1,0:T(8,128)} %get-tuple-element.281.unit_ref, ...), custom_call_target="tpu_custom_call" | custom-call | flops 1073741 | bytes 11534 | tf_op jit(solution)/shard_map/norm_back/pallas_call | solution.py:1323
  314.3 41.2 %attend_back.1 = (bf16[1024,1024]{1,0:T(8,128)(2,1)}, bf16[1024,1024]{1,0:T(8,128)(2,1)}, bf16[1024,1024]{1,0:T(8,128)(2,1)}) custom-call(bf16[16,1024,128]{2,1,0:T(8,128)(2,1)} %get-tuple-element.304.qx_ref, bf16[16,1024,128]{2,1,0:T(8,128)(2,1)} %get-tuple-element.305.kx_ref, bf16[1024,1024]{1,0:T(8,128)(2,1)} %get-tuple-element.270.v_ref, ...), custom_call_target="tpu_custom_call" | custom-call | flops 20000000 | bytes 8388 | tf_op jit(solution)/shard_map/attend_back/pallas_call | solution.py:731
  362.5 17.5 %weight_grads.1 = (bf16[16,64,1152]{2,1,0:T(8,128)(2,1)}, bf16[16,64,1152]{2,1,0:T(8,128)(2,1)}, bf16[16,64,1024]{2,1,0:T(8,128)(2,1)}, bf16[16,64,1024]{2,1,0:T(8,128)(2,1)}) custom-call(s32[2]{0:T(128)} %pad_add_fusion.place_ref, bf16[1024,1024]{1,0:T(8,128)(2,1)} %get-tuple-element.316.refs_0_, bf16[1024,1024]{1,0:T(8,128)(2,1)} %copy-done.3, ...), custom_call_target="tpu_custom_call" | custom-call | flops 4294967 | bytes 8388 | tf_op jit(solution)/shard_map/weight_grads/pallas_call | solution.py:1402
  386.3 9.2 %input_grad.2 = bf16[512,1024]{1,0:T(8,128)(2,1)} custom-call(s32[2]{0:T(128)} %pad_add_fusion.place_ref, f32[1024,1024]{1,0:T(8,128)} %get-tuple-element.342.base_ref, bf16[1024,1024]{1,0:T(8,128)(2,1)} %get-tuple-element.307.refs_3_.refs_0_, bf16[1024,1024]{1,0:T(8,128)(2,1)} %get-tuple-element.308.refs_4_.refs_1_, ...), custom_call_target="tpu_custom_call" | custom-call | flops 1610612 | bytes 7340 | tf_op jit(solution)/shard_map/input_grad/pallas_call | solution.py:1434
  402.4 8.9 %input_grad.3 = bf16[512,1024]{1,0:T(8,128)(2,1)} custom-call(s32[2]{0:T(128)} %pad_add_fusion.place_ref, f32[1024,1024]{1,0:T(8,128)} %get-tuple-element.342.base_ref, bf16[1024,1024]{1,0:T(8,128)(2,1)} %get-tuple-element.307.refs_3_.refs_0_, bf16[1024,1024]{1,0:T(8,128)(2,1)} %get-tuple-element.308.refs_4_.refs_1_, ...), custom_call_target="tpu_custom_call" | custom-call | flops 1610612 | bytes 7340 | tf_op jit(solution)/shard_map/input_grad/pallas_call | solution.py:1434
  419.7 6.5 %collective-permute-done.36 = bf16[8,64,1024]{2,1,0:T(8,128)(2,1)} collective-permute-done((bf16[8,64,1024]{2,1,0:T(8,128)(2,1)}, bf16[8,64,1024]{2,1,0:T(8,128)(2,1)}, u32[]{:S(2)}, u32[]{:S(2)}) %collective-permute-start.36) | collective-permute-done | bytes 1048608 | tf_op jit(solution)/shard_map/ppermute | solution.py:378
  426.2 9.5 %collective-permute-done.35 = bf16[8,64,1152]{2,1,0:T(8,128)(2,1)} collective-permute-done((bf16[8,64,1152]{2,1,0:T(8,128)(2,1)}, bf16[8,64,1152]{2,1,0:T(8,128)(2,1)}, u32[]{:S(2)}, u32[]{:S(2)}) %collective-permute-start.35) | collective-permute-done | bytes 1179680 | tf_op jit(solution)/shard_map/ppermute | solution.py:378
  440.2 6.6 %collective-permute-done.44 = bf16[2,64,2048]{2,1,0:T(8,128)(2,1)S(1)} collective-permute-done((bf16[2,64,2048]{2,1,0:T(8,128)(2,1)S(1)}, bf16[2,64,2048]{2,1,0:T(8,128)(2,1)S(1)}, u32[]{:S(2)}, u32[]{:S(2)}) %collective-permute-start.44) | collective-permute-done | bytes 524320 | tf_op jit(solution)/shard_map/ppermute | solution.py:378
  451.7 5.5 %collective-permute-done.38 = bf16[4,64,1024]{2,1,0:T(8,128)(2,1)S(1)} collective-permute-done((bf16[4,64,1024]{2,1,0:T(8,128)(2,1)S(1)}, bf16[4,64,1024]{2,1,0:T(8,128)(2,1)S(1)}, u32[]{:S(2)}, u32[]{:S(2)}) %collective-permute-start.38) | collective-permute-done | bytes 524320 | tf_op jit(solution)/shard_map/ppermute | solution.py:378
  465.3 9.2 %collective-permute-done.41 = bf16[2,64,1024]{2,1,0:T(8,128)(2,1)S(1)} collective-permute-done((bf16[2,64,1024]{2,1,0:T(8,128)(2,1)S(1)}, bf16[2,64,1024]{2,1,0:T(8,128)(2,1)S(1)}, u32[]{:S(2)}, u32[]{:S(2)}) %collective-permute-start.41) | collective-permute-done | bytes 262176 | tf_op jit(solution)/shard_map/ppermute | solution.py:378
  479.1 8.8 %collective-permute-done.46 = bf16[1,64,2048]{2,1,0:T(8,128)(2,1)S(1)} collective-permute-done((bf16[1,64,2048]{2,1,0:T(8,128)(2,1)S(1)}, bf16[1,64,2048]{2,1,0:T(8,128)(2,1)S(1)}, u32[]{:S(2)}, u32[]{:S(2)}) %collective-permute-start.46) | collective-permute-done | bytes 262176 | tf_op jit(solution)/shard_map/ppermute | solution.py:378
  (260 shorter events, 143.9 us)
Async XLA Ops:
  7.2 159.0 %all-gather.3.cloned.1.call-start = ((), (), s32[]{:S(2)}) async-start(), calls=%async_computation | async-start | bytes 10813440 | tf_op jit(solution)/shard_map/all_gather | solution.py:1547
  9.5 27.1 %collective-permute-start.4 = (bf16[512,1024]{1,0:T(8,128)(2,1)}, bf16[512,1024]{1,0:T(8,128)(2,1)S(1)}, u32[]{:S(2)}, u32[]{:S(2)}) collective-permute-start(bf16[512,1024]{1,0:T(8,128)(2,1)} %dynamic-slice_bitcast_fusion.1), channel_id=1, source_target_pairs={{0,1},{1,0},{2,3},{3,2},{4,5},{5,4},{6,7},{7,6},{8,9},{9,8},{10,11... | collective-permute-start | bytes 3145736 | tf_op jit(solution)/shard_map/ppermute | solution.py:381
  55.1 25.8 %collective-permute-start.7 = (bf16[8,64,896]{2,1,0:T(8,128)(2,1)S(1)}, bf16[8,64,896]{2,1,0:T(8,128)(2,1)}, u32[]{:S(2)}, u32[]{:S(2)}) collective-permute-start(bf16[8,64,896]{2,1,0:T(8,128)(2,1)S(1)} %constant_dynamic-update-slice_fusion.8.refs_0_), channel_id=1, source_target_pairs={{0,4},{2,6},{4,0},{6,2},{8,12},{10,14},{12,8},{14,10},{16,20},{18,... | collective-permute-start | bytes 2752520 | tf_op jit(solution)/shard_map/ppermute | solution.py:378
  58.2 32.8 %collective-permute-start.8 = (bf16[8,64,768]{2,1,0:T(8,128)(2,1)}, bf16[8,64,768]{2,1,0:T(8,128)(2,1)}, u32[]{:S(2)}, u32[]{:S(2)}) collective-permute-start(bf16[8,64,768]{2,1,0:T(8,128)(2,1)} %constant_dynamic-update-slice_fusion.10.refs_4_), channel_id=1, source_target_pairs={{0,8},{2,10},{4,12},{6,14},{8,0},{10,2},{12,4},{14,6},{16,24},{18,... | collective-permute-start | bytes 2359304 | tf_op jit(solution)/shard_map/ppermute | solution.py:378
  59.8 35.6 %collective-permute-start.11 = (bf16[8,64,768]{2,1,0:T(8,128)(2,1)}, bf16[8,64,768]{2,1,0:T(8,128)(2,1)}, u32[]{:S(2)}, u32[]{:S(2)}) collective-permute-start(bf16[8,64,768]{2,1,0:T(8,128)(2,1)} %constant_dynamic-update-slice_fusion.10.refs_4_), channel_id=1, source_target_pairs={{0,2},{2,0},{4,6},{6,4},{8,10},{10,8},{12,14},{14,12},{16,18},{18,... | collective-permute-start | bytes 2359304 | tf_op jit(solution)/shard_map/ppermute | solution.py:378
  59.8 37.9 %collective-permute-start.9 = (bf16[8,64,896]{2,1,0:T(8,128)(2,1)S(1)}, bf16[8,64,896]{2,1,0:T(8,128)(2,1)S(1)}, u32[]{:S(2)}, u32[]{:S(2)}) collective-permute-start(bf16[8,64,896]{2,1,0:T(8,128)(2,1)S(1)} %constant_dynamic-update-slice_fusion.8.refs_0_), channel_id=1, source_target_pairs={{0,2},{2,0},{4,6},{6,4},{8,10},{10,8},{12,14},{14,12},{16,18},{18,... | collective-permute-start | bytes 2752520 | tf_op jit(solution)/shard_map/ppermute | solution.py:378
  91.0 26.0 %collective-permute-start.13 = (bf16[1,64,1152]{2,1,0:T(8,128)(2,1)}, bf16[1,64,1152]{2,1,0:T(8,128)(2,1)S(1)}, u32[]{:S(2)}, u32[]{:S(2)}) collective-permute-start(bf16[1,64,1152]{2,1,0:T(8,128)(2,1)} %bitcast.80), channel_id=1, source_target_pairs={{0,16},{2,18},{4,20},{6,22},{8,24},{10,26},{12,28},{14,30},{16,0},... | collective-permute-start | bytes 442376 | tf_op jit(solution)/shard_map/ppermute | solution.py:378
  117.1 23.0 %collective-permute-start.16 = (bf16[2,64,896]{2,1,0:T(8,128)(2,1)S(1)}, bf16[2,64,896]{2,1,0:T(8,128)(2,1)S(1)}, u32[]{:S(2)}, u32[]{:S(2)}) collective-permute-start(bf16[2,64,896]{2,1,0:T(8,128)(2,1)S(1)} %constant_dynamic-update-slice_fusion.14), channel_id=1, source_target_pairs={{0,1},{1,0},{2,3},{3,2},{4,5},{5,4},{6,7},{7,6},{8,9},{9,8},{10,11... | collective-permute-start | bytes 688136 | tf_op jit(solution)/shard_map/ppermute | solution.py:381
  144.3 51.3 %collective-permute-start.19 = (bf16[512,1024]{1,0:T(8,128)(2,1)}, bf16[512,1024]{1,0:T(8,128)(2,1)}, u32[]{:S(2)}, u32[]{:S(2)}) collective-permute-start(bf16[512,1024]{1,0:T(8,128)(2,1)} %dynamic-slice_bitcast_fusion), channel_id=1, source_target_pairs={{0,1},{1,0},{2,3},{3,2},{4,5},{5,4},{6,7},{7,6},{8,9},{9,8},{10,11... | collective-permute-start | bytes 3145736 | tf_op jit(solution)/shard_map/ppermute | solution.py:381
  162.2 29.9 %collective-permute-start.20 = (bf16[8,64,1152]{2,1,0:T(8,128)(2,1)S(1)}, bf16[8,64,1152]{2,1,0:T(8,128)(2,1)}, u32[]{:S(2)}, u32[]{:S(2)}) collective-permute-start(bf16[8,64,1152]{2,1,0:T(8,128)(2,1)S(1)} %constant_dynamic-update-slice_fusion.20.refs_0_), channel_id=1, source_target_pairs={{0,4},{2,6},{4,0},{6,2},{8,12},{10,14},{12,8},{14,10},{16,20},{18,... | collective-permute-start | bytes 3538952 | tf_op jit(solution)/shard_map/ppermute | solution.py:378
  164.9 27.2 %collective-permute-start.21 = (bf16[8,64,896]{2,1,0:T(8,128)(2,1)}, bf16[8,64,896]{2,1,0:T(8,128)(2,1)}, u32[]{:S(2)}, u32[]{:S(2)}) collective-permute-start(bf16[8,64,896]{2,1,0:T(8,128)(2,1)} %constant_dynamic-update-slice_fusion.22.refs_4_), channel_id=1, source_target_pairs={{0,8},{2,10},{4,12},{6,14},{8,0},{10,2},{12,4},{14,6},{16,24},{18,... | collective-permute-start | bytes 2752520 | tf_op jit(solution)/shard_map/ppermute | solution.py:378
  166.2 30.9 %collective-permute-start.22 = (bf16[8,64,1152]{2,1,0:T(8,128)(2,1)S(1)}, bf16[8,64,1152]{2,1,0:T(8,128)(2,1)}, u32[]{:S(2)}, u32[]{:S(2)}) collective-permute-start(bf16[8,64,1152]{2,1,0:T(8,128)(2,1)S(1)} %constant_dynamic-update-slice_fusion.20.refs_0_), channel_id=1, source_target_pairs={{0,2},{2,0},{4,6},{6,4},{8,10},{10,8},{12,14},{14,12},{16,18},{18,... | collective-permute-start | bytes 3538952 | tf_op jit(solution)/shard_map/ppermute | solution.py:378
  223.1 25.6 %collective-permute-start.26 = (bf16[512,1024]{1,0:T(8,128)(2,1)S(1)}, bf16[512,1024]{1,0:T(8,128)(2,1)S(1)}, u32[]{:S(2)}, u32[]{:S(2)}) collective-permute-start(bf16[512,1024]{1,0:T(8,128)(2,1)S(1)} %get-tuple-element.454), channel_id=1, source_target_pairs={{0,1},{1,0},{2,3},{3,2},{4,5},{5,4},{6,7},{7,6},{8,9},{9,8},{10,11... | collective-permute-start | bytes 3145736 | tf_op jit(solution)/shard_map/ppermute | solution.py:381
  242.6 45.7 %collective-permute-start.28 = (bf16[16,64,2048]{2,1,0:T(8,128)(2,1)}, bf16[16,64,2048]{2,1,0:T(8,128)(2,1)}, u32[]{:S(2)}, u32[]{:S(2)}) collective-permute-start(bf16[16,64,2048]{2,1,0:T(8,128)(2,1)} %get-tuple-element.287), channel_id=1, source_target_pairs={{0,2},{2,0},{4,6},{6,4},{8,10},{10,8},{12,14},{14,12},{16,18},{18,... | collective-permute-start | bytes 12582920 | tf_op jit(solution)/shard_map/ppermute | solution.py:378
  307.4 51.7 %collective-permute-start.29 = (bf16[8,64,2048]{2,1,0:T(8,128)(2,1)}, bf16[8,64,2048]{2,1,0:T(8,128)(2,1)}, u32[]{:S(2)}, u32[]{:S(2)}) collective-permute-start(bf16[8,64,2048]{2,1,0:T(8,128)(2,1)} %add_convert_fusion), channel_id=1, source_target_pairs={{0,8},{2,10},{4,12},{6,14},{8,0},{10,2},{12,4},{14,6},{16,24},{18,... | collective-permute-start | bytes 6291464 | tf_op jit(solution)/shard_map/ppermute | solution.py:378
  311.5 69.1 %collective-permute-start.31 = (bf16[8,64,2048]{2,1,0:T(8,128)(2,1)}, bf16[8,64,2048]{2,1,0:T(8,128)(2,1)}, u32[]{:S(2)}, u32[]{:S(2)}) collective-permute-start(bf16[8,64,2048]{2,1,0:T(8,128)(2,1)} %add_convert_fusion.1), channel_id=1, source_target_pairs={{0,1},{1,0},{2,3},{3,2},{4,5},{5,4},{6,7},{7,6},{8,9},{9,8},{10,11... | collective-permute-start | bytes 6291464 | tf_op jit(solution)/shard_map/ppermute | solution.py:381
  384.1 27.3 %collective-permute-start.32 = (bf16[4,64,2048]{2,1,0:T(8,128)(2,1)}, bf16[4,64,2048]{2,1,0:T(8,128)(2,1)}, u32[]{:S(2)}, u32[]{:S(2)}) collective-permute-start(bf16[4,64,2048]{2,1,0:T(8,128)(2,1)} %add_convert_fusion.4), channel_id=1, source_target_pairs={{0,4},{2,6},{4,0},{6,2},{8,12},{10,14},{12,8},{14,10},{16,20},{18,... | collective-permute-start | bytes 3145736 | tf_op jit(solution)/shard_map/ppermute | solution.py:378
  384.8 26.5 %collective-permute-start.30 = (bf16[4,64,2048]{2,1,0:T(8,128)(2,1)}, bf16[4,64,2048]{2,1,0:T(8,128)(2,1)}, u32[]{:S(2)}, u32[]{:S(2)}) collective-permute-start(bf16[4,64,2048]{2,1,0:T(8,128)(2,1)} %add_convert_fusion.5), channel_id=1, source_target_pairs={{0,1},{1,0},{2,3},{3,2},{4,5},{5,4},{6,7},{7,6},{8,9},{9,8},{10,11... | collective-permute-start | bytes 3145736 | tf_op jit(solution)/shard_map/ppermute | solution.py:381
  395.5 54.8 %collective-permute-start.39 = (bf16[512,1024]{1,0:T(8,128)(2,1)}, bf16[512,1024]{1,0:T(8,128)(2,1)}, u32[]{:S(2)}, u32[]{:S(2)}) collective-permute-start(bf16[512,1024]{1,0:T(8,128)(2,1)} %input_grad.2), channel_id=1, source_target_pairs={{0,1},{1,0},{2,3},{3,2},{4,5},{5,4},{6,7},{7,6},{8,9},{9,8},{10,11... | collective-permute-start | bytes 3145736 | tf_op jit(solution)/shard_map/ppermute | solution.py:381
  399.7 26.4 %collective-permute-start.36 = (bf16[8,64,1024]{2,1,0:T(8,128)(2,1)}, bf16[8,64,1024]{2,1,0:T(8,128)(2,1)}, u32[]{:S(2)}, u32[]{:S(2)}) collective-permute-start(bf16[8,64,1024]{2,1,0:T(8,128)(2,1)} %add_convert_fusion.3), channel_id=1, source_target_pairs={{0,8},{2,10},{4,12},{6,14},{8,0},{10,2},{12,4},{14,6},{16,24},{18,... | collective-permute-start | bytes 3145736 | tf_op jit(solution)/shard_map/ppermute | solution.py:378
  401.1 34.6 %collective-permute-start.35 = (bf16[8,64,1152]{2,1,0:T(8,128)(2,1)}, bf16[8,64,1152]{2,1,0:T(8,128)(2,1)}, u32[]{:S(2)}, u32[]{:S(2)}) collective-permute-start(bf16[8,64,1152]{2,1,0:T(8,128)(2,1)} %add_convert_fusion.2), channel_id=1, source_target_pairs={{0,4},{2,6},{4,0},{6,2},{8,12},{10,14},{12,8},{14,10},{16,20},{18,... | collective-permute-start | bytes 3538952 | tf_op jit(solution)/shard_map/ppermute | solution.py:378
  413.2 27.0 %collective-permute-start.45 = (bf16[2,64,2048]{2,1,0:T(8,128)(2,1)S(1)}, bf16[2,64,2048]{2,1,0:T(8,128)(2,1)S(1)}, u32[]{:S(2)}, u32[]{:S(2)}) collective-permute-start(bf16[2,64,2048]{2,1,0:T(8,128)(2,1)S(1)} %add_convert_fusion.7), channel_id=1, source_target_pairs={{0,8},{2,10},{4,12},{6,14},{8,0},{10,2},{12,4},{14,6},{16,24},{18,... | collective-permute-start | bytes 1572872 | tf_op jit(solution)/shard_map/ppermute | solution.py:378
  417.1 29.7 %collective-permute-start.44 = (bf16[2,64,2048]{2,1,0:T(8,128)(2,1)S(1)}, bf16[2,64,2048]{2,1,0:T(8,128)(2,1)S(1)}, u32[]{:S(2)}, u32[]{:S(2)}) collective-permute-start(bf16[2,64,2048]{2,1,0:T(8,128)(2,1)S(1)} %add_convert_fusion.9), channel_id=1, source_target_pairs={{0,4},{2,6},{4,0},{6,2},{8,12},{10,14},{12,8},{14,10},{16,20},{18,... | collective-permute-start | bytes 1572872 | tf_op jit(solution)/shard_map/ppermute | solution.py:378
  448.2 30.9 %collective-permute-start.47 = (bf16[1,64,2048]{2,1,0:T(8,128)(2,1)S(1)}, bf16[1,64,2048]{2,1,0:T(8,128)(2,1)S(1)}, u32[]{:S(2)}, u32[]{:S(2)}) collective-permute-start(bf16[1,64,2048]{2,1,0:T(8,128)(2,1)S(1)} %add_convert_fusion.11), channel_id=1, source_target_pairs={{0,16},{2,18},{4,20},{6,22},{8,24},{10,26},{12,28},{14,30},{16,0},... | collective-permute-start | bytes 786440 | tf_op jit(solution)/shard_map/ppermute | solution.py:378
  (53 other events, 802.9 us)
Sparse Core Ops, SparseCore 0:
  43.3 98.9 all-gather.2
